TPU v7x, 128 devices: a whole 4x4x4 slice. The times are simulated.
128 devices in a mesh: grp: 8 (over z, core), dev: 16 (over y, x).
Axes of the slice: x: 4, y: 4, z: 4, core: 2. Of those that a mesh axis runs over, the one named last changes fastest.
Arguments:
- divergence: float32 [512, 16, 256], P(('grp', 'dev')), may hold values from -4 to 4
- box_coords: int32 [512, 3], replicated, may hold values from 0 to 7, as said below
- neighbors: int32 [512, 6], replicated, may hold values from -1 to 511, as said below
Outputs:
- potential: float32 [512, 16, 256], P(('grp', 'dev'))
- residual: float32 [512, 16, 256], P(('grp', 'dev'))
Inputs may be any that keep to these rules, and one draw needn't show every extreme that they name: `box_coords`: every lattice position of 8 x 8 x 8 is held by exactly one box. Box b is held by index b // 4 of grp+dev in mesh order; the device at index g of grp and index d of dev holds the four boxes with x = g, y equal to 2 * (d // 4) or one more, and z equal to 2 * (d % 4) or one more, in an order that varies from device to device. neighbors[b, f] is the index of the box next to box b on side f, or -1 at the edge of the lattice.
All inputs are finite; a program needn't handle non-finite values.
Results may differ from a plain program's by a relative error of at most 0.00025.
Values sent between devices are 32-bit elements; how exact they have to be, the bound alone decides.
No kernel may reach another device: no remote copies, remote signals or barrier semaphores. Data moves between devices by JAX's collectives and lax.ppermute only.
A program may use at most 64 MiB of HBM per device.

v0:
```python
import jax
import jax.numpy as jnp
from jax import lax
from jax.sharding import PartitionSpec as P

KC = 4
CYCLES = 2
LZ = 8


RELAX_WEIGHT = 0.8
FACE_OPPOSITE = (1, 0, 3, 2, 5, 4)
SLOT_FLIP = (0, 0, 2, 2, 1, 1)


def with_halo(block, sides, width):
    for axis, dim in sides:
        count = lax.axis_size(axis)
        forward = [(i, i + 1) for i in range(count - 1)]
        backward = [(target, source) for source, target in forward]
        low = lax.ppermute(
            lax.slice_in_dim(block, block.shape[dim] - width, None, axis=dim), axis, forward
        )
        high = lax.ppermute(lax.slice_in_dim(block, 0, width, axis=dim), axis, backward)
        block = jnp.concatenate([low, block, high], axis=dim)
    return block


def passed_along(block, axis, distance):
    devices = range(lax.axis_size(axis))
    route = [(i - distance, i) for i in devices if i - distance in devices]
    return lax.ppermute(block, axis, route)


def box_faces(grid_field):
    box_count, box_edge, box_plane = grid_field.shape
    return jnp.stack(
        [
            grid_field[:, 0, :],
            grid_field[:, box_edge - 1, :],
            grid_field[:, :, :box_edge].reshape(box_count, box_plane),
            grid_field[:, :, box_plane - box_edge :].reshape(box_count, box_plane),
            grid_field[:, :, 0::box_edge].reshape(box_count, box_plane),
            grid_field[:, :, box_edge - 1 :: box_edge].reshape(box_count, box_plane),
        ],
        axis=1,
    )


def neighbor_total(grid_field, ghost):
    box_count, box_edge, box_plane = grid_field.shape
    k_index = jnp.arange(box_plane, dtype=jnp.int32) % box_edge
    zero_column = jnp.zeros((box_count, box_edge, 1), grid_field.dtype)
    up_x = jnp.concatenate([grid_field[:, 1:, :], ghost[:, 1][:, None, :]], axis=1)
    down_x = jnp.concatenate([ghost[:, 0][:, None, :], grid_field[:, :-1, :]], axis=1)
    up_y = jnp.concatenate(
        [grid_field[:, :, box_edge:], ghost[:, 3].reshape(box_count, box_edge, box_edge)], axis=2
    )
    down_y = jnp.concatenate(
        [
            ghost[:, 2].reshape(box_count, box_edge, box_edge),
            grid_field[:, :, : box_plane - box_edge],
        ],
        axis=2,
    )
    up_z = jnp.where(
        k_index == box_edge - 1,
        jnp.repeat(ghost[:, 5].reshape(box_count, box_edge, box_edge), box_edge, axis=2),
        jnp.concatenate([grid_field[:, :, 1:], zero_column], axis=2),
    )
    down_z = jnp.where(
        k_index == 0,
        jnp.repeat(ghost[:, 4].reshape(box_count, box_edge, box_edge), box_edge, axis=2),
        jnp.concatenate([zero_column, grid_field[:, :, :-1]], axis=2),
    )
    return up_x + down_x + (up_y + down_y) + (up_z + down_z)


def operate(grid_field, ghost):
    return 6.0 * grid_field - neighbor_total(grid_field, ghost)


def restrict_boxes(residual_now):
    box_count, box_edge, box_plane = residual_now.shape
    half_edge = box_edge // 2
    grouped = residual_now.reshape(box_count, half_edge, 2, half_edge, 2, half_edge, 2)
    coarse_blocks = jnp.sum(grouped, axis=(2, 4, 6)) * 0.125
    return jnp.transpose(coarse_blocks, (0, 3, 1, 2))


def prolong_boxes(blocks, box_edge):
    box_count = blocks.shape[0]
    fine_blocks = jnp.transpose(blocks, (0, 2, 3, 1))
    fine_blocks = jnp.repeat(jnp.repeat(jnp.repeat(fine_blocks, 2, axis=1), 2, axis=2), 2, axis=3)
    return fine_blocks.reshape(box_count, box_edge, box_edge * box_edge)


def coarse_neighbors(padded):
    center = padded[1:-1]
    zero_x = jnp.zeros_like(center[:, :1, :])
    zero_y = jnp.zeros_like(center[:, :, :1])
    along_x = jnp.concatenate([center[:, 1:, :], zero_x], axis=1) + jnp.concatenate(
        [zero_x, center[:, :-1, :]], axis=1
    )
    along_y = jnp.concatenate([center[:, :, 1:], zero_y], axis=2) + jnp.concatenate(
        [zero_y, center[:, :, :-1]], axis=2
    )
    return padded[2:] + padded[:-2] + along_x + along_y


def coarse_sweep(correction, coarse_source, padded):
    return correction + RELAX_WEIGHT / 1.5 * (
        coarse_source - 0.25 * (6.0 * correction - coarse_neighbors(padded))
    )


def block_index(box_pos, half_edge, z_base):
    offsets = jnp.arange(half_edge, dtype=jnp.int32)
    z_index = box_pos[:, 2, None, None, None] * half_edge + offsets[None, :, None, None] - z_base
    x_index = box_pos[:, 0, None, None, None] * half_edge + offsets[None, None, :, None]
    y_index = box_pos[:, 1, None, None, None] * half_edge + offsets[None, None, None, :]
    return (z_index, x_index, y_index)


def place_blocks(running, blocks, box_pos, valid_rows, z_base):
    layers = running.shape[0]
    half_edge = blocks.shape[1]
    z_index, x_index, y_index = block_index(box_pos, half_edge, z_base)
    inside_mask = valid_rows[:, None, None, None] & (z_index >= 0) & (z_index < layers)
    z_index = jnp.where(inside_mask, z_index, layers)
    return running.at[z_index, x_index, y_index].add(blocks, mode="drop")


def extract_blocks(grid_field, box_pos, z_base, half_edge):
    layers = grid_field.shape[0]
    z_index, x_index, y_index = block_index(box_pos, half_edge, z_base)
    inside_mask = (z_index >= 0) & (z_index < layers)
    values = grid_field[jnp.clip(z_index, 0, layers - 1), x_index, y_index]
    return jnp.where(inside_mask, values, 0.0)


def body(divergence, box_coords, neighbors):
    box_count, box_edge, box_plane = divergence.shape
    half_edge = box_edge // 2
    count_all = lax.axis_size(("grp", "dev"))
    count_dev = lax.axis_size("dev")
    rank_all = lax.axis_index(("grp", "dev"))
    rank_dev = lax.axis_index("dev")
    slab_depth = LZ * half_edge // count_dev
    grid_x = count_all // count_dev * half_edge
    grid_y = count_dev // 2 * half_edge
    cell_total = LZ * half_edge * grid_x * grid_y
    faces_all = box_count * 6
    row_step = LZ // 2
    group_base = rank_all - rank_dev
    group_coords = lax.dynamic_slice_in_dim(
        box_coords, group_base * box_count, count_dev * box_count, 0
    )
    my_coords = lax.dynamic_slice_in_dim(box_coords, rank_all * box_count, box_count, 0)
    z_base = rank_dev * slab_depth
    own_rows = lax.dynamic_slice_in_dim(neighbors, rank_all * box_count, box_count, 0).reshape(
        faces_all
    )
    present = own_rows >= 0
    opposite = jnp.tile(jnp.array(FACE_OPPOSITE, dtype=jnp.int32), box_count)
    wanted = jnp.where(present, own_rows % box_count, 0) * 6 + opposite
    brick_slot = my_coords[:, 1] % 2 * 2 + my_coords[:, 2] % 2
    face_side = jnp.tile(jnp.arange(6, dtype=jnp.int32), box_count)
    slot_flip = jnp.tile(jnp.array(SLOT_FLIP, dtype=jnp.int32), box_count)
    row_slot = jnp.repeat(brick_slot, 6)
    same_owner = present & (jnp.where(present, own_rows // box_count, -1) == rank_all)
    far_pick = face_side * box_count + jnp.bitwise_xor(row_slot, slot_flip)
    halo_pick = jnp.where(same_owner, faces_all + wanted, far_pick)

    def fine_ghosts(grid_field):
        faces_box = box_faces(grid_field)
        faces = faces_box.reshape(faces_all, box_plane)
        sending = (
            jnp.zeros((6, box_count, box_plane), jnp.float32)
            .at[:, brick_slot]
            .set(jnp.swapaxes(faces_box, 0, 1))
        )
        along_x = with_halo(sending[0:2], (("grp", 0),), 1)
        from_ylow = passed_along(sending[3], "dev", row_step)
        from_yhigh = passed_along(sending[2], "dev", -row_step)
        from_zlow = passed_along(sending[5], "dev", 1)
        from_zhigh = passed_along(sending[4], "dev", -1)
        received = jnp.stack(
            [along_x[0], along_x[3], from_ylow, from_yhigh, from_zlow, from_zhigh], axis=0
        )
        pool = jnp.concatenate([received.reshape(faces_all, box_plane), faces], axis=0)
        chosen = pool[halo_pick]
        return jnp.where(present[:, None], chosen, 0.0).reshape(box_count, 6, box_plane)

    def smooth_step(potential):
        return potential + RELAX_WEIGHT / 6.0 * (
            divergence - operate(potential, fine_ghosts(potential))
        )

    potential = jnp.zeros_like(divergence)
    for cycle_index in range(CYCLES):
        potential = smooth_step(potential)
        residual_now = divergence - operate(potential, fine_ghosts(potential))
        blocks = restrict_boxes(residual_now)
        empty_slab = jnp.zeros((slab_depth, grid_x, grid_y), jnp.float32)
        shard_piece = lax.all_gather(blocks, "dev", axis=0, tiled=True)
        all_valid = jnp.arange(shard_piece.shape[0], dtype=jnp.int32) >= 0
        partial_slab = place_blocks(empty_slab, shard_piece, group_coords, all_valid, z_base)
        coarse_source = lax.psum(partial_slab, "grp")
        source_total = lax.psum(jnp.sum(coarse_source), "dev")
        coarse_source = coarse_source - source_total / cell_total
        correction = jnp.zeros_like(coarse_source)
        for sweep_index in range(KC):
            padded = with_halo(correction, (("dev", 0),), 1)
            correction = coarse_sweep(correction, coarse_source, padded)
        coarse_update = extract_blocks(
            lax.all_gather(correction, "dev", axis=0, tiled=True),
            my_coords,
            jnp.int32(0),
            half_edge,
        )
        potential = potential + prolong_boxes(coarse_update, box_edge)
        potential = smooth_step(potential)
    residual = divergence - operate(potential, fine_ghosts(potential))
    return (potential, residual)


def solution(mesh):
    placed = (P(("grp", "dev"), None, None), P(), P())
    return jax.shard_map(
        body,
        mesh=mesh,
        in_specs=placed,
        out_specs=(P(("grp", "dev"), None, None), P(("grp", "dev"), None, None)),
        check_vma=False,
    )
```

profile of v0, /device:TPU:1, one launch (start us, length us, event | category | flops | bytes accessed | tf_op | source)
XLA Modules:
  0.0 1096.1 jit_solution(3200411768385095683)
XLA Ops:
  8.7 4.9 collective-permute-start
  38.3 5.4 collective-permute-start.6
  45.6 4.6 collective-permute-start.8
  63.5 26.5 %all_gather.12 = f32[64,8,8,8]{3,2,1,0:T(8,128)S(1)} all-gather(f32[4,8,8,8]{3,2,1,0:T(8,128)S(1)} %copy.293), channel_id=1, replica_groups=mesh['grp'=8,'dev'=16] {'dev'}, dimensions={0}, use_global_device_ids=true | all-gather | bytes 139264 | tf_op jit(solution)/shard_map/all_gather | solution.py:206
  91.0 174.4 %scatter_custom_fusion.7 = f32[16384]{0:T(1024)S(1)} fusion(s32[32768]{0:T(1024)S(1)} %reshape.730, f32[32768]{0:T(1024)S(1)} %reshape.732, f32[]{:T(128)} %constant.138.clone.1), kind=kCustom, calls=%fused_computation.193 | custom fusion | flops 32768 | bytes 65540
  271.8 57.5 %all-reduce.46.cloned.1.call-done = f32[4,64,64]{2,1,0:T(8,128)} async-done(((f32[4,64,64]{2,1,0:T(8,128)}), f32[4,64,64]{2,1,0:T(8,128)}) %all-reduce.46.cloned.1.call-update) | async-done | bytes 65552 | tf_op jit(solution)/shard_map/psum | solution.py:209
  330.9 33.9 %psum.29 = f32[]{:T(128)} all-reduce(f32[]{:T(128)} %reduce_sum.37), channel_id=1, replica_groups=mesh['grp'=8,'dev'=16] {'dev'}, use_global_device_ids=true, to_apply=%region_6.7 | all-reduce | flops 1 | bytes 8 | tf_op jit(solution)/shard_map/psum | solution.py:210
  375.1 4.3 collective-permute-start.17
  381.9 4.3 collective-permute-start.19
  388.5 56.0 %all-gather.3.cloned.1.call-done = f32[64,64,64]{2,1,0:T(8,128)} async-done(((f32[4,64,64]{2,1,0:T(8,128)}), f32[64,64,64]{2,1,0:T(8,128)}) %all-gather.3.cloned.1.call-update) | async-done | bytes 1048592 | tf_op jit(solution)/shard_map/all_gather | solution.py:217
  444.5 67.6 %gather_fusion.2 = f32[2048]{0:T(1024)S(1)} fusion(f32[64,64,64]{2,1,0:T(8,128)} %all-gather.3.cloned.1.call-done, s32[2048]{0:T(1024)S(1)} %reshape.622), kind=kCustom, calls=%fused_computation.2 | custom fusion | bytes 40960 | tf_op jit(solution)/shard_map/gather | solution.py:138
  514.7 4.7 collective-permute-start.20
  525.5 5.4 collective-permute-start.24
  539.1 5.4 collective-permute-start.26
  564.2 5.1 collective-permute-start.32
  590.0 25.6 %all_gather.14 = f32[64,8,8,8]{3,2,1,0:T(8,128)S(1)} all-gather(f32[4,8,8,8]{3,2,1,0:T(8,128)S(1)} %copy.325), channel_id=1, replica_groups=mesh['grp'=8,'dev'=16] {'dev'}, dimensions={0}, use_global_device_ids=true | all-gather | bytes 139264 | tf_op jit(solution)/shard_map/all_gather | solution.py:206
  616.6 174.4 %scatter_custom_fusion.8 = f32[16384]{0:T(1024)S(1)} fusion(s32[32768]{0:T(1024)S(1)} %reshape.730, f32[32768]{0:T(1024)S(1)} %reshape.738, f32[]{:T(128)} %constant.138.clone.1), kind=kCustom, calls=%fused_computation.191 | custom fusion | flops 32768 | bytes 65540
  791.8 64.1 %all-reduce.48.cloned.1.call-done = f32[4,64,64]{2,1,0:T(8,128)} async-done(((f32[4,64,64]{2,1,0:T(8,128)}), f32[4,64,64]{2,1,0:T(8,128)}) %all-reduce.48.cloned.1.call-update) | async-done | bytes 65552 | tf_op jit(solution)/shard_map/psum | solution.py:209
  857.5 33.9 %psum.31 = f32[]{:T(128)} all-reduce(f32[]{:T(128)} %reduce_sum.39), channel_id=1, replica_groups=mesh['grp'=8,'dev'=16] {'dev'}, use_global_device_ids=true, to_apply=%region_14.15 | all-reduce | flops 1 | bytes 8 | tf_op jit(solution)/shard_map/psum | solution.py:210
  914.5 56.5 %all-gather.5.cloned.1.call-done = f32[64,64,64]{2,1,0:T(8,128)} async-done(((f32[4,64,64]{2,1,0:T(8,128)}), f32[64,64,64]{2,1,0:T(8,128)}) %all-gather.5.cloned.1.call-update) | async-done | bytes 1048592 | tf_op jit(solution)/shard_map/all_gather | solution.py:217
  971.0 67.6 %gather_fusion.6 = f32[2048]{0:T(1024)S(1)} fusion(f32[64,64,64]{2,1,0:T(8,128)} %all-gather.5.cloned.1.call-done, s32[2048]{0:T(1024)S(1)} %reshape.622), kind=kCustom, calls=%fused_computation.6 | custom fusion | bytes 40960 | tf_op jit(solution)/shard_map/gather | solution.py:138
  1041.2 4.7 collective-permute-start.44
  1052.0 5.4 collective-permute-start.48
  1065.7 5.4 collective-permute-start.50
  (499 shorter events, 181.2 us)
Async XLA Ops:
  7.2 322.1 %all-reduce.46.cloned.1.call-start = ((), (), s32[]{:S(2)}) async-start(), calls=%async_computation | async-start | bytes 262144 | tf_op jit(solution)/shard_map/psum | solution.py:209
  8.7 21.4 %collective-permute-start = (f32[1,4,256]{2,1,0:T(4,128)S(1)}, f32[1,4,256]{2,1,0:T(4,128)S(1)}, u32[]{:S(2)}, u32[]{:S(2)}) collective-permute-start(f32[1,4,256]{2,1,0:T(4,128)S(1)} %copy.354), channel_id=1, source_target_pairs={{0,16},{16,32},{32,48},{48,64},{64,80},{80,96},{96,112},{1,17},{17... | collective-permute-start | bytes 12296 | tf_op jit(solution)/shard_map/ppermute | solution.py:21
  13.6 17.8 %collective-permute-start.1 = (f32[1,4,256]{2,1,0:T(4,128)S(1)}, f32[1,4,256]{2,1,0:T(4,128)S(1)}, u32[]{:S(2)}, u32[]{:S(2)}) collective-permute-start(f32[1,4,256]{2,1,0:T(4,128)S(1)} %copy.355), channel_id=1, source_target_pairs={{16,0},{32,16},{48,32},{64,48},{80,64},{96,80},{112,96},{17,1},{33... | collective-permute-start | bytes 12296 | tf_op jit(solution)/shard_map/ppermute | solution.py:24
  15.5 15.9 %collective-permute-start.2 = (f32[4,256]{1,0:T(4,128)S(1)}, f32[4,256]{1,0:T(4,128)S(1)}, u32[]{:S(2)}, u32[]{:S(2)}) collective-permute-start(f32[4,256]{1,0:T(4,128)S(1)} %bitcast.222), channel_id=1, source_target_pairs={{0,4},{1,5},{2,6},{3,7},{4,8},{5,9},{6,10},{7,11},{8,12},{9,13},{1... | collective-permute-start | bytes 12296 | tf_op jit(solution)/shard_map/ppermute | solution.py:32
  18.8 12.7 %collective-permute-start.3 = (f32[4,256]{1,0:T(4,128)S(1)}, f32[4,256]{1,0:T(4,128)S(1)}, u32[]{:S(2)}, u32[]{:S(2)}) collective-permute-start(f32[4,256]{1,0:T(4,128)S(1)} %bitcast.221), channel_id=1, source_target_pairs={{4,0},{5,1},{6,2},{7,3},{8,4},{9,5},{10,6},{11,7},{12,8},{13,9},{1... | collective-permute-start | bytes 12296 | tf_op jit(solution)/shard_map/ppermute | solution.py:32
  20.1 11.4 %collective-permute-start.4 = (f32[4,256]{1,0:T(4,128)S(1)}, f32[4,256]{1,0:T(4,128)S(1)}, u32[]{:S(2)}, u32[]{:S(2)}) collective-permute-start(f32[4,256]{1,0:T(4,128)S(1)} %bitcast.220), channel_id=1, source_target_pairs={{0,1},{1,2},{2,3},{3,4},{4,5},{5,6},{6,7},{7,8},{8,9},{9,10},{10,1... | collective-permute-start | bytes 12296 | tf_op jit(solution)/shard_map/ppermute | solution.py:32
  38.3 16.1 %collective-permute-start.6 = (f32[1,4,256]{2,1,0:T(4,128)S(1)}, f32[1,4,256]{2,1,0:T(4,128)S(1)}, u32[]{:S(2)}, u32[]{:S(2)}) collective-permute-start(f32[1,4,256]{2,1,0:T(4,128)S(1)} %copy.359), channel_id=1, source_target_pairs={{0,16},{16,32},{32,48},{48,64},{64,80},{80,96},{96,112},{1,17},{17... | collective-permute-start | bytes 12296 | tf_op jit(solution)/shard_map/ppermute | solution.py:21
  43.7 12.0 %collective-permute-start.7 = (f32[1,4,256]{2,1,0:T(4,128)S(1)}, f32[1,4,256]{2,1,0:T(4,128)S(1)}, u32[]{:S(2)}, u32[]{:S(2)}) collective-permute-start(f32[1,4,256]{2,1,0:T(4,128)S(1)} %copy.360), channel_id=1, source_target_pairs={{16,0},{32,16},{48,32},{64,48},{80,64},{96,80},{112,96},{17,1},{33... | collective-permute-start | bytes 12296 | tf_op jit(solution)/shard_map/ppermute | solution.py:24
  266.2 178.2 %all-gather.3.cloned.1.call-start = ((), (), s32[]{:S(2)}) async-start(), calls=%async_computation.1 | async-start | bytes 2228224 | tf_op jit(solution)/shard_map/all_gather | solution.py:217
  266.3 99.2 %collective-permute-start.12 = (f32[1,64,64]{2,1,0:T(8,128)S(1)}, f32[1,64,64]{2,1,0:T(8,128)S(1)}, u32[]{:S(2)}, u32[]{:S(2)}) collective-permute-start(f32[1,64,64]{2,1,0:T(8,128)S(1)} %broadcast.621), channel_id=1, source_target_pairs={{1,0},{2,1},{3,2},{4,3},{5,4},{6,5},{7,6},{8,7},{9,8},{10,9},{11,1... | collective-permute-start | bytes 49160 | tf_op jit(solution)/shard_map/ppermute | solution.py:24
  267.6 97.9 %collective-permute-start.13 = (f32[1,64,64]{2,1,0:T(8,128)S(1)}, f32[1,64,64]{2,1,0:T(8,128)S(1)}, u32[]{:S(2)}, u32[]{:S(2)}) collective-permute-start(f32[1,64,64]{2,1,0:T(8,128)S(1)} %broadcast.621), channel_id=1, source_target_pairs={{0,1},{1,2},{2,3},{3,4},{4,5},{5,6},{6,7},{7,8},{8,9},{9,10},{10,1... | collective-permute-start | bytes 49160 | tf_op jit(solution)/shard_map/ppermute | solution.py:21
  388.0 467.9 %all-reduce.48.cloned.1.call-start = ((), (), s32[]{:S(2)}) async-start(), calls=%async_computation.2 | async-start | bytes 262144 | tf_op jit(solution)/shard_map/psum | solution.py:209
  514.7 16.2 %collective-permute-start.20 = (f32[1,4,256]{2,1,0:T(4,128)S(1)}, f32[1,4,256]{2,1,0:T(4,128)S(1)}, u32[]{:S(2)}, u32[]{:S(2)}) collective-permute-start(f32[1,4,256]{2,1,0:T(4,128)S(1)} %copy.364), channel_id=1, source_target_pairs={{0,16},{16,32},{32,48},{48,64},{64,80},{80,96},{96,112},{1,17},{17... | collective-permute-start | bytes 12296 | tf_op jit(solution)/shard_map/ppermute | solution.py:21
  519.4 12.8 %collective-permute-start.21 = (f32[1,4,256]{2,1,0:T(4,128)S(1)}, f32[1,4,256]{2,1,0:T(4,128)S(1)}, u32[]{:S(2)}, u32[]{:S(2)}) collective-permute-start(f32[1,4,256]{2,1,0:T(4,128)S(1)} %copy.365), channel_id=1, source_target_pairs={{16,0},{32,16},{48,32},{64,48},{80,64},{96,80},{112,96},{17,1},{33... | collective-permute-start | bytes 12296 | tf_op jit(solution)/shard_map/ppermute | solution.py:24
  521.3 10.9 collective-permute-start.22
  539.1 16.5 %collective-permute-start.26 = (f32[1,4,256]{2,1,0:T(4,128)S(1)}, f32[1,4,256]{2,1,0:T(4,128)S(1)}, u32[]{:S(2)}, u32[]{:S(2)}) collective-permute-start(f32[1,4,256]{2,1,0:T(4,128)S(1)} %copy.369), channel_id=1, source_target_pairs={{0,16},{16,32},{32,48},{48,64},{64,80},{80,96},{96,112},{1,17},{17... | collective-permute-start | bytes 12296 | tf_op jit(solution)/shard_map/ppermute | solution.py:21
  544.5 12.4 %collective-permute-start.27 = (f32[1,4,256]{2,1,0:T(4,128)S(1)}, f32[1,4,256]{2,1,0:T(4,128)S(1)}, u32[]{:S(2)}, u32[]{:S(2)}) collective-permute-start(f32[1,4,256]{2,1,0:T(4,128)S(1)} %copy.370), channel_id=1, source_target_pairs={{16,0},{32,16},{48,32},{64,48},{80,64},{96,80},{112,96},{17,1},{33... | collective-permute-start | bytes 12296 | tf_op jit(solution)/shard_map/ppermute | solution.py:24
  564.2 16.4 %collective-permute-start.32 = (f32[1,4,256]{2,1,0:T(4,128)S(1)}, f32[1,4,256]{2,1,0:T(4,128)S(1)}, u32[]{:S(2)}, u32[]{:S(2)}) collective-permute-start(f32[1,4,256]{2,1,0:T(4,128)S(1)} %copy.374), channel_id=1, source_target_pairs={{0,16},{16,32},{32,48},{48,64},{64,80},{80,96},{96,112},{1,17},{17... | collective-permute-start | bytes 12296 | tf_op jit(solution)/shard_map/ppermute | solution.py:21
  569.3 12.6 %collective-permute-start.33 = (f32[1,4,256]{2,1,0:T(4,128)S(1)}, f32[1,4,256]{2,1,0:T(4,128)S(1)}, u32[]{:S(2)}, u32[]{:S(2)}) collective-permute-start(f32[1,4,256]{2,1,0:T(4,128)S(1)} %copy.375), channel_id=1, source_target_pairs={{16,0},{32,16},{48,32},{64,48},{80,64},{96,80},{112,96},{17,1},{33... | collective-permute-start | bytes 12296 | tf_op jit(solution)/shard_map/ppermute | solution.py:24
  791.7 179.3 %all-gather.5.cloned.1.call-start = ((), (), s32[]{:S(2)}) async-start(), calls=%async_computation.3 | async-start | bytes 2228224 | tf_op jit(solution)/shard_map/all_gather | solution.py:217
  1041.2 16.2 %collective-permute-start.44 = (f32[1,4,256]{2,1,0:T(4,128)S(1)}, f32[1,4,256]{2,1,0:T(4,128)S(1)}, u32[]{:S(2)}, u32[]{:S(2)}) collective-permute-start(f32[1,4,256]{2,1,0:T(4,128)S(1)} %copy.379), channel_id=1, source_target_pairs={{0,16},{16,32},{32,48},{48,64},{64,80},{80,96},{96,112},{1,17},{17... | collective-permute-start | bytes 12296 | tf_op jit(solution)/shard_map/ppermute | solution.py:21
  1045.9 12.8 %collective-permute-start.45 = (f32[1,4,256]{2,1,0:T(4,128)S(1)}, f32[1,4,256]{2,1,0:T(4,128)S(1)}, u32[]{:S(2)}, u32[]{:S(2)}) collective-permute-start(f32[1,4,256]{2,1,0:T(4,128)S(1)} %copy.380), channel_id=1, source_target_pairs={{16,0},{32,16},{48,32},{64,48},{80,64},{96,80},{112,96},{17,1},{33... | collective-permute-start | bytes 12296 | tf_op jit(solution)/shard_map/ppermute | solution.py:24
  1065.7 16.5 %collective-permute-start.50 = (f32[1,4,256]{2,1,0:T(4,128)S(1)}, f32[1,4,256]{2,1,0:T(4,128)S(1)}, u32[]{:S(2)}, u32[]{:S(2)}) collective-permute-start(f32[1,4,256]{2,1,0:T(4,128)S(1)} %copy.384), channel_id=1, source_target_pairs={{0,16},{16,32},{32,48},{48,64},{64,80},{80,96},{96,112},{1,17},{17... | collective-permute-start | bytes 12296 | tf_op jit(solution)/shard_map/ppermute | solution.py:21
  1071.1 12.4 %collective-permute-start.51 = (f32[1,4,256]{2,1,0:T(4,128)S(1)}, f32[1,4,256]{2,1,0:T(4,128)S(1)}, u32[]{:S(2)}, u32[]{:S(2)}) collective-permute-start(f32[1,4,256]{2,1,0:T(4,128)S(1)} %copy.385), channel_id=1, source_target_pairs={{16,0},{32,16},{48,32},{64,48},{80,64},{96,80},{112,96},{17,1},{33... | collective-permute-start | bytes 12296 | tf_op jit(solution)/shard_map/ppermute | solution.py:24
  (42 other events, 377.1 us)
Sparse Core Ops, SparseCore 0:
  266.3 62.8 all-reduce.45
  388.1 56.3 all-gather.2
  791.9 63.9 all-reduce.47
  914.7 56.3 all-gather.4
where the time goes:
time: 1100 us
  other arithmetic  366 us (33%)
  waiting for transfers between devices  261 us (24%)
  local copies, waits for them, and re-layouts  173 us (16%)
  starting transfers between devices  159 us (14%)
  blocking collectives  120 us (11%)
  between operations  17.6 us (2%)
    unnamed x5, other arithmetic  350 us
    gather x4, local copies, waits for them, and re-layouts, extract_blocks(): values = grid_field[jnp.clip(z_index, 0, layers - 1), x_index, y_index]  135 us
    psum x2, waiting for transfers between devices, body(): coarse_source = lax.psum(partial_slab, 'grp')  122 us
    all_gather x2, waiting for transfers between devices, body(): lax.all_gather(correction, 'dev', axis=0, tiled=True)  112 us
    ppermute x28, starting transfers between devices, passed_along(): return lax.ppermute(block, axis, route)  71.8 us
    psum x2, blocking collectives, body(): source_total = lax.psum(jnp.sum(coarse_source), 'dev')  67.9 us
    ppermute x14, starting transfers between devices, with_halo(): lax.ppermute(lax.slice_in_dim(block, block.shape[dim] - width, None, axis...  64.6 us
    all_gather x2, blocking collectives, body(): shard_piece = lax.all_gather(blocks, 'dev', axis=0, tiled=True)  52.1 us
  transfers between devices with their start and end apart: 60, of which 17 were waited for; matrix products, arithmetic and copies ran while one was open for 1% of the time, Pallas kernels for 0%

commit v1 on v0

v1 whole, which is shorter than its diff:
```python
import functools

import numpy as np

import jax
import jax.numpy as jnp
from jax import lax
from jax.experimental import pallas as pl
from jax.experimental.pallas import tpu as pltpu
from jax.sharding import PartitionSpec as P

KC = 4
CYCLES = 2
W = 0.8 / 6.0
BETA = 0.8 / 1.5
CELLS = 128**3
BLOCK = 16
LANES = 128
F32 = jnp.float32


def _apply(v):
    total = 6.0 * v
    for axis in range(3):
        lo = [slice(None)] * 3
        hi = [slice(None)] * 3
        lo[axis], hi[axis] = slice(None, -1), slice(1, None)
        total[tuple(lo)] -= v[tuple(hi)]
        total[tuple(hi)] -= v[tuple(lo)]
    return total


def _mean_weights():
    ones = np.ones((128, 128, 128))
    relax = lambda v: v - W * _apply(v)
    k0 = _apply(ones)
    k1 = relax(k0)
    k2 = relax(k1)
    q = k2.reshape(64, 2, 64, 2, 64, 2).sum(axis=(1, 3, 5))
    s = np.zeros_like(q)
    for _ in range(KC):
        s = s + BETA * (q - 0.25 * _apply(s))
    back = np.repeat(np.repeat(np.repeat(s, 2, 0), 2, 1), 2, 2) / 8.0
    full = ones - W * (k0 + k1 + k2) - relax(back) + (s.sum() / CELLS) * relax(ones)
    blocks = []
    for x in (0, 3, 7):
        for y in (0, 1, 3):
            for z in (0, 1, 3):
                b = full[16 * x : 16 * x + 16, 32 * y : 32 * y + 32, 32 * z : 32 * z + 32]
                b = b.reshape(16, 4, 8, 2, 16).transpose(1, 3, 0, 2, 4)
                blocks.append(b.reshape(8, 16, LANES))
    return np.stack(blocks).astype(np.float32)


def _iota(shape, dim):
    return lax.broadcasted_iota(jnp.int32, shape, dim)


def _roll(v, shift, axis):
    shift = shift % v.shape[axis]
    return v if shift == 0 else pltpu.roll(v, shift, axis)


def _position():
    d = lax.axis_index("dev")
    return lax.axis_index("grp"), d // 4, d % 4


def _blk(ref, i):
    return ref[BLOCK * i : BLOCK * (i + 1), :]


def _put(ref, i, v):
    ref[BLOCK * i : BLOCK * (i + 1), :] = v


def _fetch_kernel(div, w2, raw, weight, sem):
    g, yb, zb = _position()
    kind = lambda i, n: jnp.where(i == 0, 0, jnp.where(i == n - 1, 2, 1))
    which = kind(g, 8) * 9 + kind(yb, 4) * 3 + kind(zb, 4)
    copies = (
        pltpu.make_async_copy(div, raw, sem.at[0]),
        pltpu.make_async_copy(w2.at[which], weight, sem.at[1]),
    )
    for copy in copies:
        copy.start()
    for copy in copies:
        copy.wait()


def _sort_kernel(coords, raw, weight, own, sums, order, plain):
    g, yb, zb = _position()
    row = _iota((16, LANES), 0)
    lane = _iota((16, LANES), 1)
    j, k = lane // 16, lane % 16
    edge_x = ((row == 0) & (g == 0)).astype(F32) + ((row == 15) & (g == 7)).astype(F32)
    s1 = jnp.zeros((16, LANES), F32)
    s2 = jnp.zeros((16, LANES), F32)
    box_of = _box_of(coords, g, yb, zb)
    row8 = _iota((8, LANES), 0)
    order[...] = sum(jnp.where(row8 == h, box_of[h], 0) for h in range(4))
    for o in range(4):
        for h in range(2):
            v = raw[box_of[(o // 2) * 2 + h], :, (o % 2) * LANES : (o % 2 + 1) * LANES]
            at = BLOCK * (o * 2 + h)
            plain[at : at + BLOCK, :] = v
            edge = edge_x
            if o == 0:
                edge += ((j == 0) & (yb == 0)).astype(F32)
            if o == 3:
                edge += ((j == 7) & (yb == 3)).astype(F32)
            if h == 0:
                edge += ((k == 0) & (zb == 0)).astype(F32)
            else:
                edge += ((k == 15) & (zb == 3)).astype(F32)
            s1 += (1.0 - W * edge) * v
            s2 += weight[o * 2 + h] * v
    for i in range(16):
        own[8 * i : 8 * i + 8, :] = plain[pl.ds(BLOCK * (i // 2) + i % 2, 8, stride=2), :]
    s1, s2 = (jnp.sum(v, axis=0, keepdims=True) for v in (s1, s2))
    sums[...] = jnp.where(row8 == 0, s1, jnp.where(row8 == 1, s2, 0.0))


def _box_of(coords, g, yb, zb):
    mine = (g * 4 + yb) * 4 + zb
    at = pl.ds(pl.multiple_of(mine // 32 * LANES, LANES), LANES)
    slot = coords[1:2, at] % 2 * 2 + coords[2:3, at] % 2
    box = _iota((1, LANES), 1) - mine % 32 * 4
    inside = (box >= 0) & (box < 4)
    return [jnp.sum(jnp.where(inside & (slot == h), box, 0)) for h in range(4)]


def _ext(own, below, above, q, h):
    if q == 0:
        return _roll(_blk(below, 4), 64 * h, 1)
    if q < 3:
        return _blk(below, (q - 1) * 2 + h)
    if q < 7:
        return _blk(own, (q - 3) * 2 + h)
    if q < 9:
        return _blk(above, (q - 7) * 2 + h)
    return _roll(_blk(above, 4), 64 * h, 1)


def _pack_quads(pieces, src_quad):
    quad = _iota(pieces[0].shape, 1) % 16 // 4
    out = _roll(pieces[0], 4 * (0 - src_quad), 1)
    for s in range(1, len(pieces)):
        out = jnp.where(quad == s, _roll(pieces[s], 4 * (s - src_quad), 1), out)
    return out


Y_FAR, Y_SUMS, Y_MESSAGE = 64, 80, 88


def _y_kernel(own, sums, up, down):
    half = _iota((BLOCK, LANES), 1) < 64
    for i in range(4):
        _put(up, i, _blk(own, i + 4))
        _put(down, i, _blk(own, i))
    _put(up, 4, jnp.where(half, _roll(_blk(own, 3), 64, 1), _blk(own, 2)))
    _put(down, 4, jnp.where(half, _blk(own, 4), _roll(_blk(own, 5), 64, 1)))
    for ref in (up, down):
        ref[Y_SUMS:Y_MESSAGE, :] = sums[...]


def _total_kernel(sums, below, above, across, total):
    total[...] = sums[...] + below[Y_SUMS:Y_MESSAGE, :] + above[Y_SUMS:Y_MESSAGE, :] + across[...]


def _z_kernel(own, below, above, total, up, down):
    ext = lambda q, h: _ext(own, below, above, q, h)
    for q in range(1, 9):
        _put(up, q - 1, ext(q, 1))
        _put(down, q - 1, ext(q, 0))
    for ref, near, quad in ((up, 1, 3), (down, 0, 0)):
        far = [ext(q, 1 - near) for q in range(2, 8)]
        _put(ref, 8, _pack_quads(far[:4], quad))
        _put(ref, 9, _pack_quads([*far[4:], ext(0, near), ext(9, near)], quad))
        ref[160:168, :] = total[...]


OUTER, TAIL, SUMS, MESSAGE = 384, 480, 512, 520
OWN_EY, OWN_COLS = 512, 576


def _rows_to(pieces):
    row = _iota((8, LANES), 0)
    out = None
    for i, (v, r) in enumerate(pieces):
        v = _roll(v, 2 * i - r, 0)
        out = v if out is None else jnp.where(row < 2 * i, out, v)
    return out


def _share(lo, hi, near):
    row, lane = _iota((8, LANES), 0), _iota((8, LANES), 1)
    middle = jnp.where(lane % 16 < 8, hi, lo)
    edge = jnp.where((row // 2) == near // 2, lo, _roll(hi, 2 if near else -2, 0))
    return jnp.where((row >= 2) & (row < 6), middle, edge)


def _x_kernel(own, below, above, zbelow, zabove, total, across, mine, up, down, high, low, part):
    ext = lambda q, h: _ext(own, below, above, q, h)
    two_away = []
    for q in range(1, 9):
        pieces = (_blk(zbelow, q - 1), ext(q, 0), ext(q, 1), _blk(zabove, q - 1))
        for p in range(4):
            _put(mine, (q - 1) * 4 + p, pieces[p])
        if 2 <= q <= 7:
            two_away += pieces[1:3]
            for p in range(4):
                _put(up, (q - 2) * 4 + p, pieces[p])
                _put(down, (q - 2) * 4 + p, pieces[p])
            continue
        at = OUTER + (0 if q == 1 else 48)
        for ref, near in ((up, 6), (down, 0)):
            ref[at : at + 16, :] = pieces[1]
            ref[at + 16 : at + 32, :] = pieces[2]
            for s in (0, 8):
                ref[at + 32 + s : at + 40 + s, :] = _share(pieces[0][s : s + 8], pieces[3][s : s + 8], near)
    for src, quad in ((zbelow, 3), (zabove, 0)):
        near = [_blk(src, q - 1) for q in range(2, 8)]
        two_away += [_pack_quads(near[:4], quad), _pack_quads(near[4:], quad)]
    for ref, r in ((high, 6), (low, 0)):
        for i in range(0, 16, 2):
            a, b = two_away[i : i + 2]
            ref[4 * i : 4 * i + 8, :] = _rows_to([(a[:8], r), (b[:8], r), (a[8:], r), (b[8:], r)])
    extra = [ext(q, h) for q in (0, 9) for h in range(2)]
    extra += [_blk(zbelow, 8), _blk(zbelow, 9), _blk(zabove, 8), _blk(zabove, 9)]
    for i, v in enumerate(extra):
        _put(mine, 32 + i, v)
    for ref, r in ((up, 6), (down, 0)):
        for t in range(4):
            rows = slice(8 * (t % 2), 8 * (t % 2) + 8)
            tile = _rows_to([(v[rows], r) for v in extra[4 * (t // 2) : 4 * (t // 2) + 4]])
            ref[TAIL + 8 * t : TAIL + 8 * t + 8, :] = tile
    t = total[...] + zbelow[160:168, :] + zabove[160:168, :] + across[...]
    part[...] = t
    for ref, at in ((up, SUMS), (down, SUMS), (high, 64), (low, 64)):
        ref[at : at + 8, :] = t


def _window_kernel(mine, xm1, xp1, xm2, xp2, out, send):
    odd = _position()[0] % 2 == 1
    low = xm1[SUMS:MESSAGE, :] + xm2[64:72, :]
    high = xp1[SUMS:MESSAGE, :] + xp2[64:72, :]
    out[...] = mine[...] + (low + high)
    send[...] = mine[...] + jnp.where(odd, high, low)


FINE, COARSE = 40, 20


def _inside(pos, start, limit):
    return ((pos + start >= 0) & (pos + start < limit)).astype(F32)


def _ring_mask(g, zb):
    row = _iota((32, LANES), 0)
    offset = jnp.where(row < 4, row + 16, row - 16)
    return _inside(offset, g * 8, 64) * _inside(_iota((32, LANES), 1) % 64 - 16, zb * 32, 128)


def _fold_mask(yb):
    below, above = (yb > 0).astype(F32), (yb < 3).astype(F32)
    return jnp.where(_iota((8, LANES), 1) < 64, below, above)


def _tall(mask, n):
    return jnp.concatenate([mask] * (n // 8), axis=0)


def _blocks(first, count, size, fn):
    n = (count - 1) // size
    if n:

        def step(i, _):
            fn(first + i * size, size)
            return 0

        lax.fori_loop(0, n, step, 0)
    fn(first + n * size, count - n * size)


def _store(ref, i, v, last):
    ref[i] = v
    if isinstance(i, int) and i == last:
        ref[i + 1] = _roll(v, 64, 1)


def _lanes():
    lane = _iota((8, LANES), 1)
    return lane < 64, lane // 16


def _pick(cond, a, b):
    if a is None and b is None:
        return None
    return jnp.where(cond, 0.0 if a is None else a, 0.0 if b is None else b)


def _turn(v, shift):
    return None if v is None else _roll(v, shift, 1)


def _unfold(groups):
    half, block = _lanes()
    vs = [
        [_pick(half, a, c) for a, c in zip(low, high)] + [_turn(_pick(half, c, a), 64) for a, c in zip(low, high)]
        for low, high in groups
    ]
    for bit in (2, 1):
        vs = [_swap_bit(v, block, bit) for v in vs]
    return [[_pick(half, v[i], v[i ^ 3]) for i in range(8)] for v in vs]


def _swap_bit(v, block, bit):
    zero = (block & bit) == 0
    out = [None] * 8
    for i in range(8):
        if not i & bit:
            x, y = v[i], v[i | bit]
            out[i] = _pick(zero, x, _turn(y, 16 * bit))
            out[i | bit] = _pick(zero, _turn(x, -16 * bit), y)
    return out


def _refold(groups):
    half, block = _lanes()
    vs = [[_pick(half, rows[i], rows[i ^ 3]) for i in range(8)] for rows in groups]
    for bit in (1, 2):
        vs = [_swap_bit(v, block, bit) for v in vs]
    turned = [{p: _turn(v[p | 4], 64) for p in (1, 2)} for v in vs]
    return [
        ([_pick(half, v[p], u[p]) for p in (1, 2)], [_pick(half, u[p], v[p]) for p in (1, 2)])
        for v, u in zip(vs, turned)
    ]


class _Own:
    def __init__(self, ref):
        self.ref = ref

    def tile(self, at):
        return self.ref[at : at + 8, :]

    def core(self, q, p, s):
        return self.tile((q - 1) * 64 + 16 * p + 8 * s)

    def outer(self, i, s):
        return self.tile(OWN_EY + 16 * i + 8 * s)

    def quads(self, i, s):
        return self.tile(OWN_COLS + 16 * i + 8 * s)


class _Sent(_Own):
    def __init__(self, ref, from_below):
        self.ref, self.first = ref, 6 if from_below else 0

    def core(self, q, p, s):
        if 2 <= q <= 7:
            return self.tile((q - 2) * 64 + 16 * p + 8 * s)
        at = OUTER + (0 if q == 1 else 48) + 8 * s
        if p in (1, 2):
            return self.tile(at + 16 * (p - 1))
        shared = self.tile(at + 32)
        if p == 0:
            return shared
        near = _iota((8, LANES), 0) // 2 == self.first // 2
        return jnp.where(near, _roll(shared, -2 if self.first else 2, 0), shared)

    def short(self, i, s):
        return _roll(self.tile(TAIL + 8 * (i // 4 * 2 + s)), self.first - 2 * (i % 4), 0)

    def outer(self, i, s):
        return self.short(i, s)

    def quads(self, i, s):
        return self.short(4 + i, s)


def _pieces(at, q, s):
    if 1 <= q <= 8:
        return [at.core(q, p, s) for p in range(4)]
    slot = 2 if q == 0 else 3
    near = [_roll(at.quads(c, s), by, 1) for c, by in ((1, 4 * (3 - slot)), (3, -4 * slot))]
    return [near[0], *(at.outer((0 if q == 0 else 2) + h, s) for h in range(2)), near[1]]


def _far_pieces(at, q, s):
    c, slot = divmod(q - 2, 4)
    return [_roll(at.quads(c, s), -4 * slot, 1), None, None, _roll(at.quads(2 + c, s), 4 * (3 - slot), 1)]


def _unpack_brick(at, mask, mask_far, fold, store, store_far):
    for batch in ([(0, 0), (1, 0)], [(2, 0), (2, 1)], [(3, 0), (3, 1)], [(4, 0), (4, 1)]):
        tasks = [(q, far, s) for q, far in batch for s in range(2)]
        groups = [
            [(_far_pieces if far else _pieces)(at, o, s) for o in (q, 9 - q)] for q, far, s in tasks
        ]
        for (q, far, s), rows in zip(tasks, _unfold(groups)):
            m = _outer_mask(mask_far if far else mask, fold, q)
            for r in range(8):
                if far:
                    store_far(s, 8 * q + r - 15, rows[r] * m)
                else:
                    store(s, 8 * q + r, rows[r] * m)


def _outer_mask(mask, fold, q):
    return mask * fold if q < 3 else mask


def _far_mask(g, zb):
    row = _iota((24, LANES), 0) - 8
    lane = _iota((24, LANES), 1) % 64
    below, above = (zb > 0).astype(F32), (zb < 3).astype(F32)
    return _inside(row, g * 8, 64) * jnp.where(lane < 4, below, jnp.where(lane >= 60, above, 0.0))


def _brick_kernel(ref, tile, far, *, at, rows):
    g, yb, zb = _position()

    def store(s, i, v):
        tile[s, i] = v

    def put(s, i, v):
        far[s, i] = v

    mask_far = _far_mask(g, zb)[rows.start - 8 : rows.stop - 8]
    _unpack_brick(at(ref), _ring_mask(g, zb)[rows], mask_far, _fold_mask(yb), store, put)
    for s in range(2):
        tile[s, FINE] = _roll(tile[s, FINE - 1], 64, 1)
        far[s, FINE - 15] = _roll(far[s, FINE - 16], 64, 1)


def _beside(s, *tiles):
    return lambda i: jnp.concatenate([t[s, i] for t in tiles], axis=0)


def _coarse_kernel(t1, t2, t3, f1, f2, f3, xm2, xp2, Ae, Ao, Be, Bo, ahead_of, raw, beyond, cs, c0, c1):
    g, yb, zb = _position()
    ring, fold = _ring_mask(g, zb), _fold_mask(yb)
    De, Do = D = [_beside(s, t1, t2, t3) for s in range(2)]
    far_e, far_o = [_beside(s, f1, f2, f3) for s in range(2)]

    row = _iota((8, LANES), 0)

    def near(i, s):
        at, r = slice(8 * (i // 2), 8 * (i // 2) + 8), 4 * s + 2 * (i % 2)
        return jnp.where(row < 4, _roll(xp2[at, :], -r, 0), _roll(xm2[at, :], 6 - r, 0))

    def ahead(q, s):
        c, slot = divmod(q - 2, 4)
        lo = _roll(near(12 + c, s), 4 * (3 - slot), 1)
        hi = _roll(near(14 + c, s), -4 * slot, 1)
        return [lo, near(2 * (q - 2), s), near(2 * (q - 2) + 1, s), hi]

    tasks = [(q, s) for q in range(2, 5) for s in range(2)]
    for (q, s), rows in zip(tasks, _unfold([(ahead(q, s), ahead(9 - q, s)) for q, s in tasks])):
        m = _outer_mask(ring[:8], fold, q)
        for r in range(8):
            _store(ahead_of.at[s], 8 * q + r, rows[r] * m, FINE - 1)

    def patch(rows, pairs):
        lane = _iota((24, LANES), 1) % 64
        sums = []
        for i in rows:
            f = 2 * i - 15
            e, o = far_e(f) + far_e(f + 1), far_o(f) + far_o(f + 1)
            sums.append((e, o, e + o, (far_e(f - 1) + far_e(f + 2)) + (far_o(f - 1) + far_o(f + 2))))
        turned = [_roll(o, 1, 0) + _roll(e, -1, 0) for e, o, _, _ in sums]
        hs = [(1.0 - 3.0 * W) * fp + W * (outer + t) for (_, _, fp, outer), t in zip(sums, turned)]
        ends = [(_roll(fp, -3, 1), _roll(fp, 2, 1)) for _, _, fp, _ in sums]
        sides = []
        for (_, _, fp, _), h, pair in zip(sums, hs, pairs):
            lo = _roll(h, -2, 1) + _roll(h, -3, 1) + W * (_roll(fp, -1, 1) + pair)
            hi = _roll(h, 2, 1) + _roll(h, 3, 1) + W * (_roll(fp, 1, 1) + pair)
            sides.append((lo, hi))
        for i, (lo, hi) in zip(rows, sides):
            low = jnp.where(lane == 0, lo, _roll(lo, 1, 1))
            high = jnp.where(lane == 63, hi, _roll(hi, -1, 1))
            beyond[i - 10] = jnp.where(lane < 32, low, high) * 0.125
        return ends

    def put_source(i, c):
        raw[i] = c

    whole = [lambda y, s=s, v=v: jnp.concatenate([ahead_of[s, y], v(y)], axis=0) for s, v in enumerate(D)]
    args = (whole, 32, W, 1.0 - 5.0 * W, None)
    _restrict(*args, 3, 7, put_source, None, 4)
    _restrict(*args, 10, 10, put_source, patch, 4)
    _sweep_three(g, yb, zb, lambda i: raw[i], lambda i: beyond[i], cs, c0, c1)
    base = [lambda i, v=v: W * v(i) for v in D]
    step_masks = _step_masks(g, yb, zb)
    _correct_and_smooth(step_masks, base, D, lambda i: c0[i], Be, Bo, 7, 13, 4)
    _smooth(step_masks, (lambda i: Be[i], lambda i: Bo[i]), D, Ae, Ao, 15, 25, 9)


def _ones_kernel(Te, To, Be, Bo, cs, c0, c1):
    g, yb, zb = _position()
    one = jnp.ones((32, LANES), F32)
    _sweep_three(g, yb, zb, lambda i: one, lambda i: one[8:], cs, c0, c1)
    step_masks = _step_masks(g, yb, zb)
    _correct_and_smooth(step_masks, None, None, lambda i: c0[i], Be, Bo, 7, 13, 4)
    _smooth(step_masks, (lambda i: Be[i], lambda i: Bo[i]), None, Te, To, 15, 25, 9)


def _sweep_three(g, yb, zb, source, beyond, cs, c0, c1):
    ring, fold = BETA * _ring_mask(g, zb), _fold_mask(yb)
    outside = ring * _tall(fold, 32)
    lane = _iota((24, LANES), 1) % 64
    has_below, has_above = (zb > 0).astype(F32), (zb < 3).astype(F32)
    row = _iota((24, LANES), 0) - 8
    z_ends = jnp.where(lane < 2, has_below, jnp.where(lane >= 62, has_above, 0.0))
    beyond_mask = BETA * z_ends * _inside(row, g * 8, 64)
    beyond_outside = beyond_mask * _tall(fold, 24)
    mask = _ring_mask(g, zb)[8:]
    masks = (mask * _tall(fold, 24), mask)

    scaled = _lazily(lambda i: source(i) * (outside if i < 12 else ring))
    for i in range(4, COARSE):
        c = scaled(i)
        after = _roll(c, 64, 1) if i == COARSE - 1 else scaled(i + 1)
        near = (_roll(c, 1, 0) + _roll(c, -1, 0) + (scaled(i - 1) + after))[8:]
        c = c[8:]
        ends = None
        if i >= 10:
            ends = beyond(i - 10) * (beyond_outside if i < 12 else beyond_mask)
        cs[i] = c
        _store(c0, i, c + _sweep(c, near, lane, ends) * masks[i >= 12], COARSE - 1)
    _sweep_rows(c0, c1, cs, 5, masks)
    _sweep_rows(c1, c0, cs, 6, masks)


def _sweep(c, near, lane, ends):
    before, after = _roll(c, 2, 1), _roll(c, -2, 1)
    if ends is not None:
        before = jnp.where(lane < 2, ends, before)
        after = jnp.where(lane >= 62, ends, after)
    return 0.2 * c + W * (near + (before + after))


def _sweep_rows(src, dst, cs, first, masks):
    for i in range(first, COARSE):
        c = src[i]
        near = _roll(c, 1, 0) + _roll(c, -1, 0) + (src[i - 1] + src[i + 1])
        _store(dst, i, cs[i] + _sweep(c, near, None, None) * masks[i >= 12], COARSE - 1)


def _restrict(fields, rows, near, centre, more, first, count, store, patch, size):
    lane = _iota((rows, LANES), 1)
    even = lane % 2 == 0

    for start in range(first, first + count, size):
        even_at, odd_at = (_lazily(lambda u, v=v, start=start: v(2 * start + u)) for v in fields)
        sums = []
        us = range(min(size, first + count - start))
        for u in us:
            y = 2 * u
            ee, eo = even_at(y) + even_at(y + 1), odd_at(y) + odd_at(y + 1)
            outer = (even_at(y - 1) + even_at(y + 2)) + (odd_at(y - 1) + odd_at(y + 2))
            sums.append((ee, eo, ee + eo, outer))
        turned = [_roll(eo, 1, 0) + _roll(ee, -1, 0) for ee, eo, _, _ in sums]
        hs = []
        for u, ((_, _, pair, outer), t) in enumerate(zip(sums, turned)):
            h = (centre + 2.0 * near) * pair + near * (outer + t)
            hs.append(h if more is None else h + more(2 * (start + u)))
        sides = [(_roll(pair, 1, 1), _roll(pair, -2, 1)) for _, _, pair, _ in sums]
        if patch is not None:
            ends = patch([start + u for u in us], [pair[8:] for _, _, pair, _ in sums])
            for u, ((before, after), (low, high)) in enumerate(zip(sides, ends)):
                low = jnp.where(lane[8:] % 64 == 0, low, before[8:])
                high = jnp.where(lane[8:] % 64 == 62, high, after[8:])
                sides[u] = (
                    jnp.concatenate([before[:8], low], axis=0),
                    jnp.concatenate([after[:8], high], axis=0),
                )
        cs = [h + _roll(h, -1, 1) + near * (before + after) for h, (before, after) in zip(hs, sides)]
        cs = [jnp.where(even, c, _roll(c, 1, 1)) * 0.125 for c in cs]
        for u, c in enumerate(cs):
            store(start + u, c)


def _step_masks(g, yb, zb):
    mask = _ring_mask(g, zb)[8:]
    masks = (mask * _tall(_fold_mask(yb), 24), mask)
    return masks, [0.2 * m for m in masks], [W * m for m in masks]


def _of_row(pair, i, own_first):
    if isinstance(i, int):
        return pair[i >= own_first]
    return jnp.where(i < own_first, *pair)


def _relax(even, odd, i, n, store, batch=2):
    for first in range(0, n, batch):
        us = range(first, min(first + batch, n))
        turned = []
        for u in us:
            e, o = even(u), odd(u)
            turned.append((_roll(e, 1, 1), _roll(e, -1, 1), _roll(o, 1, 1), _roll(o, -1, 1), _roll(o, 1, 0), _roll(e, -1, 0)))
        for u, (e1, e2, o1, o2, before, after) in zip(us, turned):
            e, o = even(u), odd(u)
            ye = ((even(u - 1) + even(u + 1)) + (e1 + e2)) + (o + before)
            yo = ((odd(u - 1) + odd(u + 1)) + (o1 + o2)) + (e + after)
            store(i + u, e, o, ye, yo)


def _smooth_to(step_masks, D, dst_e, dst_o):
    def store(i, e, o, ye, yo):
        m, n = _of_row(step_masks[1], i, 24), _of_row(step_masks[2], i, 24)
        if D is not None:
            ye, yo = ye + D[0](i), yo + D[1](i)
        _store(dst_e, i, e * m + ye * n, FINE - 1)
        _store(dst_o, i, o * m + yo * n, FINE - 1)

    return store


def _smooth(step_masks, src, D, dst_e, dst_o, first, count, size):
    def fn(i, n):
        even, odd = (_lazily(lambda u, v=v: v(i + u)) for v in src)
        _relax(even, odd, i, n, _smooth_to(step_masks, D, dst_e, dst_o))

    _blocks(first, count, size, fn)


def _correct_and_smooth(step_masks, base, D, correction, dst_e, dst_o, first, count, size):
    def fn(start, n):
        i = 2 * start
        c = _lazily(lambda u: correction(start + u))
        if base is None:
            even = odd = lambda u: c(u // 2)
        else:
            even, odd = (_lazily(lambda u, v=v: v(i + u) + c(u // 2)) for v in base)
        _relax(even, odd, i, 2 * n, _smooth_to(step_masks, D, dst_e, dst_o))

    _blocks(first, count, size, fn)


def _cycle_kernel(
    order, t1, t2, t3, Re, Ro, Te, To, part, across, pot, res, Be, Bo, cs, c0, c1, boxes, place, sem
):
    g, yb, zb = _position()
    fetch = pltpu.make_async_copy(order, place, sem.at[0])
    fetch.start()
    totals = part[...] + across[...]
    mean1 = jnp.sum(totals[0:1]) * (1.0 / CELLS)
    mean2 = jnp.sum(totals[1:2]) * (1.0 / CELLS)
    step_masks = _step_masks(g, yb, zb)
    masks = step_masks[0]

    all_of = lambda ref: lambda i: ref[i]

    De, Do = D = [_beside(s, t1, t2, t3) for s in range(2)]
    A = (lambda i: Re[i] - mean1 * Te[i], lambda i: Ro[i] - mean1 * To[i])

    def again(i, c):
        _store(cs, i, (c - mean2) * (_of_row(masks, i, 12) * BETA), COARSE - 1)

    pair_of = lambda i: (De(i) + De(i + 1)) + (Do(i) + Do(i + 1))
    _restrict(A, 24, 1.0, -5.0, pair_of, 8, 12, again, None, 4)
    _sweep_rows(cs, c0, cs, 9, masks)
    _sweep_rows(c0, c1, cs, 10, masks)
    _sweep_rows(c1, c0, cs, 11, masks)
    _correct_and_smooth(step_masks, A, D, all_of(c0), Be, Bo, 11, 9, 5)

    fetch.wait()
    box_of = [place[h, 0] for h in range(4)]
    for q in (3, 4):
        i0 = 8 * q
        even = _lazily(lambda u: Be[i0 + u])
        odd = _lazily(lambda u: Bo[i0 + u])
        left = ([], [])

        def store(i, e, o, ye, yo):
            left[0].append(t2[0, i] - (6.0 * e - ye)[8:16])
            left[1].append(t2[1, i] - (6.0 * o - yo)[8:16])

        _relax(even, odd, i0, 8, store)
        tasks = [(f, s) for f in range(2) for s in range(2)]
        done = [[v(u)[8:16] for u in range(8)] for v in (even, odd)]
        groups = [(done, left)[f][s] for f, s in tasks]
        for (f, s), sides in zip(tasks, _refold(groups)):
            for o, pieces in zip((q - 3, 6 - q), sides):
                for h in range(2):
                    at = BLOCK * ((f * 4 + o) * 2 + h) + s
                    boxes[pl.ds(at, 8, stride=2), :] = pieces[h]
    for f, out in enumerate((pot, res)):
        for o in range(4):
            for h in range(2):
                v = _blk(boxes, (f * 4 + o) * 2 + h)
                out[box_of[(o // 2) * 2 + h], :, (o % 2) * LANES : (o % 2 + 1) * LANES] = v


def _lazily(fn):
    made = {}

    def get(u):
        if u not in made:
            made[u] = fn(u)
        return made[u]

    return get


def _shape(*dims):
    return jax.ShapeDtypeStruct(dims, F32)


def _rows(n):
    return _shape(n, LANES)


VMEM = pl.BlockSpec(memory_space=pltpu.VMEM)
HBM = pl.BlockSpec(memory_space=pltpu.HBM)


def _call(kernel, specs, outs, scratch=(), us=0.1, grant=40.0):
    return pl.pallas_call(
        kernel,
        out_shape=outs,
        in_specs=specs,
        out_specs=[VMEM] * len(outs),
        scratch_shapes=scratch,
        cost_estimate=pl.CostEstimate(flops=0, transcendentals=0, bytes_accessed=int(us * 3.5e6)),
        compiler_params=pltpu.CompilerParams(vmem_limit_bytes=int(grant * 2**20)),
    )


def _y_shift(n):
    return [(4 * y + z, 4 * ((y + n) % 4) + z) for y in range(4) for z in range(4)]


def _z_shift(n):
    return [(4 * y + z, 4 * y + (z + n) % 4) for y in range(4) for z in range(4)]


def _x_shift(n):
    return [(x, (x + n) % 8) for x in range(8)]


def _body(weights, divergence, box_coords, neighbors):
    coords = box_coords.T
    raw, weight = _call(
        _fetch_kernel,
        [HBM, HBM],
        [_shape(*divergence.shape), _shape(*weights.shape[1:])],
        [pltpu.SemaphoreType.DMA((2,))],
        us=1.0,
        grant=53.79,
    )(divergence, weights)
    own, sums, order = _call(
        _sort_kernel,
        [VMEM] * 3,
        [_rows(128), _rows(8), jax.ShapeDtypeStruct((8, LANES), jnp.int32)],
        [pltpu.VMEM((128, LANES), F32)],
    )(coords, raw, weight)
    across = lax.ppermute(sums, "dev", _y_shift(2))
    up, down = _call(_y_kernel, [VMEM] * 2, [_rows(Y_MESSAGE), _rows(Y_MESSAGE)])(own, sums)
    below = lax.ppermute(up, "dev", _y_shift(1))
    above = lax.ppermute(down, "dev", _y_shift(-1))

    plane = pltpu.VMEM((COARSE + 1, 24, LANES), F32)
    fine = _shape(FINE + 1, 24, LANES)
    inner = pltpu.VMEM((FINE + 1, 24, LANES), F32)
    ones = _call(_ones_kernel, [], [fine, fine], [inner, inner, plane, plane, plane], us=1.0)()
    sums, ones = lax.optimization_barrier((sums, ones))
    total = _call(_total_kernel, [VMEM] * 4, [_rows(8)])(sums, below, above, across)[0]
    zacross = lax.ppermute(total, "dev", _z_shift(2))
    up, down = _call(_z_kernel, [VMEM] * 4, [_rows(168), _rows(168)])(own, below, above, total)
    zbelow = lax.ppermute(up, "dev", _z_shift(1))
    zabove = lax.ppermute(down, "dev", _z_shift(-1))

    mine, up, down, high, low, part = _call(
        _x_kernel,
        [VMEM] * 7,
        [_rows(640), _rows(MESSAGE), _rows(MESSAGE), _rows(72), _rows(72), _rows(8)],
    )(own, below, above, zbelow, zabove, total, zacross)
    xm1 = lax.ppermute(up, "grp", _x_shift(1))
    xp1 = lax.ppermute(down, "grp", _x_shift(-1))
    xm2 = lax.ppermute(high, "grp", _x_shift(2))
    xp2 = lax.ppermute(low, "grp", _x_shift(-2))
    bricks = []
    for ref, at, rows in (
        (xm1, functools.partial(_Sent, from_below=True), slice(8, 16)),
        (mine, _Own, slice(16, 24)),
        (xp1, functools.partial(_Sent, from_below=False), slice(24, 32)),
    ):
        kernel = functools.partial(_brick_kernel, at=at, rows=rows)
        outs = [_shape(2, FINE + 1, 8, LANES), _shape(2, 26, 8, LANES)]
        bricks.append(_call(kernel, [VMEM], outs, us=0.8)(ref))
    part, bricks = lax.optimization_barrier((part, bricks))
    tiles, fars = zip(*bricks)
    part, send = _call(_window_kernel, [VMEM] * 5, [_rows(8), _rows(8)])(part, xm1, xp1, xm2, xp2)
    xacross = lax.ppermute(send, "grp", [(x, (x + 3 - 6 * (x % 2)) % 8) for x in range(8)])

    start = _call(
        _coarse_kernel,
        [VMEM] * 8,
        [fine, fine],
        [
            inner,
            inner,
            pltpu.VMEM((2, FINE + 1, 8, LANES), F32),
            pltpu.VMEM((COARSE, 32, LANES), F32),
            pltpu.VMEM((12, 24, LANES), F32),
            plane,
            plane,
            plane,
        ],
        us=3,
    )(*tiles, *fars, xm2, xp2)

    boxes = pltpu.VMEM((16 * BLOCK, LANES), F32)
    pot, res = _call(
        _cycle_kernel,
        [VMEM] * 10,
        [_shape(4, 16, 256), _shape(4, 16, 256)],
        [inner, inner, plane, plane, plane, boxes, pltpu.SMEM((8, LANES), jnp.int32), pltpu.SemaphoreType.DMA((1,))],
    )(order, *tiles, *start, *ones, part, xacross)
    return pot, res


def solution(mesh):
    table = _mean_weights()

    def body(divergence, box_coords, neighbors):
        return _body(jnp.asarray(table), divergence, box_coords, neighbors)

    split = P(("grp", "dev"), None, None)
    return jax.shard_map(
        body, mesh=mesh, in_specs=(split, P(), P()), out_specs=(split, split), check_vma=False
    )
```

time: 1100 us -> 36.3 us (0.03)
  other arithmetic: 366 us -> 0 us
  waiting for transfers between devices: 261 us -> 5.62 us
  local copies, waits for them, and re-layouts: 173 us -> 0.01 us
  starting transfers between devices: 159 us -> 19.9 us
  blocking collectives: 120 us -> 0 us
  between operations: 17.6 us -> 0.72 us
    unnamed x5 -> x0, other arithmetic: 350 us -> none
    gather x18 -> x0, local copies, waits for them, and re-layouts: 139 us -> none  [the longest x4 135 us: extract_blocks(): values = grid_field[jnp.clip(z_index, 0, layers - 1), x_index, y_index]]
    ppermute x56 -> x11, starting transfers between devices: 159 us -> 19.9 us  [the longest x1 3.78 us: _body(): xp1 = lax.ppermute(down, 'grp', _x_shift(-1))]
    psum x2 -> x0, waiting for transfers between devices: 122 us -> none  [body(): coarse_source = lax.psum(partial_slab, 'grp')]
    all_gather x2 -> x0, waiting for transfers between devices: 112 us -> none  [body(): lax.all_gather(correction, 'dev', axis=0, tiled=True)]
    psum x2 -> x0, blocking collectives: 67.9 us -> none  [body(): source_total = lax.psum(jnp.sum(coarse_source), 'dev')]
    all_gather x2 -> x0, blocking collectives: 52.1 us -> none  [body(): shard_piece = lax.all_gather(blocks, 'dev', axis=0, tiled=True)]
    ppermute x56 -> x11, waiting for transfers between devices: 27 us -> 5.62 us  [the longest x1 2.53 us: _body(): zacross = lax.ppermute(total, 'dev', _z_shift(2))]
  transfers between devices with their start and end apart: 60 -> 11, of which waited for: 17 -> 4; matrix products, arithmetic and copies ran while one was open for 1% -> 0% of each run, Pallas kernels for 0% -> 18%
where the time goes in v1:
time: 36.3 us; the launch traced here: 36.1 us
  starting transfers between devices  19.9 us (55%)
  Pallas kernels  9.89 us (27%)
  waiting for transfers between devices  5.62 us (15%)
  between operations  0.72 us (2%)
    ppermute x1, starting transfers between devices, _body(): xp1 = lax.ppermute(down, 'grp', _x_shift(-1))  3.78 us
    pallas_call x1, Pallas kernels, _body(): _call(_coarse_kernel, [VMEM] * 8, [fine, fine], [inner, inner, pltpu.VMEM...  3.05 us
    ppermute x1, waiting for transfers between devices, _body(): zacross = lax.ppermute(total, 'dev', _z_shift(2))  2.53 us
    ppermute x1, starting transfers between devices, _body(): lax.ppermute(send, 'grp', [(x, (x + 3 - 6 * (x % 2)) % 8) for x in range(...  2.34 us
    ppermute x1, starting transfers between devices, _body(): below = lax.ppermute(up, 'dev', _y_shift(1))  2.14 us
    pallas_call x1, Pallas kernels, _body(): _call(_cycle_kernel, [VMEM] * 10, [_shape(4, 16, 256), _shape(4, 16, 256)...  2.01 us
    pallas_call x3, Pallas kernels, _body(): bricks.append(_call(kernel, [VMEM], outs, us=0.8)(ref))  1.99 us
    ppermute x1, starting transfers between devices, _body(): xm2 = lax.ppermute(high, 'grp', _x_shift(2))  1.64 us
  transfers between devices with their start and end apart: 11, of which 4 were waited for; matrix products, arithmetic and copies ran while one was open for 0% of the time, Pallas kernels for 18%

profile of v1, /device:TPU:1, one launch (start us, length us, event | category | flops | bytes accessed | tf_op | source)
XLA Modules:
  0.0 36.1 jit_solution(6255862465787751216)
XLA Ops:
  0.6 0.9 %shard_map.50 = (f32[4,16,256]{2,1,0:T(8,128)S(1)}, f32[8,16,128]{2,1,0:T(8,128)S(1)}) custom-call(f32[4,16,256]{2,1,0:T(8,128)} %div.1, f32[27,8,16,128]{3,2,1,0:T(8,128)} %constant.2.clone.w2), custom_call_target="tpu_custom_call" | custom-call | bytes 3500000 | tf_op jit(solution)/shard_map/pallas_call | solution.py:749
  1.6 0.2 shard_map.51
  1.8 2.1 %collective-permute-start = (f32[88,128]{1,0:T(8,128)S(1)}, f32[88,128]{1,0:T(8,128)S(1)}, u32[]{:S(2)}, u32[]{:S(2)}) collective-permute-start(f32[88,128]{1,0:T(8,128)S(1)} %get-tuple-element.44), channel_id=1, source_target_pairs={{0,4},{1,5},{2,6},{3,7},{4,8},{5,9},{6,10},{7,11},{8,12},{9,13},{1... | collective-permute-start | bytes 135176 | tf_op jit(solution)/shard_map/ppermute | solution.py:765
  4.0 1.5 %collective-permute-start.1 = (f32[88,128]{1,0:T(8,128)S(1)}, f32[88,128]{1,0:T(8,128)S(1)}, u32[]{:S(2)}, u32[]{:S(2)}) collective-permute-start(f32[88,128]{1,0:T(8,128)S(1)} %get-tuple-element.45), channel_id=1, source_target_pairs={{0,12},{1,13},{2,14},{3,15},{4,0},{5,1},{6,2},{7,3},{8,4},{9,5},{1... | collective-permute-start | bytes 135176 | tf_op jit(solution)/shard_map/ppermute | solution.py:766
  5.5 1.6 %collective-permute-start.2 = (f32[8,128]{1,0:T(8,128)S(1)}, f32[8,128]{1,0:T(8,128)S(1)}, u32[]{:S(2)}, u32[]{:S(2)}) collective-permute-start(f32[8,128]{1,0:T(8,128)S(1)} %get-tuple-element.48.sums), channel_id=1, source_target_pairs={{0,8},{1,9},{2,10},{3,11},{4,12},{5,13},{6,14},{7,15},{8,0},{9,1},... | collective-permute-start | bytes 12296 | tf_op jit(solution)/shard_map/ppermute | solution.py:763
  7.0 1.4 %shard_map.53 = (f32[41,24,128]{2,1,0:T(8,128)S(1)}, f32[41,24,128]{2,1,0:T(8,128)S(1)}) custom-call(), custom_call_target="tpu_custom_call" | custom-call | bytes 3500000 | tf_op jit(solution)/shard_map/pallas_call | solution.py:771
  8.5 1.0 %collective-permute-done.2.across = f32[8,128]{1,0:T(8,128)S(1)} collective-permute-done((f32[8,128]{1,0:T(8,128)S(1)}, f32[8,128]{1,0:T(8,128)S(1)}, u32[]{:S(2)}, u32[]{:S(2)}) %collective-permute-start.2) | collective-permute-done | bytes 4128 | tf_op jit(solution)/shard_map/ppermute | solution.py:763
  9.5 0.1 shard_map.55
  9.6 1.2 %collective-permute-start.3 = (f32[168,128]{1,0:T(8,128)S(1)}, f32[168,128]{1,0:T(8,128)S(1)}, u32[]{:S(2)}, u32[]{:S(2)}) collective-permute-start(f32[168,128]{1,0:T(8,128)S(1)} %get-tuple-element.49), channel_id=1, source_target_pairs={{0,1},{1,2},{2,3},{3,0},{4,5},{5,6},{6,7},{7,4},{8,9},{9,10},{10,1... | collective-permute-start | bytes 258056 | tf_op jit(solution)/shard_map/ppermute | solution.py:776
  10.8 1.5 %collective-permute-start.4 = (f32[168,128]{1,0:T(8,128)S(1)}, f32[168,128]{1,0:T(8,128)S(1)}, u32[]{:S(2)}, u32[]{:S(2)}) collective-permute-start(f32[168,128]{1,0:T(8,128)S(1)} %get-tuple-element.50), channel_id=1, source_target_pairs={{0,3},{1,0},{2,1},{3,2},{4,7},{5,4},{6,5},{7,6},{8,11},{9,8},{10,9... | collective-permute-start | bytes 258056 | tf_op jit(solution)/shard_map/ppermute | solution.py:777
  12.3 1.5 %collective-permute-start.5 = (f32[8,128]{1,0:T(8,128)S(1)}, f32[8,128]{1,0:T(8,128)S(1)}, u32[]{:S(2)}, u32[]{:S(2)}) collective-permute-start(f32[8,128]{1,0:T(8,128)S(1)} %shard_map.54.total), channel_id=1, source_target_pairs={{0,2},{1,3},{2,0},{3,1},{4,6},{5,7},{6,4},{7,5},{8,10},{9,11},{10,... | collective-permute-start | bytes 12296 | tf_op jit(solution)/shard_map/ppermute | solution.py:774
  13.8 2.5 %collective-permute-done.5.across = f32[8,128]{1,0:T(8,128)S(1)} collective-permute-done((f32[8,128]{1,0:T(8,128)S(1)}, f32[8,128]{1,0:T(8,128)S(1)}, u32[]{:S(2)}, u32[]{:S(2)}) %collective-permute-start.5) | collective-permute-done | bytes 4128 | tf_op jit(solution)/shard_map/ppermute | solution.py:774
  16.5 3.8 %collective-permute-start.7 = (f32[520,128]{1,0:T(8,128)S(1)}, f32[520,128]{1,0:T(8,128)S(1)}, u32[]{:S(2)}, u32[]{:S(2)}) collective-permute-start(f32[520,128]{1,0:T(8,128)S(1)} %get-tuple-element.58), channel_id=1, source_target_pairs={{0,112},{16,0},{32,16},{48,32},{64,48},{80,64},{96,80},{112,96},{1... | collective-permute-start | bytes 798728 | tf_op jit(solution)/shard_map/ppermute | solution.py:785
  20.3 1.6 %collective-permute-start.6 = (f32[520,128]{1,0:T(8,128)S(1)}, f32[520,128]{1,0:T(8,128)S(1)}, u32[]{:S(2)}, u32[]{:S(2)}) collective-permute-start(f32[520,128]{1,0:T(8,128)S(1)} %get-tuple-element.52), channel_id=1, source_target_pairs={{0,16},{16,32},{32,48},{48,64},{64,80},{80,96},{96,112},{112,0},{1... | collective-permute-start | bytes 798728 | tf_op jit(solution)/shard_map/ppermute | solution.py:784
  21.9 1.6 %collective-permute-start.8 = (f32[72,128]{1,0:T(8,128)S(1)}, f32[72,128]{1,0:T(8,128)S(1)}, u32[]{:S(2)}, u32[]{:S(2)}) collective-permute-start(f32[72,128]{1,0:T(8,128)S(1)} %get-tuple-element.67), channel_id=1, source_target_pairs={{0,32},{16,48},{32,64},{48,80},{64,96},{80,112},{96,0},{112,16},{1... | collective-permute-start | bytes 110600 | tf_op jit(solution)/shard_map/ppermute | solution.py:786
  23.5 1.0 %collective-permute-start.9 = (f32[72,128]{1,0:T(8,128)S(1)}, f32[72,128]{1,0:T(8,128)S(1)}, u32[]{:S(2)}, u32[]{:S(2)}) collective-permute-start(f32[72,128]{1,0:T(8,128)S(1)} %get-tuple-element.68), channel_id=1, source_target_pairs={{0,96},{16,112},{32,0},{48,16},{64,32},{80,48},{96,64},{112,80},{1... | collective-permute-start | bytes 110600 | tf_op jit(solution)/shard_map/ppermute | solution.py:787
  24.6 0.6 %shard_map.58 = (f32[2,41,8,128]{3,2,1,0:T(8,128)S(1)}, f32[2,26,8,128]{3,2,1,0:T(8,128)S(1)}) custom-call(f32[640,128]{1,0:T(8,128)S(1)} %get-tuple-element.55.ref), custom_call_target="tpu_custom_call" | custom-call | bytes 2800000 | tf_op jit(solution)/shard_map/pallas_call | solution.py:796
  25.2 1.0 %collective-permute-done.7.ref.xp1 = f32[520,128]{1,0:T(8,128)S(1)} collective-permute-done((f32[520,128]{1,0:T(8,128)S(1)}, f32[520,128]{1,0:T(8,128)S(1)}, u32[]{:S(2)}, u32[]{:S(2)}) %collective-permute-start.7) | collective-permute-done | bytes 266272 | tf_op jit(solution)/shard_map/ppermute | solution.py:785
  26.3 0.7 %shard_map.59 = (f32[2,41,8,128]{3,2,1,0:T(8,128)S(1)}, f32[2,26,8,128]{3,2,1,0:T(8,128)S(1)}) custom-call(f32[520,128]{1,0:T(8,128)S(1)} %collective-permute-done.7.ref.xp1), custom_call_target="tpu_custom_call" | custom-call | bytes 2800000 | tf_op jit(solution)/shard_map/pallas_call | solution.py:796
  27.0 0.7 %shard_map.57 = (f32[2,41,8,128]{3,2,1,0:T(8,128)S(1)}, f32[2,26,8,128]{3,2,1,0:T(8,128)S(1)}) custom-call(f32[520,128]{1,0:T(8,128)S(1)} %collective-permute-done.6.ref.xm1), custom_call_target="tpu_custom_call" | custom-call | bytes 2800000 | tf_op jit(solution)/shard_map/pallas_call | solution.py:796
  27.6 1.1 %collective-permute-done.8.xm2 = f32[72,128]{1,0:T(8,128)S(1)} collective-permute-done((f32[72,128]{1,0:T(8,128)S(1)}, f32[72,128]{1,0:T(8,128)S(1)}, u32[]{:S(2)}, u32[]{:S(2)}) %collective-permute-start.8) | collective-permute-done | bytes 36896 | tf_op jit(solution)/shard_map/ppermute | solution.py:786
  28.7 2.3 %collective-permute-start.10 = (f32[8,128]{1,0:T(8,128)S(1)}, f32[8,128]{1,0:T(8,128)S(1)}, u32[]{:S(2)}, u32[]{:S(2)}) collective-permute-start(f32[8,128]{1,0:T(8,128)S(1)} %get-tuple-element.75), channel_id=1, source_target_pairs={{0,48},{16,96},{32,80},{48,0},{64,112},{80,32},{96,16},{112,64},{1... | collective-permute-start | bytes 12296 | tf_op jit(solution)/shard_map/ppermute | solution.py:800
  31.1 3.1 %shard_map.60 = (f32[41,24,128]{2,1,0:T(8,128)S(1)}, f32[41,24,128]{2,1,0:T(8,128)S(1)}) custom-call(f32[2,41,8,128]{3,2,1,0:T(8,128)S(1)} %get-tuple-element.61.t1, f32[2,41,8,128]{3,2,1,0:T(8,128)S(1)} %get-tuple-element.62.t2, f32[2,41,8,128]{3,2,1,0:T(8,128)S(1)} %get-tuple-element.63.t3, f32[2,26,8,128]{3,2,1,0:T(8,128)S(1)} %get-tuple-element.64.f1, ...), custom_call_target="tpu_custom_call" | custom-call | bytes 10500000 | tf_op jit(solution)/shard_map/pallas_call | solution.py:802
  34.1 2.0 %shard_map.62 = (f32[4,16,256]{2,1,0:T(8,128)}, f32[4,16,256]{2,1,0:T(8,128)}) custom-call(s32[8,128]{1,0:T(8,128)S(1)} %get-tuple-element.41.order, f32[2,41,8,128]{3,2,1,0:T(8,128)S(1)} %get-tuple-element.61.t1, f32[2,41,8,128]{3,2,1,0:T(8,128)S(1)} %get-tuple-element.62.t2, f32[2,41,8,128]{3,2,1,0:T(8,128)S(1)} %get-tuple-element.63.t3, ...), custom_call_target="tpu_custom_call" | custom-call | bytes 350000 | tf_op jit(solution)/shard_map/pallas_call | solution.py:820
  (13 shorter events, 0.2 us)
Async XLA Ops:
  0.6 0.9 %copy-start = (s32[512,3]{0,1:T(4,128)S(1)}, s32[512,3]{0,1:T(4,128)}, u32[]{:S(2)}) copy-start(s32[512,3]{0,1:T(4,128)} %param.5) | copy-start | bytes 18436
  1.8 7.6 %collective-permute-start = (f32[88,128]{1,0:T(8,128)S(1)}, f32[88,128]{1,0:T(8,128)S(1)}, u32[]{:S(2)}, u32[]{:S(2)}) collective-permute-start(f32[88,128]{1,0:T(8,128)S(1)} %get-tuple-element.44), channel_id=1, source_target_pairs={{0,4},{1,5},{2,6},{3,7},{4,8},{5,9},{6,10},{7,11},{8,12},{9,13},{1... | collective-permute-start | bytes 135176 | tf_op jit(solution)/shard_map/ppermute | solution.py:765
  4.0 5.5 %collective-permute-start.1 = (f32[88,128]{1,0:T(8,128)S(1)}, f32[88,128]{1,0:T(8,128)S(1)}, u32[]{:S(2)}, u32[]{:S(2)}) collective-permute-start(f32[88,128]{1,0:T(8,128)S(1)} %get-tuple-element.45), channel_id=1, source_target_pairs={{0,12},{1,13},{2,14},{3,15},{4,0},{5,1},{6,2},{7,3},{8,4},{9,5},{1... | collective-permute-start | bytes 135176 | tf_op jit(solution)/shard_map/ppermute | solution.py:766
  5.5 4.0 %collective-permute-start.2 = (f32[8,128]{1,0:T(8,128)S(1)}, f32[8,128]{1,0:T(8,128)S(1)}, u32[]{:S(2)}, u32[]{:S(2)}) collective-permute-start(f32[8,128]{1,0:T(8,128)S(1)} %get-tuple-element.48.sums), channel_id=1, source_target_pairs={{0,8},{1,9},{2,10},{3,11},{4,12},{5,13},{6,14},{7,15},{8,0},{9,1},... | collective-permute-start | bytes 12296 | tf_op jit(solution)/shard_map/ppermute | solution.py:763
  9.6 6.8 %collective-permute-start.3 = (f32[168,128]{1,0:T(8,128)S(1)}, f32[168,128]{1,0:T(8,128)S(1)}, u32[]{:S(2)}, u32[]{:S(2)}) collective-permute-start(f32[168,128]{1,0:T(8,128)S(1)} %get-tuple-element.49), channel_id=1, source_target_pairs={{0,1},{1,2},{2,3},{3,0},{4,5},{5,6},{6,7},{7,4},{8,9},{9,10},{10,1... | collective-permute-start | bytes 258056 | tf_op jit(solution)/shard_map/ppermute | solution.py:776
  10.8 5.5 %collective-permute-start.4 = (f32[168,128]{1,0:T(8,128)S(1)}, f32[168,128]{1,0:T(8,128)S(1)}, u32[]{:S(2)}, u32[]{:S(2)}) collective-permute-start(f32[168,128]{1,0:T(8,128)S(1)} %get-tuple-element.50), channel_id=1, source_target_pairs={{0,3},{1,0},{2,1},{3,2},{4,7},{5,4},{6,5},{7,6},{8,11},{9,8},{10,9... | collective-permute-start | bytes 258056 | tf_op jit(solution)/shard_map/ppermute | solution.py:777
  12.3 4.1 %collective-permute-start.5 = (f32[8,128]{1,0:T(8,128)S(1)}, f32[8,128]{1,0:T(8,128)S(1)}, u32[]{:S(2)}, u32[]{:S(2)}) collective-permute-start(f32[8,128]{1,0:T(8,128)S(1)} %shard_map.54.total), channel_id=1, source_target_pairs={{0,2},{1,3},{2,0},{3,1},{4,6},{5,7},{6,4},{7,5},{8,10},{9,11},{10,... | collective-permute-start | bytes 12296 | tf_op jit(solution)/shard_map/ppermute | solution.py:774
  16.5 9.8 %collective-permute-start.7 = (f32[520,128]{1,0:T(8,128)S(1)}, f32[520,128]{1,0:T(8,128)S(1)}, u32[]{:S(2)}, u32[]{:S(2)}) collective-permute-start(f32[520,128]{1,0:T(8,128)S(1)} %get-tuple-element.58), channel_id=1, source_target_pairs={{0,112},{16,0},{32,16},{48,32},{64,48},{80,64},{96,80},{112,96},{1... | collective-permute-start | bytes 798728 | tf_op jit(solution)/shard_map/ppermute | solution.py:785
  20.3 6.7 %collective-permute-start.6 = (f32[520,128]{1,0:T(8,128)S(1)}, f32[520,128]{1,0:T(8,128)S(1)}, u32[]{:S(2)}, u32[]{:S(2)}) collective-permute-start(f32[520,128]{1,0:T(8,128)S(1)} %get-tuple-element.52), channel_id=1, source_target_pairs={{0,16},{16,32},{32,48},{48,64},{64,80},{80,96},{96,112},{112,0},{1... | collective-permute-start | bytes 798728 | tf_op jit(solution)/shard_map/ppermute | solution.py:784
  21.9 6.8 %collective-permute-start.8 = (f32[72,128]{1,0:T(8,128)S(1)}, f32[72,128]{1,0:T(8,128)S(1)}, u32[]{:S(2)}, u32[]{:S(2)}) collective-permute-start(f32[72,128]{1,0:T(8,128)S(1)} %get-tuple-element.67), channel_id=1, source_target_pairs={{0,32},{16,48},{32,64},{48,80},{64,96},{80,112},{96,0},{112,16},{1... | collective-permute-start | bytes 110600 | tf_op jit(solution)/shard_map/ppermute | solution.py:786
  23.5 5.2 %collective-permute-start.9 = (f32[72,128]{1,0:T(8,128)S(1)}, f32[72,128]{1,0:T(8,128)S(1)}, u32[]{:S(2)}, u32[]{:S(2)}) collective-permute-start(f32[72,128]{1,0:T(8,128)S(1)} %get-tuple-element.68), channel_id=1, source_target_pairs={{0,96},{16,112},{32,0},{48,16},{64,32},{80,48},{96,64},{112,80},{1... | collective-permute-start | bytes 110600 | tf_op jit(solution)/shard_map/ppermute | solution.py:787
  28.7 5.4 %collective-permute-start.10 = (f32[8,128]{1,0:T(8,128)S(1)}, f32[8,128]{1,0:T(8,128)S(1)}, u32[]{:S(2)}, u32[]{:S(2)}) collective-permute-start(f32[8,128]{1,0:T(8,128)S(1)} %get-tuple-element.75), channel_id=1, source_target_pairs={{0,48},{16,96},{32,80},{48,0},{64,112},{80,32},{96,16},{112,64},{1... | collective-permute-start | bytes 12296 | tf_op jit(solution)/shard_map/ppermute | solution.py:800

commit v2 on v1

--- a/solution.py
+++ b/solution.py
@@ -180,7 +180,7 @@
         ref[160:168, :] = total[...]
 
 
-OUTER, TAIL, SUMS, MESSAGE = 384, 480, 512, 520
+OUTER, SUMS, MESSAGE = 384, 480, 488
 OWN_EY, OWN_COLS = 512, 576
 
 
@@ -193,6 +193,18 @@
     return out
 
 
+def _rows_far(near):
+    return _iota((8, LANES), 0) // 2 == (0 if near else 3)
+
+
+def _lower_lanes():
+    return _iota((8, LANES), 1) % 16 < 8
+
+
+def _hide(v, tile, near):
+    return jnp.where(_rows_far(near), _roll(v, 2 if near else -2, 0), tile)
+
+
 def _share(lo, hi, near):
     row, lane = _iota((8, LANES), 0), _iota((8, LANES), 1)
     middle = jnp.where(lane % 16 < 8, hi, lo)
@@ -202,6 +214,10 @@
 
 def _x_kernel(own, below, above, zbelow, zabove, total, across, mine, up, down, high, low, part):
     ext = lambda q, h: _ext(own, below, above, q, h)
+    extra = [ext(q, h) for q in (0, 9) for h in range(2)]
+    extra += [_blk(zbelow, 8), _blk(zbelow, 9), _blk(zabove, 8), _blk(zabove, 9)]
+    for i, v in enumerate(extra):
+        _put(mine, 32 + i, v)
     two_away = []
     for q in range(1, 9):
         pieces = (_blk(zbelow, q - 1), ext(q, 0), ext(q, 1), _blk(zabove, q - 1))
@@ -209,13 +225,21 @@
             _put(mine, (q - 1) * 4 + p, pieces[p])
         if 2 <= q <= 7:
             two_away += pieces[1:3]
-            for p in range(4):
-                _put(up, (q - 2) * 4 + p, pieces[p])
-                _put(down, (q - 2) * 4 + p, pieces[p])
+            for ref, near in ((up, 6), (down, 0)):
+                for p in (1, 2):
+                    _put(ref, (q - 2) * 4 + p, pieces[p])
+                for s in (0, 8):
+                    lo, hi = (pieces[p][s : s + 8] for p in (0, 3))
+                    far = _rows_far(near)
+                    at = (q - 2) * 64 + s
+                    ref[at : at + 8, :] = jnp.where(far & _lower_lanes(), hi, lo)
+                    ref[at + 48 : at + 56, :] = _hide(extra[q - 2][s : s + 8], hi, near)
             continue
         at = OUTER + (0 if q == 1 else 48)
         for ref, near in ((up, 6), (down, 0)):
-            ref[at : at + 16, :] = pieces[1]
+            for s in (0, 8):
+                hidden = extra[6 if q == 1 else 7][s : s + 8]
+                ref[at + s : at + s + 8, :] = _hide(hidden, pieces[1][s : s + 8], near)
             ref[at + 16 : at + 32, :] = pieces[2]
             for s in (0, 8):
                 ref[at + 32 + s : at + 40 + s, :] = _share(pieces[0][s : s + 8], pieces[3][s : s + 8], near)
@@ -226,15 +250,6 @@
         for i in range(0, 16, 2):
             a, b = two_away[i : i + 2]
             ref[4 * i : 4 * i + 8, :] = _rows_to([(a[:8], r), (b[:8], r), (a[8:], r), (b[8:], r)])
-    extra = [ext(q, h) for q in (0, 9) for h in range(2)]
-    extra += [_blk(zbelow, 8), _blk(zbelow, 9), _blk(zabove, 8), _blk(zabove, 9)]
-    for i, v in enumerate(extra):
-        _put(mine, 32 + i, v)
-    for ref, r in ((up, 6), (down, 0)):
-        for t in range(4):
-            rows = slice(8 * (t % 2), 8 * (t % 2) + 8)
-            tile = _rows_to([(v[rows], r) for v in extra[4 * (t // 2) : 4 * (t // 2) + 4]])
-            ref[TAIL + 8 * t : TAIL + 8 * t + 8, :] = tile
     t = total[...] + zbelow[160:168, :] + zabove[160:168, :] + across[...]
     part[...] = t
     for ref, at in ((up, SUMS), (down, SUMS), (high, 64), (low, 64)):
@@ -361,7 +376,8 @@
 
     def core(self, q, p, s):
         if 2 <= q <= 7:
-            return self.tile((q - 2) * 64 + 16 * p + 8 * s)
+            v = self.tile((q - 2) * 64 + 16 * p + 8 * s)
+            return jnp.where(_rows_far(self.first), self.core(q, 0, s), v) if p == 3 else v
         at = OUTER + (0 if q == 1 else 48) + 8 * s
         if p in (1, 2):
             return self.tile(at + 16 * (p - 1))
@@ -372,7 +388,8 @@
         return jnp.where(near, _roll(shared, -2 if self.first else 2, 0), shared)
 
     def short(self, i, s):
-        return _roll(self.tile(TAIL + 8 * (i // 4 * 2 + s)), self.first - 2 * (i % 4), 0)
+        at = i * 64 + 48 if i < 6 else OUTER + 48 * (i - 6)
+        return _roll(self.tile(at + 8 * s), -2 if self.first else 2, 0)
 
     def outer(self, i, s):
         return self.short(i, s)
@@ -395,7 +412,7 @@
 
 
 def _unpack_brick(at, mask, mask_far, fold, store, store_far):
-    for batch in ([(0, 0), (1, 0)], [(2, 0), (2, 1)], [(3, 0), (3, 1)], [(4, 0), (4, 1)]):
+    for batch in ([(0, 0), (1, 0), (2, 0)], [(3, 0), (4, 0), (2, 1)], [(3, 1), (4, 1)]):
         tasks = [(q, far, s) for q, far in batch for s in range(2)]
         groups = [
             [(_far_pieces if far else _pieces)(at, o, s) for o in (q, 9 - q)] for q, far, s in tasks
@@ -490,8 +507,8 @@
 
     whole = [lambda y, s=s, v=v: jnp.concatenate([ahead_of[s, y], v(y)], axis=0) for s, v in enumerate(D)]
     args = (whole, 32, W, 1.0 - 5.0 * W, None)
-    _restrict(*args, 3, 7, put_source, None, 4)
-    _restrict(*args, 10, 10, put_source, patch, 4)
+    _restrict(*args, 3, 7, put_source, None, 7)
+    _restrict(*args, 10, 10, put_source, patch, 5)
     _sweep_three(g, yb, zb, lambda i: raw[i], lambda i: beyond[i], cs, c0, c1)
     base = [lambda i, v=v: W * v(i) for v in D]
     step_masks = _step_masks(g, yb, zb)
@@ -596,7 +613,7 @@
     return jnp.where(i < own_first, *pair)
 
 
-def _relax(even, odd, i, n, store, batch=2):
+def _relax(even, odd, i, n, store, batch=3):
     for first in range(0, n, batch):
         us = range(first, min(first + batch, n))
         turned = []
@@ -663,7 +680,7 @@
         _store(cs, i, (c - mean2) * (_of_row(masks, i, 12) * BETA), COARSE - 1)
 
     pair_of = lambda i: (De(i) + De(i + 1)) + (Do(i) + Do(i + 1))
-    _restrict(A, 24, 1.0, -5.0, pair_of, 8, 12, again, None, 4)
+    _restrict(A, 24, 1.0, -5.0, pair_of, 8, 12, again, None, 6)
     _sweep_rows(cs, c0, cs, 9, masks)
     _sweep_rows(c0, c1, cs, 10, masks)
     _sweep_rows(c1, c0, cs, 11, masks)

time: 36.3 us -> 35.8 us (0.986)
  Pallas kernels: 9.89 us -> 9.46 us
  transfers between devices with their start and end apart: 11 -> 11, of which waited for: 4 -> 4; matrix products, arithmetic and copies ran while one was open for 0% -> 0% of each run, Pallas kernels for 18% -> 17%
where the time goes in v2:
time: 35.8 us; the launch traced here: 35.7 us
  starting transfers between devices  19.8 us (55%)
  Pallas kernels  9.46 us (26%)
  waiting for transfers between devices  5.67 us (16%)
  between operations  0.72 us (2%)
    ppermute x1, starting transfers between devices, _body(): xp1 = lax.ppermute(down, 'grp', _x_shift(-1))  3.78 us
    pallas_call x1, Pallas kernels, _body(): _call(_coarse_kernel, [VMEM] * 8, [fine, fine], [inner, inner, pltpu.VMEM...  2.84 us
    ppermute x1, waiting for transfers between devices, _body(): zacross = lax.ppermute(total, 'dev', _z_shift(2))  2.53 us
    ppermute x1, starting transfers between devices, _body(): lax.ppermute(send, 'grp', [(x, (x + 3 - 6 * (x % 2)) % 8) for x in range(...  2.26 us
    ppermute x1, starting transfers between devices, _body(): below = lax.ppermute(up, 'dev', _y_shift(1))  2.14 us
    pallas_call x1, Pallas kernels, _body(): _call(_cycle_kernel, [VMEM] * 10, [_shape(4, 16, 256), _shape(4, 16, 256)...  2.01 us
    pallas_call x3, Pallas kernels, _body(): bricks.append(_call(kernel, [VMEM], outs, us=0.8)(ref))  1.77 us
    ppermute x1, starting transfers between devices, _body(): xm2 = lax.ppermute(high, 'grp', _x_shift(2))  1.64 us
  transfers between devices with their start and end apart: 11, of which 4 were waited for; matrix products, arithmetic and copies ran while one was open for 0% of the time, Pallas kernels for 17%

profile of v2, /device:TPU:1, one launch (start us, length us, event | category | flops | bytes accessed | tf_op | source)
XLA Modules:
  0.0 35.7 jit_solution(500279359217225193)
XLA Ops:
  0.6 0.9 %shard_map.50 = (f32[4,16,256]{2,1,0:T(8,128)S(1)}, f32[8,16,128]{2,1,0:T(8,128)S(1)}) custom-call(f32[4,16,256]{2,1,0:T(8,128)} %div.1, f32[27,8,16,128]{3,2,1,0:T(8,128)} %constant.2.clone.w2), custom_call_target="tpu_custom_call" | custom-call | bytes 3500000 | tf_op jit(solution)/shard_map/pallas_call | solution.py:766
  1.6 0.2 shard_map.51
  1.8 2.1 %collective-permute-start = (f32[88,128]{1,0:T(8,128)S(1)}, f32[88,128]{1,0:T(8,128)S(1)}, u32[]{:S(2)}, u32[]{:S(2)}) collective-permute-start(f32[88,128]{1,0:T(8,128)S(1)} %get-tuple-element.44), channel_id=1, source_target_pairs={{0,4},{1,5},{2,6},{3,7},{4,8},{5,9},{6,10},{7,11},{8,12},{9,13},{1... | collective-permute-start | bytes 135176 | tf_op jit(solution)/shard_map/ppermute | solution.py:782
  4.0 1.5 %collective-permute-start.1 = (f32[88,128]{1,0:T(8,128)S(1)}, f32[88,128]{1,0:T(8,128)S(1)}, u32[]{:S(2)}, u32[]{:S(2)}) collective-permute-start(f32[88,128]{1,0:T(8,128)S(1)} %get-tuple-element.45), channel_id=1, source_target_pairs={{0,12},{1,13},{2,14},{3,15},{4,0},{5,1},{6,2},{7,3},{8,4},{9,5},{1... | collective-permute-start | bytes 135176 | tf_op jit(solution)/shard_map/ppermute | solution.py:783
  5.5 1.6 %collective-permute-start.2 = (f32[8,128]{1,0:T(8,128)S(1)}, f32[8,128]{1,0:T(8,128)S(1)}, u32[]{:S(2)}, u32[]{:S(2)}) collective-permute-start(f32[8,128]{1,0:T(8,128)S(1)} %get-tuple-element.48.sums), channel_id=1, source_target_pairs={{0,8},{1,9},{2,10},{3,11},{4,12},{5,13},{6,14},{7,15},{8,0},{9,1},... | collective-permute-start | bytes 12296 | tf_op jit(solution)/shard_map/ppermute | solution.py:780
  7.0 1.4 %shard_map.53 = (f32[41,24,128]{2,1,0:T(8,128)S(1)}, f32[41,24,128]{2,1,0:T(8,128)S(1)}) custom-call(), custom_call_target="tpu_custom_call" | custom-call | bytes 3500000 | tf_op jit(solution)/shard_map/pallas_call | solution.py:788
  8.5 1.0 %collective-permute-done.2.across = f32[8,128]{1,0:T(8,128)S(1)} collective-permute-done((f32[8,128]{1,0:T(8,128)S(1)}, f32[8,128]{1,0:T(8,128)S(1)}, u32[]{:S(2)}, u32[]{:S(2)}) %collective-permute-start.2) | collective-permute-done | bytes 4128 | tf_op jit(solution)/shard_map/ppermute | solution.py:780
  9.5 0.1 shard_map.55
  9.6 1.2 %collective-permute-start.3 = (f32[168,128]{1,0:T(8,128)S(1)}, f32[168,128]{1,0:T(8,128)S(1)}, u32[]{:S(2)}, u32[]{:S(2)}) collective-permute-start(f32[168,128]{1,0:T(8,128)S(1)} %get-tuple-element.49), channel_id=1, source_target_pairs={{0,1},{1,2},{2,3},{3,0},{4,5},{5,6},{6,7},{7,4},{8,9},{9,10},{10,1... | collective-permute-start | bytes 258056 | tf_op jit(solution)/shard_map/ppermute | solution.py:793
  10.8 1.5 %collective-permute-start.4 = (f32[168,128]{1,0:T(8,128)S(1)}, f32[168,128]{1,0:T(8,128)S(1)}, u32[]{:S(2)}, u32[]{:S(2)}) collective-permute-start(f32[168,128]{1,0:T(8,128)S(1)} %get-tuple-element.50), channel_id=1, source_target_pairs={{0,3},{1,0},{2,1},{3,2},{4,7},{5,4},{6,5},{7,6},{8,11},{9,8},{10,9... | collective-permute-start | bytes 258056 | tf_op jit(solution)/shard_map/ppermute | solution.py:794
  12.3 1.5 %collective-permute-start.5 = (f32[8,128]{1,0:T(8,128)S(1)}, f32[8,128]{1,0:T(8,128)S(1)}, u32[]{:S(2)}, u32[]{:S(2)}) collective-permute-start(f32[8,128]{1,0:T(8,128)S(1)} %shard_map.54.total), channel_id=1, source_target_pairs={{0,2},{1,3},{2,0},{3,1},{4,6},{5,7},{6,4},{7,5},{8,10},{9,11},{10,... | collective-permute-start | bytes 12296 | tf_op jit(solution)/shard_map/ppermute | solution.py:791
  13.8 2.5 %collective-permute-done.5.across = f32[8,128]{1,0:T(8,128)S(1)} collective-permute-done((f32[8,128]{1,0:T(8,128)S(1)}, f32[8,128]{1,0:T(8,128)S(1)}, u32[]{:S(2)}, u32[]{:S(2)}) %collective-permute-start.5) | collective-permute-done | bytes 4128 | tf_op jit(solution)/shard_map/ppermute | solution.py:791
  16.5 3.8 %collective-permute-start.7 = (f32[488,128]{1,0:T(8,128)S(1)}, f32[488,128]{1,0:T(8,128)S(1)}, u32[]{:S(2)}, u32[]{:S(2)}) collective-permute-start(f32[488,128]{1,0:T(8,128)S(1)} %get-tuple-element.58), channel_id=1, source_target_pairs={{0,112},{16,0},{32,16},{48,32},{64,48},{80,64},{96,80},{112,96},{1... | collective-permute-start | bytes 749576 | tf_op jit(solution)/shard_map/ppermute | solution.py:802
  20.3 1.6 %collective-permute-start.6 = (f32[488,128]{1,0:T(8,128)S(1)}, f32[488,128]{1,0:T(8,128)S(1)}, u32[]{:S(2)}, u32[]{:S(2)}) collective-permute-start(f32[488,128]{1,0:T(8,128)S(1)} %get-tuple-element.52), channel_id=1, source_target_pairs={{0,16},{16,32},{32,48},{48,64},{64,80},{80,96},{96,112},{112,0},{1... | collective-permute-start | bytes 749576 | tf_op jit(solution)/shard_map/ppermute | solution.py:801
  21.9 1.6 %collective-permute-start.8 = (f32[72,128]{1,0:T(8,128)S(1)}, f32[72,128]{1,0:T(8,128)S(1)}, u32[]{:S(2)}, u32[]{:S(2)}) collective-permute-start(f32[72,128]{1,0:T(8,128)S(1)} %get-tuple-element.67), channel_id=1, source_target_pairs={{0,32},{16,48},{32,64},{48,80},{64,96},{80,112},{96,0},{112,16},{1... | collective-permute-start | bytes 110600 | tf_op jit(solution)/shard_map/ppermute | solution.py:803
  23.5 1.0 %collective-permute-start.9 = (f32[72,128]{1,0:T(8,128)S(1)}, f32[72,128]{1,0:T(8,128)S(1)}, u32[]{:S(2)}, u32[]{:S(2)}) collective-permute-start(f32[72,128]{1,0:T(8,128)S(1)} %get-tuple-element.68), channel_id=1, source_target_pairs={{0,96},{16,112},{32,0},{48,16},{64,32},{80,48},{96,64},{112,80},{1... | collective-permute-start | bytes 110600 | tf_op jit(solution)/shard_map/ppermute | solution.py:804
  24.6 0.6 %shard_map.58 = (f32[2,41,8,128]{3,2,1,0:T(8,128)S(1)}, f32[2,26,8,128]{3,2,1,0:T(8,128)S(1)}) custom-call(f32[640,128]{1,0:T(8,128)S(1)} %get-tuple-element.55.ref), custom_call_target="tpu_custom_call" | custom-call | bytes 2800000 | tf_op jit(solution)/shard_map/pallas_call | solution.py:813
  25.2 0.9 %collective-permute-done.7.ref.xp1 = f32[488,128]{1,0:T(8,128)S(1)} collective-permute-done((f32[488,128]{1,0:T(8,128)S(1)}, f32[488,128]{1,0:T(8,128)S(1)}, u32[]{:S(2)}, u32[]{:S(2)}) %collective-permute-start.7) | collective-permute-done | bytes 249888 | tf_op jit(solution)/shard_map/ppermute | solution.py:802
  26.1 0.6 %shard_map.59 = (f32[2,41,8,128]{3,2,1,0:T(8,128)S(1)}, f32[2,26,8,128]{3,2,1,0:T(8,128)S(1)}) custom-call(f32[488,128]{1,0:T(8,128)S(1)} %collective-permute-done.7.ref.xp1), custom_call_target="tpu_custom_call" | custom-call | bytes 2800000 | tf_op jit(solution)/shard_map/pallas_call | solution.py:813
  26.7 0.6 %shard_map.57 = (f32[2,41,8,128]{3,2,1,0:T(8,128)S(1)}, f32[2,26,8,128]{3,2,1,0:T(8,128)S(1)}) custom-call(f32[488,128]{1,0:T(8,128)S(1)} %collective-permute-done.6.ref.xm1), custom_call_target="tpu_custom_call" | custom-call | bytes 2800000 | tf_op jit(solution)/shard_map/pallas_call | solution.py:813
  27.3 1.2 %collective-permute-done.8.xm2 = f32[72,128]{1,0:T(8,128)S(1)} collective-permute-done((f32[72,128]{1,0:T(8,128)S(1)}, f32[72,128]{1,0:T(8,128)S(1)}, u32[]{:S(2)}, u32[]{:S(2)}) %collective-permute-start.8) | collective-permute-done | bytes 36896 | tf_op jit(solution)/shard_map/ppermute | solution.py:803
  28.5 2.3 %collective-permute-start.10 = (f32[8,128]{1,0:T(8,128)S(1)}, f32[8,128]{1,0:T(8,128)S(1)}, u32[]{:S(2)}, u32[]{:S(2)}) collective-permute-start(f32[8,128]{1,0:T(8,128)S(1)} %get-tuple-element.75), channel_id=1, source_target_pairs={{0,48},{16,96},{32,80},{48,0},{64,112},{80,32},{96,16},{112,64},{1... | collective-permute-start | bytes 12296 | tf_op jit(solution)/shard_map/ppermute | solution.py:817
  30.8 2.8 %shard_map.60 = (f32[41,24,128]{2,1,0:T(8,128)S(1)}, f32[41,24,128]{2,1,0:T(8,128)S(1)}) custom-call(f32[2,41,8,128]{3,2,1,0:T(8,128)S(1)} %get-tuple-element.61.t1, f32[2,41,8,128]{3,2,1,0:T(8,128)S(1)} %get-tuple-element.62.t2, f32[2,41,8,128]{3,2,1,0:T(8,128)S(1)} %get-tuple-element.63.t3, f32[2,26,8,128]{3,2,1,0:T(8,128)S(1)} %get-tuple-element.64.f1, ...), custom_call_target="tpu_custom_call" | custom-call | bytes 10500000 | tf_op jit(solution)/shard_map/pallas_call | solution.py:819
  33.7 2.0 %shard_map.62 = (f32[4,16,256]{2,1,0:T(8,128)}, f32[4,16,256]{2,1,0:T(8,128)}) custom-call(s32[8,128]{1,0:T(8,128)S(1)} %get-tuple-element.41.order, f32[2,41,8,128]{3,2,1,0:T(8,128)S(1)} %get-tuple-element.61.t1, f32[2,41,8,128]{3,2,1,0:T(8,128)S(1)} %get-tuple-element.62.t2, f32[2,41,8,128]{3,2,1,0:T(8,128)S(1)} %get-tuple-element.63.t3, ...), custom_call_target="tpu_custom_call" | custom-call | bytes 350000 | tf_op jit(solution)/shard_map/pallas_call | solution.py:837
  (13 shorter events, 0.2 us)
Async XLA Ops:
  0.6 0.9 %copy-start = (s32[512,3]{0,1:T(4,128)S(1)}, s32[512,3]{0,1:T(4,128)}, u32[]{:S(2)}) copy-start(s32[512,3]{0,1:T(4,128)} %param.5) | copy-start | bytes 18436
  1.8 7.6 %collective-permute-start = (f32[88,128]{1,0:T(8,128)S(1)}, f32[88,128]{1,0:T(8,128)S(1)}, u32[]{:S(2)}, u32[]{:S(2)}) collective-permute-start(f32[88,128]{1,0:T(8,128)S(1)} %get-tuple-element.44), channel_id=1, source_target_pairs={{0,4},{1,5},{2,6},{3,7},{4,8},{5,9},{6,10},{7,11},{8,12},{9,13},{1... | collective-permute-start | bytes 135176 | tf_op jit(solution)/shard_map/ppermute | solution.py:782
  4.0 5.5 %collective-permute-start.1 = (f32[88,128]{1,0:T(8,128)S(1)}, f32[88,128]{1,0:T(8,128)S(1)}, u32[]{:S(2)}, u32[]{:S(2)}) collective-permute-start(f32[88,128]{1,0:T(8,128)S(1)} %get-tuple-element.45), channel_id=1, source_target_pairs={{0,12},{1,13},{2,14},{3,15},{4,0},{5,1},{6,2},{7,3},{8,4},{9,5},{1... | collective-permute-start | bytes 135176 | tf_op jit(solution)/shard_map/ppermute | solution.py:783
  5.5 4.0 %collective-permute-start.2 = (f32[8,128]{1,0:T(8,128)S(1)}, f32[8,128]{1,0:T(8,128)S(1)}, u32[]{:S(2)}, u32[]{:S(2)}) collective-permute-start(f32[8,128]{1,0:T(8,128)S(1)} %get-tuple-element.48.sums), channel_id=1, source_target_pairs={{0,8},{1,9},{2,10},{3,11},{4,12},{5,13},{6,14},{7,15},{8,0},{9,1},... | collective-permute-start | bytes 12296 | tf_op jit(solution)/shard_map/ppermute | solution.py:780
  9.6 6.8 %collective-permute-start.3 = (f32[168,128]{1,0:T(8,128)S(1)}, f32[168,128]{1,0:T(8,128)S(1)}, u32[]{:S(2)}, u32[]{:S(2)}) collective-permute-start(f32[168,128]{1,0:T(8,128)S(1)} %get-tuple-element.49), channel_id=1, source_target_pairs={{0,1},{1,2},{2,3},{3,0},{4,5},{5,6},{6,7},{7,4},{8,9},{9,10},{10,1... | collective-permute-start | bytes 258056 | tf_op jit(solution)/shard_map/ppermute | solution.py:793
  10.8 5.5 %collective-permute-start.4 = (f32[168,128]{1,0:T(8,128)S(1)}, f32[168,128]{1,0:T(8,128)S(1)}, u32[]{:S(2)}, u32[]{:S(2)}) collective-permute-start(f32[168,128]{1,0:T(8,128)S(1)} %get-tuple-element.50), channel_id=1, source_target_pairs={{0,3},{1,0},{2,1},{3,2},{4,7},{5,4},{6,5},{7,6},{8,11},{9,8},{10,9... | collective-permute-start | bytes 258056 | tf_op jit(solution)/shard_map/ppermute | solution.py:794
  12.3 4.1 %collective-permute-start.5 = (f32[8,128]{1,0:T(8,128)S(1)}, f32[8,128]{1,0:T(8,128)S(1)}, u32[]{:S(2)}, u32[]{:S(2)}) collective-permute-start(f32[8,128]{1,0:T(8,128)S(1)} %shard_map.54.total), channel_id=1, source_target_pairs={{0,2},{1,3},{2,0},{3,1},{4,6},{5,7},{6,4},{7,5},{8,10},{9,11},{10,... | collective-permute-start | bytes 12296 | tf_op jit(solution)/shard_map/ppermute | solution.py:791
  16.5 9.6 %collective-permute-start.7 = (f32[488,128]{1,0:T(8,128)S(1)}, f32[488,128]{1,0:T(8,128)S(1)}, u32[]{:S(2)}, u32[]{:S(2)}) collective-permute-start(f32[488,128]{1,0:T(8,128)S(1)} %get-tuple-element.58), channel_id=1, source_target_pairs={{0,112},{16,0},{32,16},{48,32},{64,48},{80,64},{96,80},{112,96},{1... | collective-permute-start | bytes 749576 | tf_op jit(solution)/shard_map/ppermute | solution.py:802
  20.3 6.4 %collective-permute-start.6 = (f32[488,128]{1,0:T(8,128)S(1)}, f32[488,128]{1,0:T(8,128)S(1)}, u32[]{:S(2)}, u32[]{:S(2)}) collective-permute-start(f32[488,128]{1,0:T(8,128)S(1)} %get-tuple-element.52), channel_id=1, source_target_pairs={{0,16},{16,32},{32,48},{48,64},{64,80},{80,96},{96,112},{112,0},{1... | collective-permute-start | bytes 749576 | tf_op jit(solution)/shard_map/ppermute | solution.py:801
  21.9 6.6 %collective-permute-start.8 = (f32[72,128]{1,0:T(8,128)S(1)}, f32[72,128]{1,0:T(8,128)S(1)}, u32[]{:S(2)}, u32[]{:S(2)}) collective-permute-start(f32[72,128]{1,0:T(8,128)S(1)} %get-tuple-element.67), channel_id=1, source_target_pairs={{0,32},{16,48},{32,64},{48,80},{64,96},{80,112},{96,0},{112,16},{1... | collective-permute-start | bytes 110600 | tf_op jit(solution)/shard_map/ppermute | solution.py:803
  23.5 5.0 %collective-permute-start.9 = (f32[72,128]{1,0:T(8,128)S(1)}, f32[72,128]{1,0:T(8,128)S(1)}, u32[]{:S(2)}, u32[]{:S(2)}) collective-permute-start(f32[72,128]{1,0:T(8,128)S(1)} %get-tuple-element.68), channel_id=1, source_target_pairs={{0,96},{16,112},{32,0},{48,16},{64,32},{80,48},{96,64},{112,80},{1... | collective-permute-start | bytes 110600 | tf_op jit(solution)/shard_map/ppermute | solution.py:804
  28.5 5.1 %collective-permute-start.10 = (f32[8,128]{1,0:T(8,128)S(1)}, f32[8,128]{1,0:T(8,128)S(1)}, u32[]{:S(2)}, u32[]{:S(2)}) collective-permute-start(f32[8,128]{1,0:T(8,128)S(1)} %get-tuple-element.75), channel_id=1, source_target_pairs={{0,48},{16,96},{32,80},{48,0},{64,112},{80,32},{96,16},{112,64},{1... | collective-permute-start | bytes 12296 | tf_op jit(solution)/shard_map/ppermute | solution.py:817

commit v3 on v2

--- a/solution.py
+++ b/solution.py
@@ -547,24 +547,29 @@
         if i >= 10:
             ends = beyond(i - 10) * (beyond_outside if i < 12 else beyond_mask)
         cs[i] = c
-        _store(c0, i, c + _sweep(c, near, lane, ends) * masks[i >= 12], COARSE - 1)
+        turns = _roll(c, 2, 1), _roll(c, -2, 1)
+        _store(c0, i, c + _sweep(c, near, turns, lane, ends) * masks[i >= 12], COARSE - 1)
     _sweep_rows(c0, c1, cs, 5, masks)
     _sweep_rows(c1, c0, cs, 6, masks)
 
 
-def _sweep(c, near, lane, ends):
-    before, after = _roll(c, 2, 1), _roll(c, -2, 1)
+def _sweep(c, near, turns, lane, ends):
+    before, after = turns
     if ends is not None:
         before = jnp.where(lane < 2, ends, before)
         after = jnp.where(lane >= 62, ends, after)
     return 0.2 * c + W * (near + (before + after))
 
 
-def _sweep_rows(src, dst, cs, first, masks):
-    for i in range(first, COARSE):
-        c = src[i]
-        near = _roll(c, 1, 0) + _roll(c, -1, 0) + (src[i - 1] + src[i + 1])
-        _store(dst, i, cs[i] + _sweep(c, near, None, None) * masks[i >= 12], COARSE - 1)
+def _sweep_rows(src, dst, cs, first, masks, batch=4):
+    for start in range(first, COARSE, batch):
+        rows = range(start, min(start + batch, COARSE))
+        turned = [
+            (_roll(src[i], 1, 0), _roll(src[i], -1, 0), _roll(src[i], 2, 1), _roll(src[i], -2, 1)) for i in rows
+        ]
+        for i, (low, high, *turns) in zip(rows, turned):
+            near = (low + high) + (src[i - 1] + src[i + 1])
+            _store(dst, i, cs[i] + _sweep(src[i], near, turns, None, None) * masks[i >= 12], COARSE - 1)
 
 
 def _restrict(fields, rows, near, centre, more, first, count, store, patch, size):
@@ -666,8 +671,9 @@
     fetch = pltpu.make_async_copy(order, place, sem.at[0])
     fetch.start()
     totals = part[...] + across[...]
-    mean1 = jnp.sum(totals[0:1]) * (1.0 / CELLS)
-    mean2 = jnp.sum(totals[1:2]) * (1.0 / CELLS)
+    means = jnp.sum(totals, axis=1, keepdims=True) * (1.0 / CELLS)
+    mean1 = jnp.broadcast_to(means[0:1], (24, LANES))
+    mean2 = jnp.broadcast_to(means[1:2], (24, LANES))
     step_masks = _step_masks(g, yb, zb)
     masks = step_masks[0]
 

time: 35.8 us -> 35.8 us (level)
  no operation moved by 1% of the time
where the time goes in v3:
time: 35.8 us; the launch traced here: 35.6 us
  starting transfers between devices  19.8 us (55%)
  Pallas kernels  9.41 us (26%)
  waiting for transfers between devices  5.67 us (16%)
  between operations  0.72 us (2%)
    ppermute x1, starting transfers between devices, _body(): xp1 = lax.ppermute(down, 'grp', _x_shift(-1))  3.78 us
    pallas_call x1, Pallas kernels, _body(): _call(_coarse_kernel, [VMEM] * 8, [fine, fine], [inner, inner, pltpu.VMEM...  2.84 us
    ppermute x1, waiting for transfers between devices, _body(): zacross = lax.ppermute(total, 'dev', _z_shift(2))  2.53 us
    ppermute x1, starting transfers between devices, _body(): lax.ppermute(send, 'grp', [(x, (x + 3 - 6 * (x % 2)) % 8) for x in range(...  2.26 us
    ppermute x1, starting transfers between devices, _body(): below = lax.ppermute(up, 'dev', _y_shift(1))  2.14 us
    pallas_call x1, Pallas kernels, _body(): _call(_cycle_kernel, [VMEM] * 10, [_shape(4, 16, 256), _shape(4, 16, 256)...  1.96 us
    pallas_call x3, Pallas kernels, _body(): bricks.append(_call(kernel, [VMEM], outs, us=0.8)(ref))  1.77 us
    ppermute x1, starting transfers between devices, _body(): xm2 = lax.ppermute(high, 'grp', _x_shift(2))  1.64 us
  transfers between devices with their start and end apart: 11, of which 4 were waited for; matrix products, arithmetic and copies ran while one was open for 0% of the time, Pallas kernels for 17%

profile of v3, /device:TPU:1, one launch (start us, length us, event | category | flops | bytes accessed | tf_op | source)
XLA Modules:
  0.0 35.6 jit_solution(15726718765631723630)
XLA Ops:
  0.6 0.9 %shard_map.50 = (f32[4,16,256]{2,1,0:T(8,128)S(1)}, f32[8,16,128]{2,1,0:T(8,128)S(1)}) custom-call(f32[4,16,256]{2,1,0:T(8,128)} %div.1, f32[27,8,16,128]{3,2,1,0:T(8,128)} %constant.2.clone.w2), custom_call_target="tpu_custom_call" | custom-call | bytes 3500000 | tf_op jit(solution)/shard_map/pallas_call | solution.py:772
  1.6 0.2 shard_map.51
  1.8 2.1 %collective-permute-start = (f32[88,128]{1,0:T(8,128)S(1)}, f32[88,128]{1,0:T(8,128)S(1)}, u32[]{:S(2)}, u32[]{:S(2)}) collective-permute-start(f32[88,128]{1,0:T(8,128)S(1)} %get-tuple-element.44), channel_id=1, source_target_pairs={{0,4},{1,5},{2,6},{3,7},{4,8},{5,9},{6,10},{7,11},{8,12},{9,13},{1... | collective-permute-start | bytes 135176 | tf_op jit(solution)/shard_map/ppermute | solution.py:788
  4.0 1.5 %collective-permute-start.1 = (f32[88,128]{1,0:T(8,128)S(1)}, f32[88,128]{1,0:T(8,128)S(1)}, u32[]{:S(2)}, u32[]{:S(2)}) collective-permute-start(f32[88,128]{1,0:T(8,128)S(1)} %get-tuple-element.45), channel_id=1, source_target_pairs={{0,12},{1,13},{2,14},{3,15},{4,0},{5,1},{6,2},{7,3},{8,4},{9,5},{1... | collective-permute-start | bytes 135176 | tf_op jit(solution)/shard_map/ppermute | solution.py:789
  5.5 1.6 %collective-permute-start.2 = (f32[8,128]{1,0:T(8,128)S(1)}, f32[8,128]{1,0:T(8,128)S(1)}, u32[]{:S(2)}, u32[]{:S(2)}) collective-permute-start(f32[8,128]{1,0:T(8,128)S(1)} %get-tuple-element.48.sums), channel_id=1, source_target_pairs={{0,8},{1,9},{2,10},{3,11},{4,12},{5,13},{6,14},{7,15},{8,0},{9,1},... | collective-permute-start | bytes 12296 | tf_op jit(solution)/shard_map/ppermute | solution.py:786
  7.0 1.4 %shard_map.53 = (f32[41,24,128]{2,1,0:T(8,128)S(1)}, f32[41,24,128]{2,1,0:T(8,128)S(1)}) custom-call(), custom_call_target="tpu_custom_call" | custom-call | bytes 3500000 | tf_op jit(solution)/shard_map/pallas_call | solution.py:794
  8.5 1.0 %collective-permute-done.2.across = f32[8,128]{1,0:T(8,128)S(1)} collective-permute-done((f32[8,128]{1,0:T(8,128)S(1)}, f32[8,128]{1,0:T(8,128)S(1)}, u32[]{:S(2)}, u32[]{:S(2)}) %collective-permute-start.2) | collective-permute-done | bytes 4128 | tf_op jit(solution)/shard_map/ppermute | solution.py:786
  9.5 0.1 shard_map.55
  9.6 1.2 %collective-permute-start.3 = (f32[168,128]{1,0:T(8,128)S(1)}, f32[168,128]{1,0:T(8,128)S(1)}, u32[]{:S(2)}, u32[]{:S(2)}) collective-permute-start(f32[168,128]{1,0:T(8,128)S(1)} %get-tuple-element.49), channel_id=1, source_target_pairs={{0,1},{1,2},{2,3},{3,0},{4,5},{5,6},{6,7},{7,4},{8,9},{9,10},{10,1... | collective-permute-start | bytes 258056 | tf_op jit(solution)/shard_map/ppermute | solution.py:799
  10.8 1.5 %collective-permute-start.4 = (f32[168,128]{1,0:T(8,128)S(1)}, f32[168,128]{1,0:T(8,128)S(1)}, u32[]{:S(2)}, u32[]{:S(2)}) collective-permute-start(f32[168,128]{1,0:T(8,128)S(1)} %get-tuple-element.50), channel_id=1, source_target_pairs={{0,3},{1,0},{2,1},{3,2},{4,7},{5,4},{6,5},{7,6},{8,11},{9,8},{10,9... | collective-permute-start | bytes 258056 | tf_op jit(solution)/shard_map/ppermute | solution.py:800
  12.3 1.5 %collective-permute-start.5 = (f32[8,128]{1,0:T(8,128)S(1)}, f32[8,128]{1,0:T(8,128)S(1)}, u32[]{:S(2)}, u32[]{:S(2)}) collective-permute-start(f32[8,128]{1,0:T(8,128)S(1)} %shard_map.54.total), channel_id=1, source_target_pairs={{0,2},{1,3},{2,0},{3,1},{4,6},{5,7},{6,4},{7,5},{8,10},{9,11},{10,... | collective-permute-start | bytes 12296 | tf_op jit(solution)/shard_map/ppermute | solution.py:797
  13.8 2.5 %collective-permute-done.5.across = f32[8,128]{1,0:T(8,128)S(1)} collective-permute-done((f32[8,128]{1,0:T(8,128)S(1)}, f32[8,128]{1,0:T(8,128)S(1)}, u32[]{:S(2)}, u32[]{:S(2)}) %collective-permute-start.5) | collective-permute-done | bytes 4128 | tf_op jit(solution)/shard_map/ppermute | solution.py:797
  16.5 3.8 %collective-permute-start.7 = (f32[488,128]{1,0:T(8,128)S(1)}, f32[488,128]{1,0:T(8,128)S(1)}, u32[]{:S(2)}, u32[]{:S(2)}) collective-permute-start(f32[488,128]{1,0:T(8,128)S(1)} %get-tuple-element.58), channel_id=1, source_target_pairs={{0,112},{16,0},{32,16},{48,32},{64,48},{80,64},{96,80},{112,96},{1... | collective-permute-start | bytes 749576 | tf_op jit(solution)/shard_map/ppermute | solution.py:808
  20.3 1.6 %collective-permute-start.6 = (f32[488,128]{1,0:T(8,128)S(1)}, f32[488,128]{1,0:T(8,128)S(1)}, u32[]{:S(2)}, u32[]{:S(2)}) collective-permute-start(f32[488,128]{1,0:T(8,128)S(1)} %get-tuple-element.52), channel_id=1, source_target_pairs={{0,16},{16,32},{32,48},{48,64},{64,80},{80,96},{96,112},{112,0},{1... | collective-permute-start | bytes 749576 | tf_op jit(solution)/shard_map/ppermute | solution.py:807
  21.9 1.6 %collective-permute-start.8 = (f32[72,128]{1,0:T(8,128)S(1)}, f32[72,128]{1,0:T(8,128)S(1)}, u32[]{:S(2)}, u32[]{:S(2)}) collective-permute-start(f32[72,128]{1,0:T(8,128)S(1)} %get-tuple-element.67), channel_id=1, source_target_pairs={{0,32},{16,48},{32,64},{48,80},{64,96},{80,112},{96,0},{112,16},{1... | collective-permute-start | bytes 110600 | tf_op jit(solution)/shard_map/ppermute | solution.py:809
  23.5 1.0 %collective-permute-start.9 = (f32[72,128]{1,0:T(8,128)S(1)}, f32[72,128]{1,0:T(8,128)S(1)}, u32[]{:S(2)}, u32[]{:S(2)}) collective-permute-start(f32[72,128]{1,0:T(8,128)S(1)} %get-tuple-element.68), channel_id=1, source_target_pairs={{0,96},{16,112},{32,0},{48,16},{64,32},{80,48},{96,64},{112,80},{1... | collective-permute-start | bytes 110600 | tf_op jit(solution)/shard_map/ppermute | solution.py:810
  24.6 0.6 %shard_map.58 = (f32[2,41,8,128]{3,2,1,0:T(8,128)S(1)}, f32[2,26,8,128]{3,2,1,0:T(8,128)S(1)}) custom-call(f32[640,128]{1,0:T(8,128)S(1)} %get-tuple-element.55.ref), custom_call_target="tpu_custom_call" | custom-call | bytes 2800000 | tf_op jit(solution)/shard_map/pallas_call | solution.py:819
  25.2 0.9 %collective-permute-done.7.ref.xp1 = f32[488,128]{1,0:T(8,128)S(1)} collective-permute-done((f32[488,128]{1,0:T(8,128)S(1)}, f32[488,128]{1,0:T(8,128)S(1)}, u32[]{:S(2)}, u32[]{:S(2)}) %collective-permute-start.7) | collective-permute-done | bytes 249888 | tf_op jit(solution)/shard_map/ppermute | solution.py:808
  26.1 0.6 %shard_map.59 = (f32[2,41,8,128]{3,2,1,0:T(8,128)S(1)}, f32[2,26,8,128]{3,2,1,0:T(8,128)S(1)}) custom-call(f32[488,128]{1,0:T(8,128)S(1)} %collective-permute-done.7.ref.xp1), custom_call_target="tpu_custom_call" | custom-call | bytes 2800000 | tf_op jit(solution)/shard_map/pallas_call | solution.py:819
  26.7 0.6 %shard_map.57 = (f32[2,41,8,128]{3,2,1,0:T(8,128)S(1)}, f32[2,26,8,128]{3,2,1,0:T(8,128)S(1)}) custom-call(f32[488,128]{1,0:T(8,128)S(1)} %collective-permute-done.6.ref.xm1), custom_call_target="tpu_custom_call" | custom-call | bytes 2800000 | tf_op jit(solution)/shard_map/pallas_call | solution.py:819
  27.3 1.2 %collective-permute-done.8.xm2 = f32[72,128]{1,0:T(8,128)S(1)} collective-permute-done((f32[72,128]{1,0:T(8,128)S(1)}, f32[72,128]{1,0:T(8,128)S(1)}, u32[]{:S(2)}, u32[]{:S(2)}) %collective-permute-start.8) | collective-permute-done | bytes 36896 | tf_op jit(solution)/shard_map/ppermute | solution.py:809
  28.5 2.3 %collective-permute-start.10 = (f32[8,128]{1,0:T(8,128)S(1)}, f32[8,128]{1,0:T(8,128)S(1)}, u32[]{:S(2)}, u32[]{:S(2)}) collective-permute-start(f32[8,128]{1,0:T(8,128)S(1)} %get-tuple-element.75), channel_id=1, source_target_pairs={{0,48},{16,96},{32,80},{48,0},{64,112},{80,32},{96,16},{112,64},{1... | collective-permute-start | bytes 12296 | tf_op jit(solution)/shard_map/ppermute | solution.py:823
  30.8 2.8 %shard_map.60 = (f32[41,24,128]{2,1,0:T(8,128)S(1)}, f32[41,24,128]{2,1,0:T(8,128)S(1)}) custom-call(f32[2,41,8,128]{3,2,1,0:T(8,128)S(1)} %get-tuple-element.61.t1, f32[2,41,8,128]{3,2,1,0:T(8,128)S(1)} %get-tuple-element.62.t2, f32[2,41,8,128]{3,2,1,0:T(8,128)S(1)} %get-tuple-element.63.t3, f32[2,26,8,128]{3,2,1,0:T(8,128)S(1)} %get-tuple-element.64.f1, ...), custom_call_target="tpu_custom_call" | custom-call | bytes 10500000 | tf_op jit(solution)/shard_map/pallas_call | solution.py:825
  33.7 2.0 %shard_map.62 = (f32[4,16,256]{2,1,0:T(8,128)}, f32[4,16,256]{2,1,0:T(8,128)}) custom-call(s32[8,128]{1,0:T(8,128)S(1)} %get-tuple-element.41.order, f32[2,41,8,128]{3,2,1,0:T(8,128)S(1)} %get-tuple-element.61.t1, f32[2,41,8,128]{3,2,1,0:T(8,128)S(1)} %get-tuple-element.62.t2, f32[2,41,8,128]{3,2,1,0:T(8,128)S(1)} %get-tuple-element.63.t3, ...), custom_call_target="tpu_custom_call" | custom-call | bytes 350000 | tf_op jit(solution)/shard_map/pallas_call | solution.py:843
  (13 shorter events, 0.2 us)
Async XLA Ops:
  0.6 0.9 %copy-start = (s32[512,3]{0,1:T(4,128)S(1)}, s32[512,3]{0,1:T(4,128)}, u32[]{:S(2)}) copy-start(s32[512,3]{0,1:T(4,128)} %param.5) | copy-start | bytes 18436
  1.8 7.6 %collective-permute-start = (f32[88,128]{1,0:T(8,128)S(1)}, f32[88,128]{1,0:T(8,128)S(1)}, u32[]{:S(2)}, u32[]{:S(2)}) collective-permute-start(f32[88,128]{1,0:T(8,128)S(1)} %get-tuple-element.44), channel_id=1, source_target_pairs={{0,4},{1,5},{2,6},{3,7},{4,8},{5,9},{6,10},{7,11},{8,12},{9,13},{1... | collective-permute-start | bytes 135176 | tf_op jit(solution)/shard_map/ppermute | solution.py:788
  4.0 5.5 %collective-permute-start.1 = (f32[88,128]{1,0:T(8,128)S(1)}, f32[88,128]{1,0:T(8,128)S(1)}, u32[]{:S(2)}, u32[]{:S(2)}) collective-permute-start(f32[88,128]{1,0:T(8,128)S(1)} %get-tuple-element.45), channel_id=1, source_target_pairs={{0,12},{1,13},{2,14},{3,15},{4,0},{5,1},{6,2},{7,3},{8,4},{9,5},{1... | collective-permute-start | bytes 135176 | tf_op jit(solution)/shard_map/ppermute | solution.py:789
  5.5 4.0 %collective-permute-start.2 = (f32[8,128]{1,0:T(8,128)S(1)}, f32[8,128]{1,0:T(8,128)S(1)}, u32[]{:S(2)}, u32[]{:S(2)}) collective-permute-start(f32[8,128]{1,0:T(8,128)S(1)} %get-tuple-element.48.sums), channel_id=1, source_target_pairs={{0,8},{1,9},{2,10},{3,11},{4,12},{5,13},{6,14},{7,15},{8,0},{9,1},... | collective-permute-start | bytes 12296 | tf_op jit(solution)/shard_map/ppermute | solution.py:786
  9.6 6.8 %collective-permute-start.3 = (f32[168,128]{1,0:T(8,128)S(1)}, f32[168,128]{1,0:T(8,128)S(1)}, u32[]{:S(2)}, u32[]{:S(2)}) collective-permute-start(f32[168,128]{1,0:T(8,128)S(1)} %get-tuple-element.49), channel_id=1, source_target_pairs={{0,1},{1,2},{2,3},{3,0},{4,5},{5,6},{6,7},{7,4},{8,9},{9,10},{10,1... | collective-permute-start | bytes 258056 | tf_op jit(solution)/shard_map/ppermute | solution.py:799
  10.8 5.5 %collective-permute-start.4 = (f32[168,128]{1,0:T(8,128)S(1)}, f32[168,128]{1,0:T(8,128)S(1)}, u32[]{:S(2)}, u32[]{:S(2)}) collective-permute-start(f32[168,128]{1,0:T(8,128)S(1)} %get-tuple-element.50), channel_id=1, source_target_pairs={{0,3},{1,0},{2,1},{3,2},{4,7},{5,4},{6,5},{7,6},{8,11},{9,8},{10,9... | collective-permute-start | bytes 258056 | tf_op jit(solution)/shard_map/ppermute | solution.py:800
  12.3 4.1 %collective-permute-start.5 = (f32[8,128]{1,0:T(8,128)S(1)}, f32[8,128]{1,0:T(8,128)S(1)}, u32[]{:S(2)}, u32[]{:S(2)}) collective-permute-start(f32[8,128]{1,0:T(8,128)S(1)} %shard_map.54.total), channel_id=1, source_target_pairs={{0,2},{1,3},{2,0},{3,1},{4,6},{5,7},{6,4},{7,5},{8,10},{9,11},{10,... | collective-permute-start | bytes 12296 | tf_op jit(solution)/shard_map/ppermute | solution.py:797
  16.5 9.6 %collective-permute-start.7 = (f32[488,128]{1,0:T(8,128)S(1)}, f32[488,128]{1,0:T(8,128)S(1)}, u32[]{:S(2)}, u32[]{:S(2)}) collective-permute-start(f32[488,128]{1,0:T(8,128)S(1)} %get-tuple-element.58), channel_id=1, source_target_pairs={{0,112},{16,0},{32,16},{48,32},{64,48},{80,64},{96,80},{112,96},{1... | collective-permute-start | bytes 749576 | tf_op jit(solution)/shard_map/ppermute | solution.py:808
  20.3 6.4 %collective-permute-start.6 = (f32[488,128]{1,0:T(8,128)S(1)}, f32[488,128]{1,0:T(8,128)S(1)}, u32[]{:S(2)}, u32[]{:S(2)}) collective-permute-start(f32[488,128]{1,0:T(8,128)S(1)} %get-tuple-element.52), channel_id=1, source_target_pairs={{0,16},{16,32},{32,48},{48,64},{64,80},{80,96},{96,112},{112,0},{1... | collective-permute-start | bytes 749576 | tf_op jit(solution)/shard_map/ppermute | solution.py:807
  21.9 6.6 %collective-permute-start.8 = (f32[72,128]{1,0:T(8,128)S(1)}, f32[72,128]{1,0:T(8,128)S(1)}, u32[]{:S(2)}, u32[]{:S(2)}) collective-permute-start(f32[72,128]{1,0:T(8,128)S(1)} %get-tuple-element.67), channel_id=1, source_target_pairs={{0,32},{16,48},{32,64},{48,80},{64,96},{80,112},{96,0},{112,16},{1... | collective-permute-start | bytes 110600 | tf_op jit(solution)/shard_map/ppermute | solution.py:809
  23.5 5.0 %collective-permute-start.9 = (f32[72,128]{1,0:T(8,128)S(1)}, f32[72,128]{1,0:T(8,128)S(1)}, u32[]{:S(2)}, u32[]{:S(2)}) collective-permute-start(f32[72,128]{1,0:T(8,128)S(1)} %get-tuple-element.68), channel_id=1, source_target_pairs={{0,96},{16,112},{32,0},{48,16},{64,32},{80,48},{96,64},{112,80},{1... | collective-permute-start | bytes 110600 | tf_op jit(solution)/shard_map/ppermute | solution.py:810
  28.5 5.1 %collective-permute-start.10 = (f32[8,128]{1,0:T(8,128)S(1)}, f32[8,128]{1,0:T(8,128)S(1)}, u32[]{:S(2)}, u32[]{:S(2)}) collective-permute-start(f32[8,128]{1,0:T(8,128)S(1)} %get-tuple-element.75), channel_id=1, source_target_pairs={{0,48},{16,96},{32,80},{48,0},{64,112},{80,32},{96,16},{112,64},{1... | collective-permute-start | bytes 12296 | tf_op jit(solution)/shard_map/ppermute | solution.py:823

commit v4 on v3

--- a/solution.py
+++ b/solution.py
@@ -457,7 +457,7 @@
     return lambda i: jnp.concatenate([t[s, i] for t in tiles], axis=0)
 
 
-def _coarse_kernel(t1, t2, t3, f1, f2, f3, xm2, xp2, Ae, Ao, Be, Bo, ahead_of, raw, beyond, cs, c0, c1):
+def _coarse_kernel(t1, t2, t3, f1, f2, f3, xm2, xp2, Ae, Ao, source, Be, Bo, ahead_of, raw, beyond, cs, c0, c1):
     g, yb, zb = _position()
     ring, fold = _ring_mask(g, zb), _fold_mask(yb)
     De, Do = D = [_beside(s, t1, t2, t3) for s in range(2)]
@@ -512,17 +512,26 @@
     _sweep_three(g, yb, zb, lambda i: raw[i], lambda i: beyond[i], cs, c0, c1)
     base = [lambda i, v=v: W * v(i) for v in D]
     step_masks = _step_masks(g, yb, zb)
-    _correct_and_smooth(step_masks, base, D, lambda i: c0[i], Be, Bo, 7, 13, 4)
-    _smooth(step_masks, (lambda i: Be[i], lambda i: Bo[i]), D, Ae, Ao, 15, 25, 9)
-
-
-def _ones_kernel(Te, To, Be, Bo, cs, c0, c1):
+    _correct_and_smooth(step_masks, base, D, lambda i: c0[i], Be, Bo, 7, 13, 13)
+    _smooth(step_masks, (lambda i: Be[i], lambda i: Bo[i]), D, Ae, Ao, 15, 25, 25)
+    pair_of = lambda i: (De(i) + De(i + 1)) + (Do(i) + Do(i + 1))
+    A = (lambda i: Ae[i], lambda i: Ao[i])
+    _restrict(A, 24, 1.0, -5.0, pair_of, 8, 12, lambda i, c: _set(source, i, c), None, 6)
+
+
+def _set(ref, i, v):
+    ref[i] = v
+
+
+def _ones_kernel(Te, To, source, Be, Bo, cs, c0, c1):
     g, yb, zb = _position()
     one = jnp.ones((32, LANES), F32)
     _sweep_three(g, yb, zb, lambda i: one, lambda i: one[8:], cs, c0, c1)
     step_masks = _step_masks(g, yb, zb)
-    _correct_and_smooth(step_masks, None, None, lambda i: c0[i], Be, Bo, 7, 13, 4)
-    _smooth(step_masks, (lambda i: Be[i], lambda i: Bo[i]), None, Te, To, 15, 25, 9)
+    _correct_and_smooth(step_masks, None, None, lambda i: c0[i], Be, Bo, 7, 13, 13)
+    _smooth(step_masks, (lambda i: Be[i], lambda i: Bo[i]), None, Te, To, 15, 25, 25)
+    T = (lambda i: Te[i], lambda i: To[i])
+    _restrict(T, 24, 1.0, -5.0, None, 8, 12, lambda i, c: _set(source, i, c), None, 6)
 
 
 def _sweep_three(g, yb, zb, source, beyond, cs, c0, c1):
@@ -665,7 +674,7 @@
 
 
 def _cycle_kernel(
-    order, t1, t2, t3, Re, Ro, Te, To, part, across, pot, res, Be, Bo, cs, c0, c1, boxes, place, sem
+    order, t1, t2, t3, Re, Ro, raw, Te, To, raw_one, part, across, pot, res, Be, Bo, cs, c0, c1, boxes, place, sem
 ):
     g, yb, zb = _position()
     fetch = pltpu.make_async_copy(order, place, sem.at[0])
@@ -682,15 +691,13 @@
     De, Do = D = [_beside(s, t1, t2, t3) for s in range(2)]
     A = (lambda i: Re[i] - mean1 * Te[i], lambda i: Ro[i] - mean1 * To[i])
 
-    def again(i, c):
-        _store(cs, i, (c - mean2) * (_of_row(masks, i, 12) * BETA), COARSE - 1)
-
-    pair_of = lambda i: (De(i) + De(i + 1)) + (Do(i) + Do(i + 1))
-    _restrict(A, 24, 1.0, -5.0, pair_of, 8, 12, again, None, 6)
+    for i in range(8, COARSE):
+        c = raw[i] - mean1 * raw_one[i] - mean2
+        _store(cs, i, c * (masks[i >= 12] * BETA), COARSE - 1)
     _sweep_rows(cs, c0, cs, 9, masks)
     _sweep_rows(c0, c1, cs, 10, masks)
     _sweep_rows(c1, c0, cs, 11, masks)
-    _correct_and_smooth(step_masks, A, D, all_of(c0), Be, Bo, 11, 9, 5)
+    _correct_and_smooth(step_masks, A, D, all_of(c0), Be, Bo, 11, 9, 9)
 
     fetch.wait()
     box_of = [place[h, 0] for h in range(4)]
@@ -791,7 +798,7 @@
     plane = pltpu.VMEM((COARSE + 1, 24, LANES), F32)
     fine = _shape(FINE + 1, 24, LANES)
     inner = pltpu.VMEM((FINE + 1, 24, LANES), F32)
-    ones = _call(_ones_kernel, [], [fine, fine], [inner, inner, plane, plane, plane], us=1.0)()
+    ones = _call(_ones_kernel, [], [fine, fine, _shape(COARSE, 24, LANES)], [inner, inner, plane, plane, plane], us=1.0)()
     sums, ones = lax.optimization_barrier((sums, ones))
     total = _call(_total_kernel, [VMEM] * 4, [_rows(8)])(sums, below, above, across)[0]
     zacross = lax.ppermute(total, "dev", _z_shift(2))
@@ -825,7 +832,7 @@
     start = _call(
         _coarse_kernel,
         [VMEM] * 8,
-        [fine, fine],
+        [fine, fine, _shape(COARSE, 24, LANES)],
         [
             inner,
             inner,
@@ -842,7 +849,7 @@
     boxes = pltpu.VMEM((16 * BLOCK, LANES), F32)
     pot, res = _call(
         _cycle_kernel,
-        [VMEM] * 10,
+        [VMEM] * 12,
         [_shape(4, 16, 256), _shape(4, 16, 256)],
         [inner, inner, plane, plane, plane, boxes, pltpu.SMEM((8, LANES), jnp.int32), pltpu.SemaphoreType.DMA((1,))],
     )(order, *tiles, *start, *ones, part, xacross)

time: 35.8 us -> 35.5 us (level)
  Pallas kernels: 9.41 us -> 8.95 us
    pallas_call x3, Pallas kernels: 6.22 us -> 5.76 us  [the longest x1 2.87 us: _body(): _call(_coarse_kernel, [VMEM] * 8, [fine, fine, _shape(COARSE, 24, LANES)]...]
where the time goes in v4:
time: 35.5 us; the launch traced here: 35.3 us
  starting transfers between devices  19.8 us (56%)
  Pallas kernels  8.95 us (25%)
  waiting for transfers between devices  5.84 us (16%)
  between operations  0.73 us (2%)
    ppermute x1, starting transfers between devices, _body(): xp1 = lax.ppermute(down, 'grp', _x_shift(-1))  3.78 us
    pallas_call x1, Pallas kernels, _body(): _call(_coarse_kernel, [VMEM] * 8, [fine, fine, _shape(COARSE, 24, LANES)]...  2.87 us
    ppermute x1, waiting for transfers between devices, _body(): zacross = lax.ppermute(total, 'dev', _z_shift(2))  2.53 us
    ppermute x1, starting transfers between devices, _body(): lax.ppermute(send, 'grp', [(x, (x + 3 - 6 * (x % 2)) % 8) for x in range(...  2.26 us
    ppermute x1, starting transfers between devices, _body(): below = lax.ppermute(up, 'dev', _y_shift(1))  2.14 us
    pallas_call x3, Pallas kernels, _body(): bricks.append(_call(kernel, [VMEM], outs, us=0.8)(ref))  1.77 us
    ppermute x1, starting transfers between devices, _body(): xm2 = lax.ppermute(high, 'grp', _x_shift(2))  1.64 us
    pallas_call x1, Pallas kernels, _body(): _call(_cycle_kernel, [VMEM] * 12, [_shape(4, 16, 256), _shape(4, 16, 256)...  1.64 us
  transfers between devices with their start and end apart: 11, of which 4 were waited for; matrix products, arithmetic and copies ran while one was open for 0% of the time, Pallas kernels for 17%

profile of v4, /device:TPU:1, one launch (start us, length us, event | category | flops | bytes accessed | tf_op | source)
XLA Modules:
  0.0 35.3 jit_solution(11584058697921029518)
XLA Ops:
  0.6 0.9 %shard_map.50 = (f32[4,16,256]{2,1,0:T(8,128)S(1)}, f32[8,16,128]{2,1,0:T(8,128)S(1)}) custom-call(f32[4,16,256]{2,1,0:T(8,128)} %div.1, f32[27,8,16,128]{3,2,1,0:T(8,128)} %constant.2.clone.w2), custom_call_target="tpu_custom_call" | custom-call | bytes 3500000 | tf_op jit(solution)/shard_map/pallas_call | solution.py:779
  1.6 0.2 shard_map.51
  1.8 2.1 %collective-permute-start = (f32[88,128]{1,0:T(8,128)S(1)}, f32[88,128]{1,0:T(8,128)S(1)}, u32[]{:S(2)}, u32[]{:S(2)}) collective-permute-start(f32[88,128]{1,0:T(8,128)S(1)} %get-tuple-element.47), channel_id=1, source_target_pairs={{0,4},{1,5},{2,6},{3,7},{4,8},{5,9},{6,10},{7,11},{8,12},{9,13},{1... | collective-permute-start | bytes 135176 | tf_op jit(solution)/shard_map/ppermute | solution.py:795
  4.0 1.5 %collective-permute-start.1 = (f32[88,128]{1,0:T(8,128)S(1)}, f32[88,128]{1,0:T(8,128)S(1)}, u32[]{:S(2)}, u32[]{:S(2)}) collective-permute-start(f32[88,128]{1,0:T(8,128)S(1)} %get-tuple-element.48), channel_id=1, source_target_pairs={{0,12},{1,13},{2,14},{3,15},{4,0},{5,1},{6,2},{7,3},{8,4},{9,5},{1... | collective-permute-start | bytes 135176 | tf_op jit(solution)/shard_map/ppermute | solution.py:796
  5.5 1.6 %collective-permute-start.2 = (f32[8,128]{1,0:T(8,128)S(1)}, f32[8,128]{1,0:T(8,128)S(1)}, u32[]{:S(2)}, u32[]{:S(2)}) collective-permute-start(f32[8,128]{1,0:T(8,128)S(1)} %get-tuple-element.52.sums), channel_id=1, source_target_pairs={{0,8},{1,9},{2,10},{3,11},{4,12},{5,13},{6,14},{7,15},{8,0},{9,1},... | collective-permute-start | bytes 12296 | tf_op jit(solution)/shard_map/ppermute | solution.py:793
  7.0 1.2 %shard_map.53 = (f32[41,24,128]{2,1,0:T(8,128)S(1)}, f32[41,24,128]{2,1,0:T(8,128)S(1)}, f32[20,24,128]{2,1,0:T(8,128)S(1)}) custom-call(), custom_call_target="tpu_custom_call" | custom-call | bytes 3500000 | tf_op jit(solution)/shard_map/pallas_call | solution.py:801
  8.3 1.1 %collective-permute-done.2.across = f32[8,128]{1,0:T(8,128)S(1)} collective-permute-done((f32[8,128]{1,0:T(8,128)S(1)}, f32[8,128]{1,0:T(8,128)S(1)}, u32[]{:S(2)}, u32[]{:S(2)}) %collective-permute-start.2) | collective-permute-done | bytes 4128 | tf_op jit(solution)/shard_map/ppermute | solution.py:793
  9.5 0.1 shard_map.55
  9.6 1.2 %collective-permute-start.3 = (f32[168,128]{1,0:T(8,128)S(1)}, f32[168,128]{1,0:T(8,128)S(1)}, u32[]{:S(2)}, u32[]{:S(2)}) collective-permute-start(f32[168,128]{1,0:T(8,128)S(1)} %get-tuple-element.53), channel_id=1, source_target_pairs={{0,1},{1,2},{2,3},{3,0},{4,5},{5,6},{6,7},{7,4},{8,9},{9,10},{10,1... | collective-permute-start | bytes 258056 | tf_op jit(solution)/shard_map/ppermute | solution.py:806
  10.8 1.5 %collective-permute-start.4 = (f32[168,128]{1,0:T(8,128)S(1)}, f32[168,128]{1,0:T(8,128)S(1)}, u32[]{:S(2)}, u32[]{:S(2)}) collective-permute-start(f32[168,128]{1,0:T(8,128)S(1)} %get-tuple-element.54), channel_id=1, source_target_pairs={{0,3},{1,0},{2,1},{3,2},{4,7},{5,4},{6,5},{7,6},{8,11},{9,8},{10,9... | collective-permute-start | bytes 258056 | tf_op jit(solution)/shard_map/ppermute | solution.py:807
  12.3 1.5 %collective-permute-start.5 = (f32[8,128]{1,0:T(8,128)S(1)}, f32[8,128]{1,0:T(8,128)S(1)}, u32[]{:S(2)}, u32[]{:S(2)}) collective-permute-start(f32[8,128]{1,0:T(8,128)S(1)} %shard_map.54.total), channel_id=1, source_target_pairs={{0,2},{1,3},{2,0},{3,1},{4,6},{5,7},{6,4},{7,5},{8,10},{9,11},{10,... | collective-permute-start | bytes 12296 | tf_op jit(solution)/shard_map/ppermute | solution.py:804
  13.8 2.5 %collective-permute-done.5.across = f32[8,128]{1,0:T(8,128)S(1)} collective-permute-done((f32[8,128]{1,0:T(8,128)S(1)}, f32[8,128]{1,0:T(8,128)S(1)}, u32[]{:S(2)}, u32[]{:S(2)}) %collective-permute-start.5) | collective-permute-done | bytes 4128 | tf_op jit(solution)/shard_map/ppermute | solution.py:804
  16.5 3.8 %collective-permute-start.7 = (f32[488,128]{1,0:T(8,128)S(1)}, f32[488,128]{1,0:T(8,128)S(1)}, u32[]{:S(2)}, u32[]{:S(2)}) collective-permute-start(f32[488,128]{1,0:T(8,128)S(1)} %get-tuple-element.62), channel_id=1, source_target_pairs={{0,112},{16,0},{32,16},{48,32},{64,48},{80,64},{96,80},{112,96},{1... | collective-permute-start | bytes 749576 | tf_op jit(solution)/shard_map/ppermute | solution.py:815
  20.3 1.6 %collective-permute-start.6 = (f32[488,128]{1,0:T(8,128)S(1)}, f32[488,128]{1,0:T(8,128)S(1)}, u32[]{:S(2)}, u32[]{:S(2)}) collective-permute-start(f32[488,128]{1,0:T(8,128)S(1)} %get-tuple-element.56), channel_id=1, source_target_pairs={{0,16},{16,32},{32,48},{48,64},{64,80},{80,96},{96,112},{112,0},{1... | collective-permute-start | bytes 749576 | tf_op jit(solution)/shard_map/ppermute | solution.py:814
  21.9 1.6 %collective-permute-start.8 = (f32[72,128]{1,0:T(8,128)S(1)}, f32[72,128]{1,0:T(8,128)S(1)}, u32[]{:S(2)}, u32[]{:S(2)}) collective-permute-start(f32[72,128]{1,0:T(8,128)S(1)} %get-tuple-element.71), channel_id=1, source_target_pairs={{0,32},{16,48},{32,64},{48,80},{64,96},{80,112},{96,0},{112,16},{1... | collective-permute-start | bytes 110600 | tf_op jit(solution)/shard_map/ppermute | solution.py:816
  23.5 1.0 %collective-permute-start.9 = (f32[72,128]{1,0:T(8,128)S(1)}, f32[72,128]{1,0:T(8,128)S(1)}, u32[]{:S(2)}, u32[]{:S(2)}) collective-permute-start(f32[72,128]{1,0:T(8,128)S(1)} %get-tuple-element.72), channel_id=1, source_target_pairs={{0,96},{16,112},{32,0},{48,16},{64,32},{80,48},{96,64},{112,80},{1... | collective-permute-start | bytes 110600 | tf_op jit(solution)/shard_map/ppermute | solution.py:817
  24.6 0.6 %shard_map.58 = (f32[2,41,8,128]{3,2,1,0:T(8,128)S(1)}, f32[2,26,8,128]{3,2,1,0:T(8,128)S(1)}) custom-call(f32[640,128]{1,0:T(8,128)S(1)} %get-tuple-element.59.ref), custom_call_target="tpu_custom_call" | custom-call | bytes 2800000 | tf_op jit(solution)/shard_map/pallas_call | solution.py:826
  25.2 0.9 %collective-permute-done.7.ref.xp1 = f32[488,128]{1,0:T(8,128)S(1)} collective-permute-done((f32[488,128]{1,0:T(8,128)S(1)}, f32[488,128]{1,0:T(8,128)S(1)}, u32[]{:S(2)}, u32[]{:S(2)}) %collective-permute-start.7) | collective-permute-done | bytes 249888 | tf_op jit(solution)/shard_map/ppermute | solution.py:815
  26.1 0.6 %shard_map.59 = (f32[2,41,8,128]{3,2,1,0:T(8,128)S(1)}, f32[2,26,8,128]{3,2,1,0:T(8,128)S(1)}) custom-call(f32[488,128]{1,0:T(8,128)S(1)} %collective-permute-done.7.ref.xp1), custom_call_target="tpu_custom_call" | custom-call | bytes 2800000 | tf_op jit(solution)/shard_map/pallas_call | solution.py:826
  26.7 0.6 %shard_map.57 = (f32[2,41,8,128]{3,2,1,0:T(8,128)S(1)}, f32[2,26,8,128]{3,2,1,0:T(8,128)S(1)}) custom-call(f32[488,128]{1,0:T(8,128)S(1)} %collective-permute-done.6.ref.xm1), custom_call_target="tpu_custom_call" | custom-call | bytes 2800000 | tf_op jit(solution)/shard_map/pallas_call | solution.py:826
  27.3 1.2 %collective-permute-done.8.xm2 = f32[72,128]{1,0:T(8,128)S(1)} collective-permute-done((f32[72,128]{1,0:T(8,128)S(1)}, f32[72,128]{1,0:T(8,128)S(1)}, u32[]{:S(2)}, u32[]{:S(2)}) %collective-permute-start.8) | collective-permute-done | bytes 36896 | tf_op jit(solution)/shard_map/ppermute | solution.py:816
  28.6 2.3 %collective-permute-start.10 = (f32[8,128]{1,0:T(8,128)S(1)}, f32[8,128]{1,0:T(8,128)S(1)}, u32[]{:S(2)}, u32[]{:S(2)}) collective-permute-start(f32[8,128]{1,0:T(8,128)S(1)} %get-tuple-element.81), channel_id=1, source_target_pairs={{0,48},{16,96},{32,80},{48,0},{64,112},{80,32},{96,16},{112,64},{1... | collective-permute-start | bytes 12296 | tf_op jit(solution)/shard_map/ppermute | solution.py:830
  30.8 2.9 %shard_map.60 = (f32[41,24,128]{2,1,0:T(8,128)S(1)}, f32[41,24,128]{2,1,0:T(8,128)S(1)}, f32[20,24,128]{2,1,0:T(8,128)S(1)}) custom-call(f32[2,41,8,128]{3,2,1,0:T(8,128)S(1)} %get-tuple-element.65.t1, f32[2,41,8,128]{3,2,1,0:T(8,128)S(1)} %get-tuple-element.66.t2, f32[2,41,8,128]{3,2,1,0:T(8,128)S(1)} %get-tuple-element.67.t3, ...), custom_call_target="tpu_custom_call" | custom-call | bytes 10500000 | tf_op jit(solution)/shard_map/pallas_call | solution.py:832
  33.7 1.6 %shard_map.62 = (f32[4,16,256]{2,1,0:T(8,128)}, f32[4,16,256]{2,1,0:T(8,128)}) custom-call(s32[8,128]{1,0:T(8,128)S(1)} %get-tuple-element.44.order, f32[2,41,8,128]{3,2,1,0:T(8,128)S(1)} %get-tuple-element.65.t1, f32[2,41,8,128]{3,2,1,0:T(8,128)S(1)} %get-tuple-element.66.t2, f32[2,41,8,128]{3,2,1,0:T(8,128)S(1)} %get-tuple-element.67.t3, ...), custom_call_target="tpu_custom_call" | custom-call | bytes 350000 | tf_op jit(solution)/shard_map/pallas_call | solution.py:850
  (13 shorter events, 0.2 us)
Async XLA Ops:
  0.6 0.9 %copy-start = (s32[512,3]{0,1:T(4,128)S(1)}, s32[512,3]{0,1:T(4,128)}, u32[]{:S(2)}) copy-start(s32[512,3]{0,1:T(4,128)} %param.5) | copy-start | bytes 18436
  1.8 7.6 %collective-permute-start = (f32[88,128]{1,0:T(8,128)S(1)}, f32[88,128]{1,0:T(8,128)S(1)}, u32[]{:S(2)}, u32[]{:S(2)}) collective-permute-start(f32[88,128]{1,0:T(8,128)S(1)} %get-tuple-element.47), channel_id=1, source_target_pairs={{0,4},{1,5},{2,6},{3,7},{4,8},{5,9},{6,10},{7,11},{8,12},{9,13},{1... | collective-permute-start | bytes 135176 | tf_op jit(solution)/shard_map/ppermute | solution.py:795
  4.0 5.5 %collective-permute-start.1 = (f32[88,128]{1,0:T(8,128)S(1)}, f32[88,128]{1,0:T(8,128)S(1)}, u32[]{:S(2)}, u32[]{:S(2)}) collective-permute-start(f32[88,128]{1,0:T(8,128)S(1)} %get-tuple-element.48), channel_id=1, source_target_pairs={{0,12},{1,13},{2,14},{3,15},{4,0},{5,1},{6,2},{7,3},{8,4},{9,5},{1... | collective-permute-start | bytes 135176 | tf_op jit(solution)/shard_map/ppermute | solution.py:796
  5.5 4.0 %collective-permute-start.2 = (f32[8,128]{1,0:T(8,128)S(1)}, f32[8,128]{1,0:T(8,128)S(1)}, u32[]{:S(2)}, u32[]{:S(2)}) collective-permute-start(f32[8,128]{1,0:T(8,128)S(1)} %get-tuple-element.52.sums), channel_id=1, source_target_pairs={{0,8},{1,9},{2,10},{3,11},{4,12},{5,13},{6,14},{7,15},{8,0},{9,1},... | collective-permute-start | bytes 12296 | tf_op jit(solution)/shard_map/ppermute | solution.py:793
  9.6 6.8 %collective-permute-start.3 = (f32[168,128]{1,0:T(8,128)S(1)}, f32[168,128]{1,0:T(8,128)S(1)}, u32[]{:S(2)}, u32[]{:S(2)}) collective-permute-start(f32[168,128]{1,0:T(8,128)S(1)} %get-tuple-element.53), channel_id=1, source_target_pairs={{0,1},{1,2},{2,3},{3,0},{4,5},{5,6},{6,7},{7,4},{8,9},{9,10},{10,1... | collective-permute-start | bytes 258056 | tf_op jit(solution)/shard_map/ppermute | solution.py:806
  10.8 5.5 %collective-permute-start.4 = (f32[168,128]{1,0:T(8,128)S(1)}, f32[168,128]{1,0:T(8,128)S(1)}, u32[]{:S(2)}, u32[]{:S(2)}) collective-permute-start(f32[168,128]{1,0:T(8,128)S(1)} %get-tuple-element.54), channel_id=1, source_target_pairs={{0,3},{1,0},{2,1},{3,2},{4,7},{5,4},{6,5},{7,6},{8,11},{9,8},{10,9... | collective-permute-start | bytes 258056 | tf_op jit(solution)/shard_map/ppermute | solution.py:807
  12.3 4.1 %collective-permute-start.5 = (f32[8,128]{1,0:T(8,128)S(1)}, f32[8,128]{1,0:T(8,128)S(1)}, u32[]{:S(2)}, u32[]{:S(2)}) collective-permute-start(f32[8,128]{1,0:T(8,128)S(1)} %shard_map.54.total), channel_id=1, source_target_pairs={{0,2},{1,3},{2,0},{3,1},{4,6},{5,7},{6,4},{7,5},{8,10},{9,11},{10,... | collective-permute-start | bytes 12296 | tf_op jit(solution)/shard_map/ppermute | solution.py:804
  16.5 9.6 %collective-permute-start.7 = (f32[488,128]{1,0:T(8,128)S(1)}, f32[488,128]{1,0:T(8,128)S(1)}, u32[]{:S(2)}, u32[]{:S(2)}) collective-permute-start(f32[488,128]{1,0:T(8,128)S(1)} %get-tuple-element.62), channel_id=1, source_target_pairs={{0,112},{16,0},{32,16},{48,32},{64,48},{80,64},{96,80},{112,96},{1... | collective-permute-start | bytes 749576 | tf_op jit(solution)/shard_map/ppermute | solution.py:815
  20.3 6.4 %collective-permute-start.6 = (f32[488,128]{1,0:T(8,128)S(1)}, f32[488,128]{1,0:T(8,128)S(1)}, u32[]{:S(2)}, u32[]{:S(2)}) collective-permute-start(f32[488,128]{1,0:T(8,128)S(1)} %get-tuple-element.56), channel_id=1, source_target_pairs={{0,16},{16,32},{32,48},{48,64},{64,80},{80,96},{96,112},{112,0},{1... | collective-permute-start | bytes 749576 | tf_op jit(solution)/shard_map/ppermute | solution.py:814
  21.9 6.6 %collective-permute-start.8 = (f32[72,128]{1,0:T(8,128)S(1)}, f32[72,128]{1,0:T(8,128)S(1)}, u32[]{:S(2)}, u32[]{:S(2)}) collective-permute-start(f32[72,128]{1,0:T(8,128)S(1)} %get-tuple-element.71), channel_id=1, source_target_pairs={{0,32},{16,48},{32,64},{48,80},{64,96},{80,112},{96,0},{112,16},{1... | collective-permute-start | bytes 110600 | tf_op jit(solution)/shard_map/ppermute | solution.py:816
  23.5 5.0 %collective-permute-start.9 = (f32[72,128]{1,0:T(8,128)S(1)}, f32[72,128]{1,0:T(8,128)S(1)}, u32[]{:S(2)}, u32[]{:S(2)}) collective-permute-start(f32[72,128]{1,0:T(8,128)S(1)} %get-tuple-element.72), channel_id=1, source_target_pairs={{0,96},{16,112},{32,0},{48,16},{64,32},{80,48},{96,64},{112,80},{1... | collective-permute-start | bytes 110600 | tf_op jit(solution)/shard_map/ppermute | solution.py:817
  28.6 5.1 %collective-permute-start.10 = (f32[8,128]{1,0:T(8,128)S(1)}, f32[8,128]{1,0:T(8,128)S(1)}, u32[]{:S(2)}, u32[]{:S(2)}) collective-permute-start(f32[8,128]{1,0:T(8,128)S(1)} %get-tuple-element.81), channel_id=1, source_target_pairs={{0,48},{16,96},{32,80},{48,0},{64,112},{80,32},{96,16},{112,64},{1... | collective-permute-start | bytes 12296 | tf_op jit(solution)/shard_map/ppermute | solution.py:830

commit v5 on v4

--- a/solution.py
+++ b/solution.py
@@ -88,7 +88,7 @@
         copy.wait()
 
 
-def _sort_kernel(coords, raw, weight, own, sums, order, plain):
+def _sort_kernel(coords, raw, weight, own, sums, order, up, down, plain):
     g, yb, zb = _position()
     row = _iota((16, LANES), 0)
     lane = _iota((16, LANES), 1)
@@ -119,6 +119,7 @@
         own[8 * i : 8 * i + 8, :] = plain[pl.ds(BLOCK * (i // 2) + i % 2, 8, stride=2), :]
     s1, s2 = (jnp.sum(v, axis=0, keepdims=True) for v in (s1, s2))
     sums[...] = jnp.where(row8 == 0, s1, jnp.where(row8 == 1, s2, 0.0))
+    _y_messages(own, sums, up, down)
 
 
 def _box_of(coords, g, yb, zb):
@@ -153,7 +154,7 @@
 Y_FAR, Y_SUMS, Y_MESSAGE = 64, 80, 88
 
 
-def _y_kernel(own, sums, up, down):
+def _y_messages(own, sums, up, down):
     half = _iota((BLOCK, LANES), 1) < 64
     for i in range(4):
         _put(up, i, _blk(own, i + 4))
@@ -224,7 +225,8 @@
         for p in range(4):
             _put(mine, (q - 1) * 4 + p, pieces[p])
         if 2 <= q <= 7:
-            two_away += pieces[1:3]
+            if 3 <= q <= 6:
+                two_away += pieces[1:3]
             for ref, near in ((up, 6), (down, 0)):
                 for p in (1, 2):
                     _put(ref, (q - 2) * 4 + p, pieces[p])
@@ -243,23 +245,25 @@
             ref[at + 16 : at + 32, :] = pieces[2]
             for s in (0, 8):
                 ref[at + 32 + s : at + 40 + s, :] = _share(pieces[0][s : s + 8], pieces[3][s : s + 8], near)
+    half = _iota((BLOCK, LANES), 1) < 64
+    two_away += [jnp.where(half, ext(7, h), ext(2, h)) for h in range(2)]
     for src, quad in ((zbelow, 3), (zabove, 0)):
         near = [_blk(src, q - 1) for q in range(2, 8)]
         two_away += [_pack_quads(near[:4], quad), _pack_quads(near[4:], quad)]
     for ref, r in ((high, 6), (low, 0)):
-        for i in range(0, 16, 2):
+        for i in range(0, 14, 2):
             a, b = two_away[i : i + 2]
             ref[4 * i : 4 * i + 8, :] = _rows_to([(a[:8], r), (b[:8], r), (a[8:], r), (b[8:], r)])
     t = total[...] + zbelow[160:168, :] + zabove[160:168, :] + across[...]
     part[...] = t
-    for ref, at in ((up, SUMS), (down, SUMS), (high, 64), (low, 64)):
+    for ref, at in ((up, SUMS), (down, SUMS), (high, 56), (low, 56)):
         ref[at : at + 8, :] = t
 
 
 def _window_kernel(mine, xm1, xp1, xm2, xp2, out, send):
     odd = _position()[0] % 2 == 1
-    low = xm1[SUMS:MESSAGE, :] + xm2[64:72, :]
-    high = xp1[SUMS:MESSAGE, :] + xp2[64:72, :]
+    low = xm1[SUMS:MESSAGE, :] + xm2[56:64, :]
+    high = xp1[SUMS:MESSAGE, :] + xp2[56:64, :]
     out[...] = mine[...] + (low + high)
     send[...] = mine[...] + jnp.where(odd, high, low)
 
@@ -471,9 +475,10 @@
 
     def ahead(q, s):
         c, slot = divmod(q - 2, 4)
-        lo = _roll(near(12 + c, s), 4 * (3 - slot), 1)
-        hi = _roll(near(14 + c, s), -4 * slot, 1)
-        return [lo, near(2 * (q - 2), s), near(2 * (q - 2) + 1, s), hi]
+        lo = _roll(near(10 + c, s), 4 * (3 - slot), 1)
+        hi = _roll(near(12 + c, s), -4 * slot, 1)
+        at = 2 * (q - 3) if 3 <= q <= 6 else 8
+        return [lo, near(at, s), near(at + 1, s), hi]
 
     tasks = [(q, s) for q in range(2, 5) for s in range(2)]
     for (q, s), rows in zip(tasks, _unfold([(ahead(q, s), ahead(9 - q, s)) for q, s in tasks])):
@@ -508,7 +513,7 @@
     whole = [lambda y, s=s, v=v: jnp.concatenate([ahead_of[s, y], v(y)], axis=0) for s, v in enumerate(D)]
     args = (whole, 32, W, 1.0 - 5.0 * W, None)
     _restrict(*args, 3, 7, put_source, None, 7)
-    _restrict(*args, 10, 10, put_source, patch, 5)
+    _restrict(*args, 10, 10, put_source, patch, 10)
     _sweep_three(g, yb, zb, lambda i: raw[i], lambda i: beyond[i], cs, c0, c1)
     base = [lambda i, v=v: W * v(i) for v in D]
     step_masks = _step_masks(g, yb, zb)
@@ -570,7 +575,7 @@
     return 0.2 * c + W * (near + (before + after))
 
 
-def _sweep_rows(src, dst, cs, first, masks, batch=4):
+def _sweep_rows(src, dst, cs, first, masks, batch=6):
     for start in range(first, COARSE, batch):
         rows = range(start, min(start + batch, COARSE))
         turned = [
@@ -627,7 +632,7 @@
     return jnp.where(i < own_first, *pair)
 
 
-def _relax(even, odd, i, n, store, batch=3):
+def _relax(even, odd, i, n, store, batch=4):
     for first in range(0, n, batch):
         us = range(first, min(first + batch, n))
         turned = []
@@ -784,14 +789,16 @@
         us=1.0,
         grant=53.79,
     )(divergence, weights)
-    own, sums, order = _call(
+    own, sums, order, up, down = _call(
         _sort_kernel,
         [VMEM] * 3,
-        [_rows(128), _rows(8), jax.ShapeDtypeStruct((8, LANES), jnp.int32)],
+        [
+            *(_rows(128), _rows(8), jax.ShapeDtypeStruct((8, LANES), jnp.int32)),
+            *(_rows(Y_MESSAGE), _rows(Y_MESSAGE)),
+        ],
         [pltpu.VMEM((128, LANES), F32)],
     )(coords, raw, weight)
     across = lax.ppermute(sums, "dev", _y_shift(2))
-    up, down = _call(_y_kernel, [VMEM] * 2, [_rows(Y_MESSAGE), _rows(Y_MESSAGE)])(own, sums)
     below = lax.ppermute(up, "dev", _y_shift(1))
     above = lax.ppermute(down, "dev", _y_shift(-1))
 
@@ -809,7 +816,7 @@
     mine, up, down, high, low, part = _call(
         _x_kernel,
         [VMEM] * 7,
-        [_rows(640), _rows(MESSAGE), _rows(MESSAGE), _rows(72), _rows(72), _rows(8)],
+        [_rows(640), _rows(MESSAGE), _rows(MESSAGE), _rows(64), _rows(64), _rows(8)],
     )(own, below, above, zbelow, zabove, total, zacross)
     xm1 = lax.ppermute(up, "grp", _x_shift(1))
     xp1 = lax.ppermute(down, "grp", _x_shift(-1))

time: 35.5 us -> 35.3 us (level)
  transfers between devices with their start and end apart: 11 -> 11, of which waited for: 4 -> 4; matrix products, arithmetic and copies ran while one was open for 0% -> 0% of each run, Pallas kernels for 17% -> 16%
where the time goes in v5:
time: 35.3 us; the launch traced here: 35.2 us
  starting transfers between devices  19.9 us (56%)
  Pallas kernels  8.81 us (25%)
  waiting for transfers between devices  5.75 us (16%)
  between operations  0.73 us (2%)
    ppermute x1, starting transfers between devices, _body(): xp1 = lax.ppermute(down, 'grp', _x_shift(-1))  3.78 us
    pallas_call x1, Pallas kernels, _body(): _call(_coarse_kernel, [VMEM] * 8, [fine, fine, _shape(COARSE, 24, LANES)]...  2.75 us
    ppermute x1, waiting for transfers between devices, _body(): zacross = lax.ppermute(total, 'dev', _z_shift(2))  2.53 us
    ppermute x1, starting transfers between devices, _body(): lax.ppermute(send, 'grp', [(x, (x + 3 - 6 * (x % 2)) % 8) for x in range(...  2.31 us
    ppermute x1, starting transfers between devices, _body(): below = lax.ppermute(up, 'dev', _y_shift(1))  2.15 us
    pallas_call x3, Pallas kernels, _body(): bricks.append(_call(kernel, [VMEM], outs, us=0.8)(ref))  1.77 us
    ppermute x1, starting transfers between devices, _body(): xm2 = lax.ppermute(high, 'grp', _x_shift(2))  1.64 us
    pallas_call x1, Pallas kernels, _body(): _call(_cycle_kernel, [VMEM] * 12, [_shape(4, 16, 256), _shape(4, 16, 256)...  1.64 us
  transfers between devices with their start and end apart: 11, of which 4 were waited for; matrix products, arithmetic and copies ran while one was open for 0% of the time, Pallas kernels for 16%

profile of v5, /device:TPU:1, one launch (start us, length us, event | category | flops | bytes accessed | tf_op | source)
XLA Modules:
  0.0 35.2 jit_solution(9430901330001124542)
XLA Ops:
  0.6 0.9 %shard_map.50 = (f32[4,16,256]{2,1,0:T(8,128)S(1)}, f32[8,16,128]{2,1,0:T(8,128)S(1)}) custom-call(f32[4,16,256]{2,1,0:T(8,128)} %div.1, f32[27,8,16,128]{3,2,1,0:T(8,128)} %constant.2.clone.w2), custom_call_target="tpu_custom_call" | custom-call | bytes 3500000 | tf_op jit(solution)/shard_map/pallas_call | solution.py:784
  1.6 0.2 shard_map.51
  1.8 2.1 %collective-permute-start = (f32[88,128]{1,0:T(8,128)S(1)}, f32[88,128]{1,0:T(8,128)S(1)}, u32[]{:S(2)}, u32[]{:S(2)}) collective-permute-start(f32[88,128]{1,0:T(8,128)S(1)} %get-tuple-element.46), channel_id=1, source_target_pairs={{0,4},{1,5},{2,6},{3,7},{4,8},{5,9},{6,10},{7,11},{8,12},{9,13},{1... | collective-permute-start | bytes 135176 | tf_op jit(solution)/shard_map/ppermute | solution.py:802
  3.9 1.5 %collective-permute-start.1 = (f32[88,128]{1,0:T(8,128)S(1)}, f32[88,128]{1,0:T(8,128)S(1)}, u32[]{:S(2)}, u32[]{:S(2)}) collective-permute-start(f32[88,128]{1,0:T(8,128)S(1)} %get-tuple-element.47), channel_id=1, source_target_pairs={{0,12},{1,13},{2,14},{3,15},{4,0},{5,1},{6,2},{7,3},{8,4},{9,5},{1... | collective-permute-start | bytes 135176 | tf_op jit(solution)/shard_map/ppermute | solution.py:803
  5.5 1.6 %collective-permute-start.2 = (f32[8,128]{1,0:T(8,128)S(1)}, f32[8,128]{1,0:T(8,128)S(1)}, u32[]{:S(2)}, u32[]{:S(2)}) collective-permute-start(f32[8,128]{1,0:T(8,128)S(1)} %get-tuple-element.52.sums), channel_id=1, source_target_pairs={{0,8},{1,9},{2,10},{3,11},{4,12},{5,13},{6,14},{7,15},{8,0},{9,1},... | collective-permute-start | bytes 12296 | tf_op jit(solution)/shard_map/ppermute | solution.py:801
  7.0 1.2 %shard_map.52 = (f32[41,24,128]{2,1,0:T(8,128)S(1)}, f32[41,24,128]{2,1,0:T(8,128)S(1)}, f32[20,24,128]{2,1,0:T(8,128)S(1)}) custom-call(), custom_call_target="tpu_custom_call" | custom-call | bytes 3500000 | tf_op jit(solution)/shard_map/pallas_call | solution.py:808
  8.3 1.1 %collective-permute-done.2.across = f32[8,128]{1,0:T(8,128)S(1)} collective-permute-done((f32[8,128]{1,0:T(8,128)S(1)}, f32[8,128]{1,0:T(8,128)S(1)}, u32[]{:S(2)}, u32[]{:S(2)}) %collective-permute-start.2) | collective-permute-done | bytes 4128 | tf_op jit(solution)/shard_map/ppermute | solution.py:801
  9.4 0.1 shard_map.54
  9.6 1.2 %collective-permute-start.3 = (f32[168,128]{1,0:T(8,128)S(1)}, f32[168,128]{1,0:T(8,128)S(1)}, u32[]{:S(2)}, u32[]{:S(2)}) collective-permute-start(f32[168,128]{1,0:T(8,128)S(1)} %get-tuple-element.53), channel_id=1, source_target_pairs={{0,1},{1,2},{2,3},{3,0},{4,5},{5,6},{6,7},{7,4},{8,9},{9,10},{10,1... | collective-permute-start | bytes 258056 | tf_op jit(solution)/shard_map/ppermute | solution.py:813
  10.8 1.5 %collective-permute-start.4 = (f32[168,128]{1,0:T(8,128)S(1)}, f32[168,128]{1,0:T(8,128)S(1)}, u32[]{:S(2)}, u32[]{:S(2)}) collective-permute-start(f32[168,128]{1,0:T(8,128)S(1)} %get-tuple-element.54), channel_id=1, source_target_pairs={{0,3},{1,0},{2,1},{3,2},{4,7},{5,4},{6,5},{7,6},{8,11},{9,8},{10,9... | collective-permute-start | bytes 258056 | tf_op jit(solution)/shard_map/ppermute | solution.py:814
  12.3 1.5 %collective-permute-start.5 = (f32[8,128]{1,0:T(8,128)S(1)}, f32[8,128]{1,0:T(8,128)S(1)}, u32[]{:S(2)}, u32[]{:S(2)}) collective-permute-start(f32[8,128]{1,0:T(8,128)S(1)} %shard_map.53.total), channel_id=1, source_target_pairs={{0,2},{1,3},{2,0},{3,1},{4,6},{5,7},{6,4},{7,5},{8,10},{9,11},{10,... | collective-permute-start | bytes 12296 | tf_op jit(solution)/shard_map/ppermute | solution.py:811
  13.8 2.5 %collective-permute-done.5.across = f32[8,128]{1,0:T(8,128)S(1)} collective-permute-done((f32[8,128]{1,0:T(8,128)S(1)}, f32[8,128]{1,0:T(8,128)S(1)}, u32[]{:S(2)}, u32[]{:S(2)}) %collective-permute-start.5) | collective-permute-done | bytes 4128 | tf_op jit(solution)/shard_map/ppermute | solution.py:811
  16.5 3.8 %collective-permute-start.7 = (f32[488,128]{1,0:T(8,128)S(1)}, f32[488,128]{1,0:T(8,128)S(1)}, u32[]{:S(2)}, u32[]{:S(2)}) collective-permute-start(f32[488,128]{1,0:T(8,128)S(1)} %get-tuple-element.62), channel_id=1, source_target_pairs={{0,112},{16,0},{32,16},{48,32},{64,48},{80,64},{96,80},{112,96},{1... | collective-permute-start | bytes 749576 | tf_op jit(solution)/shard_map/ppermute | solution.py:822
  20.3 1.6 %collective-permute-start.6 = (f32[488,128]{1,0:T(8,128)S(1)}, f32[488,128]{1,0:T(8,128)S(1)}, u32[]{:S(2)}, u32[]{:S(2)}) collective-permute-start(f32[488,128]{1,0:T(8,128)S(1)} %get-tuple-element.56), channel_id=1, source_target_pairs={{0,16},{16,32},{32,48},{48,64},{64,80},{80,96},{96,112},{112,0},{1... | collective-permute-start | bytes 749576 | tf_op jit(solution)/shard_map/ppermute | solution.py:821
  21.9 1.6 %collective-permute-start.8 = (f32[64,128]{1,0:T(8,128)S(1)}, f32[64,128]{1,0:T(8,128)S(1)}, u32[]{:S(2)}, u32[]{:S(2)}) collective-permute-start(f32[64,128]{1,0:T(8,128)S(1)} %get-tuple-element.71), channel_id=1, source_target_pairs={{0,32},{16,48},{32,64},{48,80},{64,96},{80,112},{96,0},{112,16},{1... | collective-permute-start | bytes 98312 | tf_op jit(solution)/shard_map/ppermute | solution.py:823
  23.5 1.0 %collective-permute-start.9 = (f32[64,128]{1,0:T(8,128)S(1)}, f32[64,128]{1,0:T(8,128)S(1)}, u32[]{:S(2)}, u32[]{:S(2)}) collective-permute-start(f32[64,128]{1,0:T(8,128)S(1)} %get-tuple-element.72), channel_id=1, source_target_pairs={{0,96},{16,112},{32,0},{48,16},{64,32},{80,48},{96,64},{112,80},{1... | collective-permute-start | bytes 98312 | tf_op jit(solution)/shard_map/ppermute | solution.py:824
  24.6 0.6 %shard_map.57 = (f32[2,41,8,128]{3,2,1,0:T(8,128)S(1)}, f32[2,26,8,128]{3,2,1,0:T(8,128)S(1)}) custom-call(f32[640,128]{1,0:T(8,128)S(1)} %get-tuple-element.59.ref), custom_call_target="tpu_custom_call" | custom-call | bytes 2800000 | tf_op jit(solution)/shard_map/pallas_call | solution.py:833
  25.2 0.9 %collective-permute-done.7.ref.xp1 = f32[488,128]{1,0:T(8,128)S(1)} collective-permute-done((f32[488,128]{1,0:T(8,128)S(1)}, f32[488,128]{1,0:T(8,128)S(1)}, u32[]{:S(2)}, u32[]{:S(2)}) %collective-permute-start.7) | collective-permute-done | bytes 249888 | tf_op jit(solution)/shard_map/ppermute | solution.py:822
  26.1 0.6 %shard_map.58 = (f32[2,41,8,128]{3,2,1,0:T(8,128)S(1)}, f32[2,26,8,128]{3,2,1,0:T(8,128)S(1)}) custom-call(f32[488,128]{1,0:T(8,128)S(1)} %collective-permute-done.7.ref.xp1), custom_call_target="tpu_custom_call" | custom-call | bytes 2800000 | tf_op jit(solution)/shard_map/pallas_call | solution.py:833
  26.7 0.6 %shard_map.56 = (f32[2,41,8,128]{3,2,1,0:T(8,128)S(1)}, f32[2,26,8,128]{3,2,1,0:T(8,128)S(1)}) custom-call(f32[488,128]{1,0:T(8,128)S(1)} %collective-permute-done.6.ref.xm1), custom_call_target="tpu_custom_call" | custom-call | bytes 2800000 | tf_op jit(solution)/shard_map/pallas_call | solution.py:833
  27.3 1.1 %collective-permute-done.8.xm2 = f32[64,128]{1,0:T(8,128)S(1)} collective-permute-done((f32[64,128]{1,0:T(8,128)S(1)}, f32[64,128]{1,0:T(8,128)S(1)}, u32[]{:S(2)}, u32[]{:S(2)}) %collective-permute-start.8) | collective-permute-done | bytes 32800 | tf_op jit(solution)/shard_map/ppermute | solution.py:823
  28.4 2.3 %collective-permute-start.10 = (f32[8,128]{1,0:T(8,128)S(1)}, f32[8,128]{1,0:T(8,128)S(1)}, u32[]{:S(2)}, u32[]{:S(2)}) collective-permute-start(f32[8,128]{1,0:T(8,128)S(1)} %get-tuple-element.81), channel_id=1, source_target_pairs={{0,48},{16,96},{32,80},{48,0},{64,112},{80,32},{96,16},{112,64},{1... | collective-permute-start | bytes 12296 | tf_op jit(solution)/shard_map/ppermute | solution.py:837
  30.8 2.8 %shard_map.59 = (f32[41,24,128]{2,1,0:T(8,128)S(1)}, f32[41,24,128]{2,1,0:T(8,128)S(1)}, f32[20,24,128]{2,1,0:T(8,128)S(1)}) custom-call(f32[2,41,8,128]{3,2,1,0:T(8,128)S(1)} %get-tuple-element.65.t1, f32[2,41,8,128]{3,2,1,0:T(8,128)S(1)} %get-tuple-element.66.t2, f32[2,41,8,128]{3,2,1,0:T(8,128)S(1)} %get-tuple-element.67.t3, ...), custom_call_target="tpu_custom_call" | custom-call | bytes 10500000 | tf_op jit(solution)/shard_map/pallas_call | solution.py:839
  33.5 1.6 %shard_map.61 = (f32[4,16,256]{2,1,0:T(8,128)}, f32[4,16,256]{2,1,0:T(8,128)}) custom-call(s32[8,128]{1,0:T(8,128)S(1)} %get-tuple-element.44.order, f32[2,41,8,128]{3,2,1,0:T(8,128)S(1)} %get-tuple-element.65.t1, f32[2,41,8,128]{3,2,1,0:T(8,128)S(1)} %get-tuple-element.66.t2, f32[2,41,8,128]{3,2,1,0:T(8,128)S(1)} %get-tuple-element.67.t3, ...), custom_call_target="tpu_custom_call" | custom-call | bytes 350000 | tf_op jit(solution)/shard_map/pallas_call | solution.py:857
  (12 shorter events, 0.1 us)
Async XLA Ops:
  0.6 0.9 %copy-start = (s32[512,3]{0,1:T(4,128)S(1)}, s32[512,3]{0,1:T(4,128)}, u32[]{:S(2)}) copy-start(s32[512,3]{0,1:T(4,128)} %param.5) | copy-start | bytes 18436
  1.8 7.6 %collective-permute-start = (f32[88,128]{1,0:T(8,128)S(1)}, f32[88,128]{1,0:T(8,128)S(1)}, u32[]{:S(2)}, u32[]{:S(2)}) collective-permute-start(f32[88,128]{1,0:T(8,128)S(1)} %get-tuple-element.46), channel_id=1, source_target_pairs={{0,4},{1,5},{2,6},{3,7},{4,8},{5,9},{6,10},{7,11},{8,12},{9,13},{1... | collective-permute-start | bytes 135176 | tf_op jit(solution)/shard_map/ppermute | solution.py:802
  3.9 5.5 %collective-permute-start.1 = (f32[88,128]{1,0:T(8,128)S(1)}, f32[88,128]{1,0:T(8,128)S(1)}, u32[]{:S(2)}, u32[]{:S(2)}) collective-permute-start(f32[88,128]{1,0:T(8,128)S(1)} %get-tuple-element.47), channel_id=1, source_target_pairs={{0,12},{1,13},{2,14},{3,15},{4,0},{5,1},{6,2},{7,3},{8,4},{9,5},{1... | collective-permute-start | bytes 135176 | tf_op jit(solution)/shard_map/ppermute | solution.py:803
  5.5 4.0 %collective-permute-start.2 = (f32[8,128]{1,0:T(8,128)S(1)}, f32[8,128]{1,0:T(8,128)S(1)}, u32[]{:S(2)}, u32[]{:S(2)}) collective-permute-start(f32[8,128]{1,0:T(8,128)S(1)} %get-tuple-element.52.sums), channel_id=1, source_target_pairs={{0,8},{1,9},{2,10},{3,11},{4,12},{5,13},{6,14},{7,15},{8,0},{9,1},... | collective-permute-start | bytes 12296 | tf_op jit(solution)/shard_map/ppermute | solution.py:801
  9.6 6.8 %collective-permute-start.3 = (f32[168,128]{1,0:T(8,128)S(1)}, f32[168,128]{1,0:T(8,128)S(1)}, u32[]{:S(2)}, u32[]{:S(2)}) collective-permute-start(f32[168,128]{1,0:T(8,128)S(1)} %get-tuple-element.53), channel_id=1, source_target_pairs={{0,1},{1,2},{2,3},{3,0},{4,5},{5,6},{6,7},{7,4},{8,9},{9,10},{10,1... | collective-permute-start | bytes 258056 | tf_op jit(solution)/shard_map/ppermute | solution.py:813
  10.8 5.5 %collective-permute-start.4 = (f32[168,128]{1,0:T(8,128)S(1)}, f32[168,128]{1,0:T(8,128)S(1)}, u32[]{:S(2)}, u32[]{:S(2)}) collective-permute-start(f32[168,128]{1,0:T(8,128)S(1)} %get-tuple-element.54), channel_id=1, source_target_pairs={{0,3},{1,0},{2,1},{3,2},{4,7},{5,4},{6,5},{7,6},{8,11},{9,8},{10,9... | collective-permute-start | bytes 258056 | tf_op jit(solution)/shard_map/ppermute | solution.py:814
  12.3 4.1 %collective-permute-start.5 = (f32[8,128]{1,0:T(8,128)S(1)}, f32[8,128]{1,0:T(8,128)S(1)}, u32[]{:S(2)}, u32[]{:S(2)}) collective-permute-start(f32[8,128]{1,0:T(8,128)S(1)} %shard_map.53.total), channel_id=1, source_target_pairs={{0,2},{1,3},{2,0},{3,1},{4,6},{5,7},{6,4},{7,5},{8,10},{9,11},{10,... | collective-permute-start | bytes 12296 | tf_op jit(solution)/shard_map/ppermute | solution.py:811
  16.5 9.6 %collective-permute-start.7 = (f32[488,128]{1,0:T(8,128)S(1)}, f32[488,128]{1,0:T(8,128)S(1)}, u32[]{:S(2)}, u32[]{:S(2)}) collective-permute-start(f32[488,128]{1,0:T(8,128)S(1)} %get-tuple-element.62), channel_id=1, source_target_pairs={{0,112},{16,0},{32,16},{48,32},{64,48},{80,64},{96,80},{112,96},{1... | collective-permute-start | bytes 749576 | tf_op jit(solution)/shard_map/ppermute | solution.py:822
  20.3 6.4 %collective-permute-start.6 = (f32[488,128]{1,0:T(8,128)S(1)}, f32[488,128]{1,0:T(8,128)S(1)}, u32[]{:S(2)}, u32[]{:S(2)}) collective-permute-start(f32[488,128]{1,0:T(8,128)S(1)} %get-tuple-element.56), channel_id=1, source_target_pairs={{0,16},{16,32},{32,48},{48,64},{64,80},{80,96},{96,112},{112,0},{1... | collective-permute-start | bytes 749576 | tf_op jit(solution)/shard_map/ppermute | solution.py:821
  21.9 6.5 %collective-permute-start.8 = (f32[64,128]{1,0:T(8,128)S(1)}, f32[64,128]{1,0:T(8,128)S(1)}, u32[]{:S(2)}, u32[]{:S(2)}) collective-permute-start(f32[64,128]{1,0:T(8,128)S(1)} %get-tuple-element.71), channel_id=1, source_target_pairs={{0,32},{16,48},{32,64},{48,80},{64,96},{80,112},{96,0},{112,16},{1... | collective-permute-start | bytes 98312 | tf_op jit(solution)/shard_map/ppermute | solution.py:823
  23.5 4.9 %collective-permute-start.9 = (f32[64,128]{1,0:T(8,128)S(1)}, f32[64,128]{1,0:T(8,128)S(1)}, u32[]{:S(2)}, u32[]{:S(2)}) collective-permute-start(f32[64,128]{1,0:T(8,128)S(1)} %get-tuple-element.72), channel_id=1, source_target_pairs={{0,96},{16,112},{32,0},{48,16},{64,32},{80,48},{96,64},{112,80},{1... | collective-permute-start | bytes 98312 | tf_op jit(solution)/shard_map/ppermute | solution.py:824
  28.4 5.1 %collective-permute-start.10 = (f32[8,128]{1,0:T(8,128)S(1)}, f32[8,128]{1,0:T(8,128)S(1)}, u32[]{:S(2)}, u32[]{:S(2)}) collective-permute-start(f32[8,128]{1,0:T(8,128)S(1)} %get-tuple-element.81), channel_id=1, source_target_pairs={{0,48},{16,96},{32,80},{48,0},{64,112},{80,32},{96,16},{112,64},{1... | collective-permute-start | bytes 12296 | tf_op jit(solution)/shard_map/ppermute | solution.py:837

commit v6 on v5

--- a/solution.py
+++ b/solution.py
@@ -679,7 +679,7 @@
 
 
 def _cycle_kernel(
-    order, t1, t2, t3, Re, Ro, raw, Te, To, raw_one, part, across, pot, res, Be, Bo, cs, c0, c1, boxes, place, sem
+    order, t1, t2, t3, Re, Ro, raw, Te, To, raw_one, part, across, pot, res, Be, Bo, cs, c0, c1, boxes, stage, place, sem
 ):
     g, yb, zb = _position()
     fetch = pltpu.make_async_copy(order, place, sem.at[0])
@@ -706,30 +706,38 @@
 
     fetch.wait()
     box_of = [place[h, 0] for h in range(4)]
-    for q in (3, 4):
-        i0 = 8 * q
-        even = _lazily(lambda u: Be[i0 + u])
-        odd = _lazily(lambda u: Bo[i0 + u])
+
+    def send(f, groups, out):
+        for q in (3, 4):
+            for s, sides in enumerate(_refold(groups(q))):
+                for o, pieces in zip((q - 3, 6 - q), sides):
+                    for h in range(2):
+                        at = BLOCK * ((f * 4 + o) * 2 + h) + s
+                        boxes[pl.ds(at, 8, stride=2), :] = pieces[h]
+        for o in range(4):
+            for h in range(2):
+                v = _blk(boxes, (f * 4 + o) * 2 + h)
+                stage[f, box_of[(o // 2) * 2 + h], :, (o % 2) * LANES : (o % 2 + 1) * LANES] = v
+        copy = pltpu.make_async_copy(stage.at[f], out, sem.at[1 + f])
+        copy.start()
+        return copy
+
+    sent = [send(0, lambda q: [[v[8 * q + u, 8:16, :] for u in range(8)] for v in (Be, Bo)], pot)]
+
+    def residual(q):
         left = ([], [])
 
         def store(i, e, o, ye, yo):
             left[0].append(t2[0, i] - (6.0 * e - ye)[8:16])
             left[1].append(t2[1, i] - (6.0 * o - yo)[8:16])
 
-        _relax(even, odd, i0, 8, store)
-        tasks = [(f, s) for f in range(2) for s in range(2)]
-        done = [[v(u)[8:16] for u in range(8)] for v in (even, odd)]
-        groups = [(done, left)[f][s] for f, s in tasks]
-        for (f, s), sides in zip(tasks, _refold(groups)):
-            for o, pieces in zip((q - 3, 6 - q), sides):
-                for h in range(2):
-                    at = BLOCK * ((f * 4 + o) * 2 + h) + s
-                    boxes[pl.ds(at, 8, stride=2), :] = pieces[h]
-    for f, out in enumerate((pot, res)):
-        for o in range(4):
-            for h in range(2):
-                v = _blk(boxes, (f * 4 + o) * 2 + h)
-                out[box_of[(o // 2) * 2 + h], :, (o % 2) * LANES : (o % 2 + 1) * LANES] = v
+        even, odd = (_lazily(lambda u, v=v: v[8 * q + u]) for v in (Be, Bo))
+        _relax(even, odd, 8 * q, 8, store)
+        return left
+
+    sent.append(send(1, residual, res))
+    for copy in sent:
+        copy.wait()
 
 
 def _lazily(fn):
@@ -755,12 +763,12 @@
 HBM = pl.BlockSpec(memory_space=pltpu.HBM)
 
 
-def _call(kernel, specs, outs, scratch=(), us=0.1, grant=40.0):
+def _call(kernel, specs, outs, scratch=(), us=0.1, grant=40.0, to=VMEM):
     return pl.pallas_call(
         kernel,
         out_shape=outs,
         in_specs=specs,
-        out_specs=[VMEM] * len(outs),
+        out_specs=[to] * len(outs),
         scratch_shapes=scratch,
         cost_estimate=pl.CostEstimate(flops=0, transcendentals=0, bytes_accessed=int(us * 3.5e6)),
         compiler_params=pltpu.CompilerParams(vmem_limit_bytes=int(grant * 2**20)),
@@ -858,7 +866,8 @@
         _cycle_kernel,
         [VMEM] * 12,
         [_shape(4, 16, 256), _shape(4, 16, 256)],
-        [inner, inner, plane, plane, plane, boxes, pltpu.SMEM((8, LANES), jnp.int32), pltpu.SemaphoreType.DMA((1,))],
+        [inner, inner, plane, plane, plane, boxes, pltpu.VMEM((2, 4, 16, 256), F32), pltpu.SMEM((8, LANES), jnp.int32), pltpu.SemaphoreType.DMA((3,))],
+        to=HBM,
     )(order, *tiles, *start, *ones, part, xacross)
     return pot, res
 

time: 35.3 us -> 35.3 us (level)
  no operation moved by 1% of the time
where the time goes in v6:
time: 35.3 us; the launch traced here: 35.2 us
  starting transfers between devices  19.9 us (56%)
  Pallas kernels  8.82 us (25%)
  waiting for transfers between devices  5.75 us (16%)
  between operations  0.73 us (2%)
    ppermute x1, starting transfers between devices, _body(): xp1 = lax.ppermute(down, 'grp', _x_shift(-1))  3.78 us
    pallas_call x1, Pallas kernels, _body(): _call(_coarse_kernel, [VMEM] * 8, [fine, fine, _shape(COARSE, 24, LANES)]...  2.75 us
    ppermute x1, waiting for transfers between devices, _body(): zacross = lax.ppermute(total, 'dev', _z_shift(2))  2.53 us
    ppermute x1, starting transfers between devices, _body(): lax.ppermute(send, 'grp', [(x, (x + 3 - 6 * (x % 2)) % 8) for x in range(...  2.31 us
    ppermute x1, starting transfers between devices, _body(): below = lax.ppermute(up, 'dev', _y_shift(1))  2.15 us
    pallas_call x3, Pallas kernels, _body(): bricks.append(_call(kernel, [VMEM], outs, us=0.8)(ref))  1.77 us
    pallas_call x1, Pallas kernels, _body(): _call(_cycle_kernel, [VMEM] * 12, [_shape(4, 16, 256), _shape(4, 16, 256)...  1.65 us
    ppermute x1, starting transfers between devices, _body(): xm2 = lax.ppermute(high, 'grp', _x_shift(2))  1.64 us
  transfers between devices with their start and end apart: 11, of which 4 were waited for; matrix products, arithmetic and copies ran while one was open for 0% of the time, Pallas kernels for 16%

profile of v6, /device:TPU:1, one launch (start us, length us, event | category | flops | bytes accessed | tf_op | source)
XLA Modules:
  0.0 35.2 jit_solution(17162760776700489887)
XLA Ops:
  0.6 0.9 %shard_map.50 = (f32[4,16,256]{2,1,0:T(8,128)S(1)}, f32[8,16,128]{2,1,0:T(8,128)S(1)}) custom-call(f32[4,16,256]{2,1,0:T(8,128)} %div.1, f32[27,8,16,128]{3,2,1,0:T(8,128)} %constant.2.clone.w2), custom_call_target="tpu_custom_call" | custom-call | bytes 3500000 | tf_op jit(solution)/shard_map/pallas_call | solution.py:792
  1.6 0.2 shard_map.51
  1.8 2.1 %collective-permute-start = (f32[88,128]{1,0:T(8,128)S(1)}, f32[88,128]{1,0:T(8,128)S(1)}, u32[]{:S(2)}, u32[]{:S(2)}) collective-permute-start(f32[88,128]{1,0:T(8,128)S(1)} %get-tuple-element.46), channel_id=1, source_target_pairs={{0,4},{1,5},{2,6},{3,7},{4,8},{5,9},{6,10},{7,11},{8,12},{9,13},{1... | collective-permute-start | bytes 135176 | tf_op jit(solution)/shard_map/ppermute | solution.py:810
  3.9 1.5 %collective-permute-start.1 = (f32[88,128]{1,0:T(8,128)S(1)}, f32[88,128]{1,0:T(8,128)S(1)}, u32[]{:S(2)}, u32[]{:S(2)}) collective-permute-start(f32[88,128]{1,0:T(8,128)S(1)} %get-tuple-element.47), channel_id=1, source_target_pairs={{0,12},{1,13},{2,14},{3,15},{4,0},{5,1},{6,2},{7,3},{8,4},{9,5},{1... | collective-permute-start | bytes 135176 | tf_op jit(solution)/shard_map/ppermute | solution.py:811
  5.5 1.6 %collective-permute-start.2 = (f32[8,128]{1,0:T(8,128)S(1)}, f32[8,128]{1,0:T(8,128)S(1)}, u32[]{:S(2)}, u32[]{:S(2)}) collective-permute-start(f32[8,128]{1,0:T(8,128)S(1)} %get-tuple-element.52.sums), channel_id=1, source_target_pairs={{0,8},{1,9},{2,10},{3,11},{4,12},{5,13},{6,14},{7,15},{8,0},{9,1},... | collective-permute-start | bytes 12296 | tf_op jit(solution)/shard_map/ppermute | solution.py:809
  7.0 1.2 %shard_map.52 = (f32[41,24,128]{2,1,0:T(8,128)S(1)}, f32[41,24,128]{2,1,0:T(8,128)S(1)}, f32[20,24,128]{2,1,0:T(8,128)S(1)}) custom-call(), custom_call_target="tpu_custom_call" | custom-call | bytes 3500000 | tf_op jit(solution)/shard_map/pallas_call | solution.py:816
  8.3 1.1 %collective-permute-done.2.across = f32[8,128]{1,0:T(8,128)S(1)} collective-permute-done((f32[8,128]{1,0:T(8,128)S(1)}, f32[8,128]{1,0:T(8,128)S(1)}, u32[]{:S(2)}, u32[]{:S(2)}) %collective-permute-start.2) | collective-permute-done | bytes 4128 | tf_op jit(solution)/shard_map/ppermute | solution.py:809
  9.4 0.1 shard_map.54
  9.6 1.2 %collective-permute-start.3 = (f32[168,128]{1,0:T(8,128)S(1)}, f32[168,128]{1,0:T(8,128)S(1)}, u32[]{:S(2)}, u32[]{:S(2)}) collective-permute-start(f32[168,128]{1,0:T(8,128)S(1)} %get-tuple-element.53), channel_id=1, source_target_pairs={{0,1},{1,2},{2,3},{3,0},{4,5},{5,6},{6,7},{7,4},{8,9},{9,10},{10,1... | collective-permute-start | bytes 258056 | tf_op jit(solution)/shard_map/ppermute | solution.py:821
  10.8 1.5 %collective-permute-start.4 = (f32[168,128]{1,0:T(8,128)S(1)}, f32[168,128]{1,0:T(8,128)S(1)}, u32[]{:S(2)}, u32[]{:S(2)}) collective-permute-start(f32[168,128]{1,0:T(8,128)S(1)} %get-tuple-element.54), channel_id=1, source_target_pairs={{0,3},{1,0},{2,1},{3,2},{4,7},{5,4},{6,5},{7,6},{8,11},{9,8},{10,9... | collective-permute-start | bytes 258056 | tf_op jit(solution)/shard_map/ppermute | solution.py:822
  12.3 1.5 %collective-permute-start.5 = (f32[8,128]{1,0:T(8,128)S(1)}, f32[8,128]{1,0:T(8,128)S(1)}, u32[]{:S(2)}, u32[]{:S(2)}) collective-permute-start(f32[8,128]{1,0:T(8,128)S(1)} %shard_map.53.total), channel_id=1, source_target_pairs={{0,2},{1,3},{2,0},{3,1},{4,6},{5,7},{6,4},{7,5},{8,10},{9,11},{10,... | collective-permute-start | bytes 12296 | tf_op jit(solution)/shard_map/ppermute | solution.py:819
  13.8 2.5 %collective-permute-done.5.across = f32[8,128]{1,0:T(8,128)S(1)} collective-permute-done((f32[8,128]{1,0:T(8,128)S(1)}, f32[8,128]{1,0:T(8,128)S(1)}, u32[]{:S(2)}, u32[]{:S(2)}) %collective-permute-start.5) | collective-permute-done | bytes 4128 | tf_op jit(solution)/shard_map/ppermute | solution.py:819
  16.5 3.8 %collective-permute-start.7 = (f32[488,128]{1,0:T(8,128)S(1)}, f32[488,128]{1,0:T(8,128)S(1)}, u32[]{:S(2)}, u32[]{:S(2)}) collective-permute-start(f32[488,128]{1,0:T(8,128)S(1)} %get-tuple-element.62), channel_id=1, source_target_pairs={{0,112},{16,0},{32,16},{48,32},{64,48},{80,64},{96,80},{112,96},{1... | collective-permute-start | bytes 749576 | tf_op jit(solution)/shard_map/ppermute | solution.py:830
  20.3 1.6 %collective-permute-start.6 = (f32[488,128]{1,0:T(8,128)S(1)}, f32[488,128]{1,0:T(8,128)S(1)}, u32[]{:S(2)}, u32[]{:S(2)}) collective-permute-start(f32[488,128]{1,0:T(8,128)S(1)} %get-tuple-element.56), channel_id=1, source_target_pairs={{0,16},{16,32},{32,48},{48,64},{64,80},{80,96},{96,112},{112,0},{1... | collective-permute-start | bytes 749576 | tf_op jit(solution)/shard_map/ppermute | solution.py:829
  21.9 1.6 %collective-permute-start.8 = (f32[64,128]{1,0:T(8,128)S(1)}, f32[64,128]{1,0:T(8,128)S(1)}, u32[]{:S(2)}, u32[]{:S(2)}) collective-permute-start(f32[64,128]{1,0:T(8,128)S(1)} %get-tuple-element.71), channel_id=1, source_target_pairs={{0,32},{16,48},{32,64},{48,80},{64,96},{80,112},{96,0},{112,16},{1... | collective-permute-start | bytes 98312 | tf_op jit(solution)/shard_map/ppermute | solution.py:831
  23.5 1.0 %collective-permute-start.9 = (f32[64,128]{1,0:T(8,128)S(1)}, f32[64,128]{1,0:T(8,128)S(1)}, u32[]{:S(2)}, u32[]{:S(2)}) collective-permute-start(f32[64,128]{1,0:T(8,128)S(1)} %get-tuple-element.72), channel_id=1, source_target_pairs={{0,96},{16,112},{32,0},{48,16},{64,32},{80,48},{96,64},{112,80},{1... | collective-permute-start | bytes 98312 | tf_op jit(solution)/shard_map/ppermute | solution.py:832
  24.6 0.6 %shard_map.57 = (f32[2,41,8,128]{3,2,1,0:T(8,128)S(1)}, f32[2,26,8,128]{3,2,1,0:T(8,128)S(1)}) custom-call(f32[640,128]{1,0:T(8,128)S(1)} %get-tuple-element.59.ref), custom_call_target="tpu_custom_call" | custom-call | bytes 2800000 | tf_op jit(solution)/shard_map/pallas_call | solution.py:841
  25.2 0.9 %collective-permute-done.7.ref.xp1 = f32[488,128]{1,0:T(8,128)S(1)} collective-permute-done((f32[488,128]{1,0:T(8,128)S(1)}, f32[488,128]{1,0:T(8,128)S(1)}, u32[]{:S(2)}, u32[]{:S(2)}) %collective-permute-start.7) | collective-permute-done | bytes 249888 | tf_op jit(solution)/shard_map/ppermute | solution.py:830
  26.1 0.6 %shard_map.58 = (f32[2,41,8,128]{3,2,1,0:T(8,128)S(1)}, f32[2,26,8,128]{3,2,1,0:T(8,128)S(1)}) custom-call(f32[488,128]{1,0:T(8,128)S(1)} %collective-permute-done.7.ref.xp1), custom_call_target="tpu_custom_call" | custom-call | bytes 2800000 | tf_op jit(solution)/shard_map/pallas_call | solution.py:841
  26.7 0.6 %shard_map.56 = (f32[2,41,8,128]{3,2,1,0:T(8,128)S(1)}, f32[2,26,8,128]{3,2,1,0:T(8,128)S(1)}) custom-call(f32[488,128]{1,0:T(8,128)S(1)} %collective-permute-done.6.ref.xm1), custom_call_target="tpu_custom_call" | custom-call | bytes 2800000 | tf_op jit(solution)/shard_map/pallas_call | solution.py:841
  27.3 1.1 %collective-permute-done.8.xm2 = f32[64,128]{1,0:T(8,128)S(1)} collective-permute-done((f32[64,128]{1,0:T(8,128)S(1)}, f32[64,128]{1,0:T(8,128)S(1)}, u32[]{:S(2)}, u32[]{:S(2)}) %collective-permute-start.8) | collective-permute-done | bytes 32800 | tf_op jit(solution)/shard_map/ppermute | solution.py:831
  28.4 2.3 %collective-permute-start.10 = (f32[8,128]{1,0:T(8,128)S(1)}, f32[8,128]{1,0:T(8,128)S(1)}, u32[]{:S(2)}, u32[]{:S(2)}) collective-permute-start(f32[8,128]{1,0:T(8,128)S(1)} %get-tuple-element.81), channel_id=1, source_target_pairs={{0,48},{16,96},{32,80},{48,0},{64,112},{80,32},{96,16},{112,64},{1... | collective-permute-start | bytes 12296 | tf_op jit(solution)/shard_map/ppermute | solution.py:845
  30.8 2.8 %shard_map.59 = (f32[41,24,128]{2,1,0:T(8,128)S(1)}, f32[41,24,128]{2,1,0:T(8,128)S(1)}, f32[20,24,128]{2,1,0:T(8,128)S(1)}) custom-call(f32[2,41,8,128]{3,2,1,0:T(8,128)S(1)} %get-tuple-element.65.t1, f32[2,41,8,128]{3,2,1,0:T(8,128)S(1)} %get-tuple-element.66.t2, f32[2,41,8,128]{3,2,1,0:T(8,128)S(1)} %get-tuple-element.67.t3, ...), custom_call_target="tpu_custom_call" | custom-call | bytes 10500000 | tf_op jit(solution)/shard_map/pallas_call | solution.py:847
  33.5 1.7 %shard_map.61 = (f32[4,16,256]{2,1,0:T(8,128)}, f32[4,16,256]{2,1,0:T(8,128)}) custom-call(s32[8,128]{1,0:T(8,128)S(1)} %get-tuple-element.44.order, f32[2,41,8,128]{3,2,1,0:T(8,128)S(1)} %get-tuple-element.65.t1, f32[2,41,8,128]{3,2,1,0:T(8,128)S(1)} %get-tuple-element.66.t2, f32[2,41,8,128]{3,2,1,0:T(8,128)S(1)} %get-tuple-element.67.t3, ...), custom_call_target="tpu_custom_call" | custom-call | bytes 350000 | tf_op jit(solution)/shard_map/pallas_call | solution.py:865
  (12 shorter events, 0.1 us)
Async XLA Ops:
  0.6 0.9 %copy-start = (s32[512,3]{0,1:T(4,128)S(1)}, s32[512,3]{0,1:T(4,128)}, u32[]{:S(2)}) copy-start(s32[512,3]{0,1:T(4,128)} %param.5) | copy-start | bytes 18436
  1.8 7.6 %collective-permute-start = (f32[88,128]{1,0:T(8,128)S(1)}, f32[88,128]{1,0:T(8,128)S(1)}, u32[]{:S(2)}, u32[]{:S(2)}) collective-permute-start(f32[88,128]{1,0:T(8,128)S(1)} %get-tuple-element.46), channel_id=1, source_target_pairs={{0,4},{1,5},{2,6},{3,7},{4,8},{5,9},{6,10},{7,11},{8,12},{9,13},{1... | collective-permute-start | bytes 135176 | tf_op jit(solution)/shard_map/ppermute | solution.py:810
  3.9 5.5 %collective-permute-start.1 = (f32[88,128]{1,0:T(8,128)S(1)}, f32[88,128]{1,0:T(8,128)S(1)}, u32[]{:S(2)}, u32[]{:S(2)}) collective-permute-start(f32[88,128]{1,0:T(8,128)S(1)} %get-tuple-element.47), channel_id=1, source_target_pairs={{0,12},{1,13},{2,14},{3,15},{4,0},{5,1},{6,2},{7,3},{8,4},{9,5},{1... | collective-permute-start | bytes 135176 | tf_op jit(solution)/shard_map/ppermute | solution.py:811
  5.5 4.0 %collective-permute-start.2 = (f32[8,128]{1,0:T(8,128)S(1)}, f32[8,128]{1,0:T(8,128)S(1)}, u32[]{:S(2)}, u32[]{:S(2)}) collective-permute-start(f32[8,128]{1,0:T(8,128)S(1)} %get-tuple-element.52.sums), channel_id=1, source_target_pairs={{0,8},{1,9},{2,10},{3,11},{4,12},{5,13},{6,14},{7,15},{8,0},{9,1},... | collective-permute-start | bytes 12296 | tf_op jit(solution)/shard_map/ppermute | solution.py:809
  9.6 6.8 %collective-permute-start.3 = (f32[168,128]{1,0:T(8,128)S(1)}, f32[168,128]{1,0:T(8,128)S(1)}, u32[]{:S(2)}, u32[]{:S(2)}) collective-permute-start(f32[168,128]{1,0:T(8,128)S(1)} %get-tuple-element.53), channel_id=1, source_target_pairs={{0,1},{1,2},{2,3},{3,0},{4,5},{5,6},{6,7},{7,4},{8,9},{9,10},{10,1... | collective-permute-start | bytes 258056 | tf_op jit(solution)/shard_map/ppermute | solution.py:821
  10.8 5.5 %collective-permute-start.4 = (f32[168,128]{1,0:T(8,128)S(1)}, f32[168,128]{1,0:T(8,128)S(1)}, u32[]{:S(2)}, u32[]{:S(2)}) collective-permute-start(f32[168,128]{1,0:T(8,128)S(1)} %get-tuple-element.54), channel_id=1, source_target_pairs={{0,3},{1,0},{2,1},{3,2},{4,7},{5,4},{6,5},{7,6},{8,11},{9,8},{10,9... | collective-permute-start | bytes 258056 | tf_op jit(solution)/shard_map/ppermute | solution.py:822
  12.3 4.1 %collective-permute-start.5 = (f32[8,128]{1,0:T(8,128)S(1)}, f32[8,128]{1,0:T(8,128)S(1)}, u32[]{:S(2)}, u32[]{:S(2)}) collective-permute-start(f32[8,128]{1,0:T(8,128)S(1)} %shard_map.53.total), channel_id=1, source_target_pairs={{0,2},{1,3},{2,0},{3,1},{4,6},{5,7},{6,4},{7,5},{8,10},{9,11},{10,... | collective-permute-start | bytes 12296 | tf_op jit(solution)/shard_map/ppermute | solution.py:819
  16.5 9.6 %collective-permute-start.7 = (f32[488,128]{1,0:T(8,128)S(1)}, f32[488,128]{1,0:T(8,128)S(1)}, u32[]{:S(2)}, u32[]{:S(2)}) collective-permute-start(f32[488,128]{1,0:T(8,128)S(1)} %get-tuple-element.62), channel_id=1, source_target_pairs={{0,112},{16,0},{32,16},{48,32},{64,48},{80,64},{96,80},{112,96},{1... | collective-permute-start | bytes 749576 | tf_op jit(solution)/shard_map/ppermute | solution.py:830
  20.3 6.4 %collective-permute-start.6 = (f32[488,128]{1,0:T(8,128)S(1)}, f32[488,128]{1,0:T(8,128)S(1)}, u32[]{:S(2)}, u32[]{:S(2)}) collective-permute-start(f32[488,128]{1,0:T(8,128)S(1)} %get-tuple-element.56), channel_id=1, source_target_pairs={{0,16},{16,32},{32,48},{48,64},{64,80},{80,96},{96,112},{112,0},{1... | collective-permute-start | bytes 749576 | tf_op jit(solution)/shard_map/ppermute | solution.py:829
  21.9 6.5 %collective-permute-start.8 = (f32[64,128]{1,0:T(8,128)S(1)}, f32[64,128]{1,0:T(8,128)S(1)}, u32[]{:S(2)}, u32[]{:S(2)}) collective-permute-start(f32[64,128]{1,0:T(8,128)S(1)} %get-tuple-element.71), channel_id=1, source_target_pairs={{0,32},{16,48},{32,64},{48,80},{64,96},{80,112},{96,0},{112,16},{1... | collective-permute-start | bytes 98312 | tf_op jit(solution)/shard_map/ppermute | solution.py:831
  23.5 4.9 %collective-permute-start.9 = (f32[64,128]{1,0:T(8,128)S(1)}, f32[64,128]{1,0:T(8,128)S(1)}, u32[]{:S(2)}, u32[]{:S(2)}) collective-permute-start(f32[64,128]{1,0:T(8,128)S(1)} %get-tuple-element.72), channel_id=1, source_target_pairs={{0,96},{16,112},{32,0},{48,16},{64,32},{80,48},{96,64},{112,80},{1... | collective-permute-start | bytes 98312 | tf_op jit(solution)/shard_map/ppermute | solution.py:832
  28.4 5.1 %collective-permute-start.10 = (f32[8,128]{1,0:T(8,128)S(1)}, f32[8,128]{1,0:T(8,128)S(1)}, u32[]{:S(2)}, u32[]{:S(2)}) collective-permute-start(f32[8,128]{1,0:T(8,128)S(1)} %get-tuple-element.81), channel_id=1, source_target_pairs={{0,48},{16,96},{32,80},{48,0},{64,112},{80,32},{96,16},{112,64},{1... | collective-permute-start | bytes 12296 | tf_op jit(solution)/shard_map/ppermute | solution.py:845

commit v7 on v5

--- a/solution.py
+++ b/solution.py
@@ -416,7 +416,7 @@
 
 
 def _unpack_brick(at, mask, mask_far, fold, store, store_far):
-    for batch in ([(0, 0), (1, 0), (2, 0)], [(3, 0), (4, 0), (2, 1)], [(3, 1), (4, 1)]):
+    for batch in ([(0, 0), (1, 0), (2, 0), (3, 0)], [(4, 0), (2, 1), (3, 1), (4, 1)]):
         tasks = [(q, far, s) for q, far in batch for s in range(2)]
         groups = [
             [(_far_pieces if far else _pieces)(at, o, s) for o in (q, 9 - q)] for q, far, s in tasks

time: 35.3 us -> 35.3 us (level)
  no operation moved by 1% of the time
where the time goes in v7:
time: 35.3 us; the launch traced here: 35.1 us
  starting transfers between devices  19.9 us (56%)
  Pallas kernels  8.74 us (25%)
  waiting for transfers between devices  5.81 us (16%)
  between operations  0.73 us (2%)
    ppermute x1, starting transfers between devices, _body(): xp1 = lax.ppermute(down, 'grp', _x_shift(-1))  3.78 us
    pallas_call x1, Pallas kernels, _body(): _call(_coarse_kernel, [VMEM] * 8, [fine, fine, _shape(COARSE, 24, LANES)]...  2.75 us
    ppermute x1, waiting for transfers between devices, _body(): zacross = lax.ppermute(total, 'dev', _z_shift(2))  2.53 us
    ppermute x1, starting transfers between devices, _body(): lax.ppermute(send, 'grp', [(x, (x + 3 - 6 * (x % 2)) % 8) for x in range(...  2.29 us
    ppermute x1, starting transfers between devices, _body(): below = lax.ppermute(up, 'dev', _y_shift(1))  2.15 us
    pallas_call x3, Pallas kernels, _body(): bricks.append(_call(kernel, [VMEM], outs, us=0.8)(ref))  1.71 us
    ppermute x1, starting transfers between devices, _body(): xm2 = lax.ppermute(high, 'grp', _x_shift(2))  1.64 us
    pallas_call x1, Pallas kernels, _body(): _call(_cycle_kernel, [VMEM] * 12, [_shape(4, 16, 256), _shape(4, 16, 256)...  1.64 us
  transfers between devices with their start and end apart: 11, of which 4 were waited for; matrix products, arithmetic and copies ran while one was open for 0% of the time, Pallas kernels for 16%

profile of v7, /device:TPU:1, one launch (start us, length us, event | category | flops | bytes accessed | tf_op | source)
XLA Modules:
  0.0 35.1 jit_solution(5097188313019289200)
XLA Ops:
  0.6 0.9 %shard_map.50 = (f32[4,16,256]{2,1,0:T(8,128)S(1)}, f32[8,16,128]{2,1,0:T(8,128)S(1)}) custom-call(f32[4,16,256]{2,1,0:T(8,128)} %div.1, f32[27,8,16,128]{3,2,1,0:T(8,128)} %constant.2.clone.w2), custom_call_target="tpu_custom_call" | custom-call | bytes 3500000 | tf_op jit(solution)/shard_map/pallas_call | solution.py:784
  1.6 0.2 shard_map.51
  1.8 2.1 %collective-permute-start = (f32[88,128]{1,0:T(8,128)S(1)}, f32[88,128]{1,0:T(8,128)S(1)}, u32[]{:S(2)}, u32[]{:S(2)}) collective-permute-start(f32[88,128]{1,0:T(8,128)S(1)} %get-tuple-element.46), channel_id=1, source_target_pairs={{0,4},{1,5},{2,6},{3,7},{4,8},{5,9},{6,10},{7,11},{8,12},{9,13},{1... | collective-permute-start | bytes 135176 | tf_op jit(solution)/shard_map/ppermute | solution.py:802
  3.9 1.5 %collective-permute-start.1 = (f32[88,128]{1,0:T(8,128)S(1)}, f32[88,128]{1,0:T(8,128)S(1)}, u32[]{:S(2)}, u32[]{:S(2)}) collective-permute-start(f32[88,128]{1,0:T(8,128)S(1)} %get-tuple-element.47), channel_id=1, source_target_pairs={{0,12},{1,13},{2,14},{3,15},{4,0},{5,1},{6,2},{7,3},{8,4},{9,5},{1... | collective-permute-start | bytes 135176 | tf_op jit(solution)/shard_map/ppermute | solution.py:803
  5.5 1.6 %collective-permute-start.2 = (f32[8,128]{1,0:T(8,128)S(1)}, f32[8,128]{1,0:T(8,128)S(1)}, u32[]{:S(2)}, u32[]{:S(2)}) collective-permute-start(f32[8,128]{1,0:T(8,128)S(1)} %get-tuple-element.52.sums), channel_id=1, source_target_pairs={{0,8},{1,9},{2,10},{3,11},{4,12},{5,13},{6,14},{7,15},{8,0},{9,1},... | collective-permute-start | bytes 12296 | tf_op jit(solution)/shard_map/ppermute | solution.py:801
  7.0 1.2 %shard_map.52 = (f32[41,24,128]{2,1,0:T(8,128)S(1)}, f32[41,24,128]{2,1,0:T(8,128)S(1)}, f32[20,24,128]{2,1,0:T(8,128)S(1)}) custom-call(), custom_call_target="tpu_custom_call" | custom-call | bytes 3500000 | tf_op jit(solution)/shard_map/pallas_call | solution.py:808
  8.3 1.1 %collective-permute-done.2.across = f32[8,128]{1,0:T(8,128)S(1)} collective-permute-done((f32[8,128]{1,0:T(8,128)S(1)}, f32[8,128]{1,0:T(8,128)S(1)}, u32[]{:S(2)}, u32[]{:S(2)}) %collective-permute-start.2) | collective-permute-done | bytes 4128 | tf_op jit(solution)/shard_map/ppermute | solution.py:801
  9.4 0.1 shard_map.54
  9.6 1.2 %collective-permute-start.3 = (f32[168,128]{1,0:T(8,128)S(1)}, f32[168,128]{1,0:T(8,128)S(1)}, u32[]{:S(2)}, u32[]{:S(2)}) collective-permute-start(f32[168,128]{1,0:T(8,128)S(1)} %get-tuple-element.53), channel_id=1, source_target_pairs={{0,1},{1,2},{2,3},{3,0},{4,5},{5,6},{6,7},{7,4},{8,9},{9,10},{10,1... | collective-permute-start | bytes 258056 | tf_op jit(solution)/shard_map/ppermute | solution.py:813
  10.8 1.5 %collective-permute-start.4 = (f32[168,128]{1,0:T(8,128)S(1)}, f32[168,128]{1,0:T(8,128)S(1)}, u32[]{:S(2)}, u32[]{:S(2)}) collective-permute-start(f32[168,128]{1,0:T(8,128)S(1)} %get-tuple-element.54), channel_id=1, source_target_pairs={{0,3},{1,0},{2,1},{3,2},{4,7},{5,4},{6,5},{7,6},{8,11},{9,8},{10,9... | collective-permute-start | bytes 258056 | tf_op jit(solution)/shard_map/ppermute | solution.py:814
  12.3 1.5 %collective-permute-start.5 = (f32[8,128]{1,0:T(8,128)S(1)}, f32[8,128]{1,0:T(8,128)S(1)}, u32[]{:S(2)}, u32[]{:S(2)}) collective-permute-start(f32[8,128]{1,0:T(8,128)S(1)} %shard_map.53.total), channel_id=1, source_target_pairs={{0,2},{1,3},{2,0},{3,1},{4,6},{5,7},{6,4},{7,5},{8,10},{9,11},{10,... | collective-permute-start | bytes 12296 | tf_op jit(solution)/shard_map/ppermute | solution.py:811
  13.8 2.5 %collective-permute-done.5.across = f32[8,128]{1,0:T(8,128)S(1)} collective-permute-done((f32[8,128]{1,0:T(8,128)S(1)}, f32[8,128]{1,0:T(8,128)S(1)}, u32[]{:S(2)}, u32[]{:S(2)}) %collective-permute-start.5) | collective-permute-done | bytes 4128 | tf_op jit(solution)/shard_map/ppermute | solution.py:811
  16.5 3.8 %collective-permute-start.7 = (f32[488,128]{1,0:T(8,128)S(1)}, f32[488,128]{1,0:T(8,128)S(1)}, u32[]{:S(2)}, u32[]{:S(2)}) collective-permute-start(f32[488,128]{1,0:T(8,128)S(1)} %get-tuple-element.62), channel_id=1, source_target_pairs={{0,112},{16,0},{32,16},{48,32},{64,48},{80,64},{96,80},{112,96},{1... | collective-permute-start | bytes 749576 | tf_op jit(solution)/shard_map/ppermute | solution.py:822
  20.3 1.6 %collective-permute-start.6 = (f32[488,128]{1,0:T(8,128)S(1)}, f32[488,128]{1,0:T(8,128)S(1)}, u32[]{:S(2)}, u32[]{:S(2)}) collective-permute-start(f32[488,128]{1,0:T(8,128)S(1)} %get-tuple-element.56), channel_id=1, source_target_pairs={{0,16},{16,32},{32,48},{48,64},{64,80},{80,96},{96,112},{112,0},{1... | collective-permute-start | bytes 749576 | tf_op jit(solution)/shard_map/ppermute | solution.py:821
  21.9 1.6 %collective-permute-start.8 = (f32[64,128]{1,0:T(8,128)S(1)}, f32[64,128]{1,0:T(8,128)S(1)}, u32[]{:S(2)}, u32[]{:S(2)}) collective-permute-start(f32[64,128]{1,0:T(8,128)S(1)} %get-tuple-element.71), channel_id=1, source_target_pairs={{0,32},{16,48},{32,64},{48,80},{64,96},{80,112},{96,0},{112,16},{1... | collective-permute-start | bytes 98312 | tf_op jit(solution)/shard_map/ppermute | solution.py:823
  23.5 1.0 %collective-permute-start.9 = (f32[64,128]{1,0:T(8,128)S(1)}, f32[64,128]{1,0:T(8,128)S(1)}, u32[]{:S(2)}, u32[]{:S(2)}) collective-permute-start(f32[64,128]{1,0:T(8,128)S(1)} %get-tuple-element.72), channel_id=1, source_target_pairs={{0,96},{16,112},{32,0},{48,16},{64,32},{80,48},{96,64},{112,80},{1... | collective-permute-start | bytes 98312 | tf_op jit(solution)/shard_map/ppermute | solution.py:824
  24.6 0.6 %shard_map.57 = (f32[2,41,8,128]{3,2,1,0:T(8,128)S(1)}, f32[2,26,8,128]{3,2,1,0:T(8,128)S(1)}) custom-call(f32[640,128]{1,0:T(8,128)S(1)} %get-tuple-element.59.ref), custom_call_target="tpu_custom_call" | custom-call | bytes 2800000 | tf_op jit(solution)/shard_map/pallas_call | solution.py:833
  25.1 0.9 %collective-permute-done.7.ref.xp1 = f32[488,128]{1,0:T(8,128)S(1)} collective-permute-done((f32[488,128]{1,0:T(8,128)S(1)}, f32[488,128]{1,0:T(8,128)S(1)}, u32[]{:S(2)}, u32[]{:S(2)}) %collective-permute-start.7) | collective-permute-done | bytes 249888 | tf_op jit(solution)/shard_map/ppermute | solution.py:822
  26.1 0.6 %shard_map.58 = (f32[2,41,8,128]{3,2,1,0:T(8,128)S(1)}, f32[2,26,8,128]{3,2,1,0:T(8,128)S(1)}) custom-call(f32[488,128]{1,0:T(8,128)S(1)} %collective-permute-done.7.ref.xp1), custom_call_target="tpu_custom_call" | custom-call | bytes 2800000 | tf_op jit(solution)/shard_map/pallas_call | solution.py:833
  26.7 0.6 %shard_map.56 = (f32[2,41,8,128]{3,2,1,0:T(8,128)S(1)}, f32[2,26,8,128]{3,2,1,0:T(8,128)S(1)}) custom-call(f32[488,128]{1,0:T(8,128)S(1)} %collective-permute-done.6.ref.xm1), custom_call_target="tpu_custom_call" | custom-call | bytes 2800000 | tf_op jit(solution)/shard_map/pallas_call | solution.py:833
  27.3 1.2 %collective-permute-done.8.xm2 = f32[64,128]{1,0:T(8,128)S(1)} collective-permute-done((f32[64,128]{1,0:T(8,128)S(1)}, f32[64,128]{1,0:T(8,128)S(1)}, u32[]{:S(2)}, u32[]{:S(2)}) %collective-permute-start.8) | collective-permute-done | bytes 32800 | tf_op jit(solution)/shard_map/ppermute | solution.py:823
  28.4 2.3 %collective-permute-start.10 = (f32[8,128]{1,0:T(8,128)S(1)}, f32[8,128]{1,0:T(8,128)S(1)}, u32[]{:S(2)}, u32[]{:S(2)}) collective-permute-start(f32[8,128]{1,0:T(8,128)S(1)} %get-tuple-element.81), channel_id=1, source_target_pairs={{0,48},{16,96},{32,80},{48,0},{64,112},{80,32},{96,16},{112,64},{1... | collective-permute-start | bytes 12296 | tf_op jit(solution)/shard_map/ppermute | solution.py:837
  30.7 2.8 %shard_map.59 = (f32[41,24,128]{2,1,0:T(8,128)S(1)}, f32[41,24,128]{2,1,0:T(8,128)S(1)}, f32[20,24,128]{2,1,0:T(8,128)S(1)}) custom-call(f32[2,41,8,128]{3,2,1,0:T(8,128)S(1)} %get-tuple-element.65.t1, f32[2,41,8,128]{3,2,1,0:T(8,128)S(1)} %get-tuple-element.66.t2, f32[2,41,8,128]{3,2,1,0:T(8,128)S(1)} %get-tuple-element.67.t3, ...), custom_call_target="tpu_custom_call" | custom-call | bytes 10500000 | tf_op jit(solution)/shard_map/pallas_call | solution.py:839
  33.5 1.6 %shard_map.61 = (f32[4,16,256]{2,1,0:T(8,128)}, f32[4,16,256]{2,1,0:T(8,128)}) custom-call(s32[8,128]{1,0:T(8,128)S(1)} %get-tuple-element.44.order, f32[2,41,8,128]{3,2,1,0:T(8,128)S(1)} %get-tuple-element.65.t1, f32[2,41,8,128]{3,2,1,0:T(8,128)S(1)} %get-tuple-element.66.t2, f32[2,41,8,128]{3,2,1,0:T(8,128)S(1)} %get-tuple-element.67.t3, ...), custom_call_target="tpu_custom_call" | custom-call | bytes 350000 | tf_op jit(solution)/shard_map/pallas_call | solution.py:857
  (12 shorter events, 0.1 us)
Async XLA Ops:
  0.6 0.9 %copy-start = (s32[512,3]{0,1:T(4,128)S(1)}, s32[512,3]{0,1:T(4,128)}, u32[]{:S(2)}) copy-start(s32[512,3]{0,1:T(4,128)} %param.5) | copy-start | bytes 18436
  1.8 7.6 %collective-permute-start = (f32[88,128]{1,0:T(8,128)S(1)}, f32[88,128]{1,0:T(8,128)S(1)}, u32[]{:S(2)}, u32[]{:S(2)}) collective-permute-start(f32[88,128]{1,0:T(8,128)S(1)} %get-tuple-element.46), channel_id=1, source_target_pairs={{0,4},{1,5},{2,6},{3,7},{4,8},{5,9},{6,10},{7,11},{8,12},{9,13},{1... | collective-permute-start | bytes 135176 | tf_op jit(solution)/shard_map/ppermute | solution.py:802
  3.9 5.5 %collective-permute-start.1 = (f32[88,128]{1,0:T(8,128)S(1)}, f32[88,128]{1,0:T(8,128)S(1)}, u32[]{:S(2)}, u32[]{:S(2)}) collective-permute-start(f32[88,128]{1,0:T(8,128)S(1)} %get-tuple-element.47), channel_id=1, source_target_pairs={{0,12},{1,13},{2,14},{3,15},{4,0},{5,1},{6,2},{7,3},{8,4},{9,5},{1... | collective-permute-start | bytes 135176 | tf_op jit(solution)/shard_map/ppermute | solution.py:803
  5.5 4.0 %collective-permute-start.2 = (f32[8,128]{1,0:T(8,128)S(1)}, f32[8,128]{1,0:T(8,128)S(1)}, u32[]{:S(2)}, u32[]{:S(2)}) collective-permute-start(f32[8,128]{1,0:T(8,128)S(1)} %get-tuple-element.52.sums), channel_id=1, source_target_pairs={{0,8},{1,9},{2,10},{3,11},{4,12},{5,13},{6,14},{7,15},{8,0},{9,1},... | collective-permute-start | bytes 12296 | tf_op jit(solution)/shard_map/ppermute | solution.py:801
  9.6 6.8 %collective-permute-start.3 = (f32[168,128]{1,0:T(8,128)S(1)}, f32[168,128]{1,0:T(8,128)S(1)}, u32[]{:S(2)}, u32[]{:S(2)}) collective-permute-start(f32[168,128]{1,0:T(8,128)S(1)} %get-tuple-element.53), channel_id=1, source_target_pairs={{0,1},{1,2},{2,3},{3,0},{4,5},{5,6},{6,7},{7,4},{8,9},{9,10},{10,1... | collective-permute-start | bytes 258056 | tf_op jit(solution)/shard_map/ppermute | solution.py:813
  10.8 5.5 %collective-permute-start.4 = (f32[168,128]{1,0:T(8,128)S(1)}, f32[168,128]{1,0:T(8,128)S(1)}, u32[]{:S(2)}, u32[]{:S(2)}) collective-permute-start(f32[168,128]{1,0:T(8,128)S(1)} %get-tuple-element.54), channel_id=1, source_target_pairs={{0,3},{1,0},{2,1},{3,2},{4,7},{5,4},{6,5},{7,6},{8,11},{9,8},{10,9... | collective-permute-start | bytes 258056 | tf_op jit(solution)/shard_map/ppermute | solution.py:814
  12.3 4.1 %collective-permute-start.5 = (f32[8,128]{1,0:T(8,128)S(1)}, f32[8,128]{1,0:T(8,128)S(1)}, u32[]{:S(2)}, u32[]{:S(2)}) collective-permute-start(f32[8,128]{1,0:T(8,128)S(1)} %shard_map.53.total), channel_id=1, source_target_pairs={{0,2},{1,3},{2,0},{3,1},{4,6},{5,7},{6,4},{7,5},{8,10},{9,11},{10,... | collective-permute-start | bytes 12296 | tf_op jit(solution)/shard_map/ppermute | solution.py:811
  16.5 9.6 %collective-permute-start.7 = (f32[488,128]{1,0:T(8,128)S(1)}, f32[488,128]{1,0:T(8,128)S(1)}, u32[]{:S(2)}, u32[]{:S(2)}) collective-permute-start(f32[488,128]{1,0:T(8,128)S(1)} %get-tuple-element.62), channel_id=1, source_target_pairs={{0,112},{16,0},{32,16},{48,32},{64,48},{80,64},{96,80},{112,96},{1... | collective-permute-start | bytes 749576 | tf_op jit(solution)/shard_map/ppermute | solution.py:822
  20.3 6.4 %collective-permute-start.6 = (f32[488,128]{1,0:T(8,128)S(1)}, f32[488,128]{1,0:T(8,128)S(1)}, u32[]{:S(2)}, u32[]{:S(2)}) collective-permute-start(f32[488,128]{1,0:T(8,128)S(1)} %get-tuple-element.56), channel_id=1, source_target_pairs={{0,16},{16,32},{32,48},{48,64},{64,80},{80,96},{96,112},{112,0},{1... | collective-permute-start | bytes 749576 | tf_op jit(solution)/shard_map/ppermute | solution.py:821
  21.9 6.5 %collective-permute-start.8 = (f32[64,128]{1,0:T(8,128)S(1)}, f32[64,128]{1,0:T(8,128)S(1)}, u32[]{:S(2)}, u32[]{:S(2)}) collective-permute-start(f32[64,128]{1,0:T(8,128)S(1)} %get-tuple-element.71), channel_id=1, source_target_pairs={{0,32},{16,48},{32,64},{48,80},{64,96},{80,112},{96,0},{112,16},{1... | collective-permute-start | bytes 98312 | tf_op jit(solution)/shard_map/ppermute | solution.py:823
  23.5 4.9 %collective-permute-start.9 = (f32[64,128]{1,0:T(8,128)S(1)}, f32[64,128]{1,0:T(8,128)S(1)}, u32[]{:S(2)}, u32[]{:S(2)}) collective-permute-start(f32[64,128]{1,0:T(8,128)S(1)} %get-tuple-element.72), channel_id=1, source_target_pairs={{0,96},{16,112},{32,0},{48,16},{64,32},{80,48},{96,64},{112,80},{1... | collective-permute-start | bytes 98312 | tf_op jit(solution)/shard_map/ppermute | solution.py:824
  28.4 5.1 %collective-permute-start.10 = (f32[8,128]{1,0:T(8,128)S(1)}, f32[8,128]{1,0:T(8,128)S(1)}, u32[]{:S(2)}, u32[]{:S(2)}) collective-permute-start(f32[8,128]{1,0:T(8,128)S(1)} %get-tuple-element.81), channel_id=1, source_target_pairs={{0,48},{16,96},{32,80},{48,0},{64,112},{80,32},{96,16},{112,64},{1... | collective-permute-start | bytes 12296 | tf_op jit(solution)/shard_map/ppermute | solution.py:837
